TPU v7x, 32 devices: a whole 2x2x4 slice. The times are simulated.
32 devices in a mesh: design: 2 (over x), pts: 16 (over z, y, core).
Axes of the slice: x: 2, y: 2, z: 4, core: 2. Of those that a mesh axis runs over, the one named last changes fastest.
Arguments:
- points: bfloat16 [8192, 256], P(('design', 'pts')), parts along dimension 0, may hold values from -6 to 6
- geometry: bfloat16 [16384, 256], P(('design', 'pts')), parts along dimension 0, may hold values from -6 to 6
- counts: int32 [32], P(('design', 'pts')), parts along dimension 0, may hold values from 128 to 256, as said below
- cotangent: bfloat16 [8192, 256], P(('design', 'pts')), parts along dimension 0, may hold values from -0.09375 to 0.09375
- gain_attn: float32 [256], replicated, may hold values from 0.5 to 1.5
- w_feat: bfloat16 [256, 256], replicated, may hold values from -0.375 to 0.375
- w_mid: bfloat16 [256, 256], replicated, may hold values from -0.375 to 0.375
- w_slice: bfloat16 [32, 256], replicated, may hold values from -1 to 1
- sharpness: float32 [8], replicated, may hold values from 0.5 to 6
- w_query: float32 [32, 32], replicated, may hold values from -0.5 to 0.5
- w_key: float32 [32, 32], replicated, may hold values from -0.5 to 0.5
- w_value: float32 [32, 32], replicated, may hold values from -1 to 1
- w_out: bfloat16 [256, 256], replicated, may hold values from -0.375 to 0.375
- gain_mlp: float32 [256], replicated, may hold values from 0.5 to 1.5
- w_up: bfloat16 [256, 1024], replicated, may hold values from -0.375 to 0.375
- w_down: bfloat16 [1024, 256], replicated, may hold values from -0.1875 to 0.1875
Outputs:
- layer_out: bfloat16 [8192, 256], P(('design', 'pts')), parts along dimension 0
- grad_feat: float32 [512, 256], P(('design', 'pts')), parts along dimension 0
- grad_mid: float32 [512, 256], P(('design', 'pts')), parts along dimension 0
- grad_out: float32 [512, 256], P(('design', 'pts')), parts along dimension 0
- grad_up: float32 [512, 1024], P(('design', 'pts')), parts along dimension 0
- grad_down: float32 [2048, 256], P(('design', 'pts')), parts along dimension 0
- grad_slice: float32 [64, 256], P('design'), parts along dimension 0
- grad_mix: float32 [6, 32, 32], P('design'), parts along dimension 0
There are 2 independent parts, one for each index of `design`. A program takes and returns all parts, laid end to end along the dimension named above; an argument that names none is the same for every part. Nothing has to cross between parts.
Inputs may be any that keep to these rules, and one draw needn't show every extreme that they name: `counts`: every device of a design holds at least half of its 256 slots live, and some device holds all of them.
All inputs are finite; a program needn't handle non-finite values.
Results may differ from a plain program's by a relative error of at most 0.017.
The roundings to bfloat16 on the way count: a program that leaves them out, or rounds other values in their place, can miss the bound.
Values sent between devices are 32-bit elements; how exact they have to be, the bound alone decides.
No kernel may reach another device: no remote copies, remote signals or barrier semaphores. Data moves between devices by JAX's collectives and lax.ppermute only.
A program may use at most 64 MiB of HBM per device.

v0:
```python
import math

import jax
import jax.numpy as jnp
from jax import lax
from jax.sharding import PartitionSpec as P


def layer_norm(inputs, gain):
    inputs = inputs.astype(jnp.float32)
    centre = jnp.mean(inputs, axis=-1, keepdims=True)
    shifted = inputs - centre
    spread = jnp.mean(shifted * shifted, axis=-1, keepdims=True)
    return shifted * lax.rsqrt(spread + 1e-05) * gain


def gelu_tanh(inputs):
    return jax.nn.gelu(inputs, approximate=True)


def project(inputs, gain_attn, w_feat, w_mid):
    normed = layer_norm(inputs, gain_attn).astype(jnp.bfloat16)
    features = jnp.dot(normed, w_feat, preferred_element_type=jnp.float32).astype(jnp.bfloat16)
    middle = jnp.dot(normed, w_mid, preferred_element_type=jnp.float32).astype(jnp.bfloat16)
    return (normed, features, middle)


def slice_shares(middle, w_slice, sharpness):
    count = middle.shape[0]
    heads = sharpness.shape[0]
    logits = jnp.dot(middle.reshape(count * heads, -1), w_slice, preferred_element_type=jnp.float32)
    logits = logits.reshape(count, heads, -1) * sharpness[None, :, None]
    largest = jnp.max(logits, axis=-1, keepdims=True)
    powers = jnp.exp(logits - largest)
    return powers / jnp.sum(powers, axis=-1, keepdims=True)


def slice_scan(middle, features, valid, w_slice, sharpness):
    total = middle.shape[0]
    block = math.gcd(total, 512)
    heads = sharpness.shape[0]
    width = w_slice.shape[0]
    slices = w_slice.shape[1]

    def step(carry, pieces):
        middle_block, feature_block, keep_block = pieces
        shares = slice_shares(middle_block, w_slice, sharpness)
        weights = shares * keep_block[:, None, None]
        weights_low = weights.astype(jnp.bfloat16)
        numerator = jnp.einsum(
            "bhm,bhe->hme",
            weights_low,
            feature_block.reshape(block, heads, width),
            preferred_element_type=jnp.float32,
        )
        return ((carry[0] + numerator, carry[1] + jnp.sum(weights, axis=0)), (shares, weights_low))

    start = (
        jnp.zeros((heads, slices, width), jnp.float32),
        jnp.zeros((heads, slices), jnp.float32),
    )
    sums, kept = lax.scan(
        step,
        start,
        (
            middle.reshape(-1, block, middle.shape[1]),
            features.reshape(-1, block, features.shape[1]),
            valid.reshape(-1, block),
        ),
    )
    return (sums, kept[0].reshape(total, heads, slices), kept[1].reshape(total, heads, slices))


def mix_tokens(numerator, denominator, geo_numerator, geo_denominator, w_query, w_key, w_value):
    highest = lax.Precision.HIGHEST
    field_tokens = numerator / (denominator + 1e-05)[:, :, None]
    geo_tokens = geo_numerator / (geo_denominator + 1e-05)[:, :, None]
    both = jnp.concatenate([field_tokens, geo_tokens], axis=1)
    query = jnp.einsum("hme,ef->hmf", field_tokens, w_query, precision=highest)
    key_rows = jnp.einsum("hke,ef->hkf", both, w_key, precision=highest)
    value_rows = jnp.einsum("hke,ef->hkf", both, w_value, precision=highest)
    scores = jnp.einsum("hmf,hkf->hmk", query, key_rows, precision=highest) / math.sqrt(
        w_query.shape[0]
    )
    largest = jnp.max(scores, axis=-1, keepdims=True)
    powers = jnp.exp(scores - largest)
    attention = powers / jnp.sum(powers, axis=-1, keepdims=True)
    return jnp.einsum("hmk,hkf->hmf", attention, value_rows, precision=highest)


def point_back(
    shares, valid, weights_low, features, grad_att, mixed_low, numer_low, denom_grad, sharpness
):
    count, heads, slices = shares.shape
    grad_weights = (
        jnp.einsum(
            "bhe,hme->bhm",
            features.reshape(count, heads, -1),
            numer_low,
            preferred_element_type=jnp.float32,
        )
        + denom_grad[None]
    )
    if grad_att is not None:
        grad_weights = grad_weights + jnp.einsum(
            "bhe,hme->bhm",
            grad_att.reshape(count, heads, -1),
            mixed_low,
            preferred_element_type=jnp.float32,
        )
    grad_weights = grad_weights * valid[:, None, None]
    inner = jnp.sum(shares * grad_weights, axis=-1, keepdims=True)
    logit_low = (shares * (grad_weights - inner) * sharpness[None, :, None]).astype(jnp.bfloat16)
    grad_features = jnp.einsum(
        "bhm,hme->bhe", weights_low, numer_low, preferred_element_type=jnp.float32
    )
    grad_features = grad_features.reshape(count, -1).astype(jnp.bfloat16)
    return (logit_low, grad_features)


def middle_back(logit_low, middle, w_slice):
    count, heads, slices = logit_low.shape
    flat = logit_low.reshape(count * heads, slices)
    grad_middle = lax.dot_general(
        flat, w_slice, (((1,), (1,)), ((), ())), preferred_element_type=jnp.float32
    )
    grad_middle = grad_middle.reshape(count, -1).astype(jnp.bfloat16)
    slice_term = lax.dot_general(
        middle.reshape(count * heads, -1),
        flat,
        (((0,), (0,)), ((), ())),
        preferred_element_type=jnp.float32,
    )
    return (grad_middle, slice_term)


def outer_rows(left, right):
    return jnp.einsum("rd,rw->dw", left, right, preferred_element_type=jnp.float32)


def on_device(
    points,
    geometry,
    counts,
    cotangent,
    gain_attn,
    w_feat,
    w_mid,
    w_slice,
    sharpness,
    w_query,
    w_key,
    w_value,
    w_out,
    gain_mlp,
    w_up,
    w_down,
):
    point_rows = points.shape[0]
    model_width = points.shape[1]
    heads = sharpness.shape[0]
    width = w_slice.shape[0]
    valid = (jnp.arange(point_rows, dtype=jnp.int32) < counts[0]).astype(jnp.float32)
    geo_valid = jnp.ones((geometry.shape[0],), jnp.float32)
    geo_normed, geo_features, geo_middle = project(geometry, gain_attn, w_feat, w_mid)
    geo_sums, geo_shares, geo_weights_low = slice_scan(
        geo_middle, geo_features, geo_valid, w_slice, sharpness
    )
    normed, features, middle = project(points, gain_attn, w_feat, w_mid)
    field_sums, shares, weights_low = slice_scan(middle, features, valid, w_slice, sharpness)
    numerator, denominator, geo_numerator, geo_denominator = lax.psum(
        (field_sums[0], field_sums[1], geo_sums[0], geo_sums[1]), "pts"
    )
    mixed, token_back = jax.vjp(
        mix_tokens, numerator, denominator, geo_numerator, geo_denominator, w_query, w_key, w_value
    )
    mixed_low = mixed.astype(jnp.bfloat16)
    attended = jnp.einsum(
        "bhm,hme->bhe", weights_low, mixed_low, preferred_element_type=jnp.float32
    )
    attended = attended.reshape(point_rows, -1).astype(jnp.bfloat16)
    residual = points.astype(jnp.float32) + jnp.dot(
        attended, w_out, preferred_element_type=jnp.float32
    )

    def mlp_norm(values_in):
        return layer_norm(values_in, gain_mlp)

    second, norm_back = jax.vjp(mlp_norm, residual)
    second_low = second.astype(jnp.bfloat16)
    upper = jnp.dot(second_low, w_up, preferred_element_type=jnp.float32)
    active, gelu_back = jax.vjp(gelu_tanh, upper)
    hidden = active.astype(jnp.bfloat16)
    layer_out = (residual + jnp.dot(hidden, w_down, preferred_element_type=jnp.float32)).astype(
        jnp.bfloat16
    )
    grad_hidden = lax.dot_general(
        cotangent, w_down, (((1,), (1,)), ((), ())), preferred_element_type=jnp.float32
    )
    grad_upper = gelu_back(grad_hidden)[0].astype(jnp.bfloat16)
    grad_second = lax.dot_general(
        grad_upper, w_up, (((1,), (1,)), ((), ())), preferred_element_type=jnp.float32
    )
    grad_resid = (cotangent.astype(jnp.float32) + norm_back(grad_second)[0]).astype(jnp.bfloat16)
    grad_att = lax.dot_general(
        grad_resid, w_out, (((1,), (1,)), ((), ())), preferred_element_type=jnp.float32
    ).astype(jnp.bfloat16)
    mixed_term = jnp.einsum(
        "bhm,bhe->hme",
        weights_low,
        grad_att.reshape(point_rows, heads, width),
        preferred_element_type=jnp.float32,
    )
    mixed_grad = lax.psum(mixed_term, "pts")
    grads = token_back(mixed_grad)
    numer_low = grads[0].astype(jnp.bfloat16)
    geo_numer_low = grads[2].astype(jnp.bfloat16)
    grad_mix = jnp.stack([grads[4], grads[5], grads[6]])
    logit_low, grad_features = point_back(
        shares, valid, weights_low, features, grad_att, mixed_low, numer_low, grads[1], sharpness
    )
    grad_middle, slice_term = middle_back(logit_low, middle, w_slice)
    geo_logit_low, geo_grad_features = point_back(
        geo_shares,
        geo_valid,
        geo_weights_low,
        geo_features,
        None,
        mixed_low,
        geo_numer_low,
        grads[3],
        sharpness,
    )
    geo_grad_middle, geo_slice_term = middle_back(geo_logit_low, geo_middle, w_slice)
    grad_slice = lax.psum(slice_term + geo_slice_term, "pts")
    field_right = jnp.concatenate([grad_features, grad_middle], axis=1)
    geo_right = jnp.concatenate([geo_grad_features, geo_grad_middle], axis=1)
    grad_down = lax.psum_scatter(
        outer_rows(hidden, cotangent), "pts", scatter_dimension=0, tiled=True
    )
    every_part = lax.psum_scatter(
        jnp.concatenate(
            [
                outer_rows(normed, field_right) + outer_rows(geo_normed, geo_right),
                jnp.concatenate(
                    [outer_rows(attended, grad_resid), outer_rows(second_low, grad_upper)], axis=1
                ),
            ],
            axis=1,
        ),
        "pts",
        scatter_dimension=0,
        tiled=True,
    )
    proj_part = every_part[:, : 2 * model_width]
    grad_out = every_part[:, 2 * model_width : 3 * model_width]
    grad_up = every_part[:, 3 * model_width :]
    grad_feat = proj_part[:, :model_width]
    grad_mid = proj_part[:, model_width:]
    return (layer_out, grad_feat, grad_mid, grad_out, grad_up, grad_down, grad_slice, grad_mix)


def solution(mesh):
    placed = (
        P(("design", "pts"), None),
        P(("design", "pts"), None),
        P(("design", "pts")),
        P(("design", "pts"), None),
        P(),
        P(),
        P(),
        P(),
        P(),
        P(),
        P(),
        P(),
        P(),
        P(),
        P(),
        P(),
    )
    return jax.shard_map(
        on_device,
        mesh=mesh,
        in_specs=placed,
        out_specs=(
            P(("design", "pts"), None),
            P(("design", "pts"), None),
            P(("design", "pts"), None),
            P(("design", "pts"), None),
            P(("design", "pts"), None),
            P(("design", "pts"), None),
            P("design", None),
            P("design", None, None),
        ),
        check_vma=False,
    )
```

profile of v0, /device:TPU:0, one launch (start us, length us, event | category | flops | bytes accessed | tf_op | source)
XLA Modules:
  0.0 438.0 jit_solution(4433066291697078459)
XLA Ops:
  7.3 1.0 copy.56
  8.5 1.2 convolution_convert_fusion.8
  9.7 1.2 convolution_convert_fusion.7
  10.9 1.1 convert_reduce_fusion.1
  12.1 1.2 fusion.59
  13.3 1.4 convolution_convert_fusion.4
  14.8 1.5 convolution_convert_fusion.3
  17.0 2.8 fusion.160
  19.7 3.1 fusion.163
  22.9 2.0 multiply_reduce_fusion.2
  24.9 1.0 fusion.172
  25.9 2.5 fusion.49
  28.5 2.7 fusion.125
  31.2 63.4 %all-reduce = (f32[8,256]{1,0:T(8,128)S(1)}, f32[8,256]{1,0:T(8,128)S(1)}) all-reduce(f32[8,256]{1,0:T(8,128)S(1)} %get-tuple-element.98, f32[8,256]{1,0:T(8,128)S(1)} %fusion.125), channel_id=1, replica_groups=mesh['design'=2,'pts'=16] {'pts'}, use_global_device_ids=true, to_apply=%region_6.7 | all-reduce | flops 4096 | bytes 32768 | tf_op jit(solution)/shard_map/psum | solution.py:171
  95.8 0.8 copy.63
  96.6 1.3 fusion.170
  97.9 23.5 %all-reduce.7.cloned.1.call-done = (f32[8,256,32]{1,2,0:T(8,128)}, f32[8,256,32]{1,2,0:T(8,128)}) async-done(((f32[8,256,32]{1,2,0:T(8,128)}, f32[8,256,32]{1,2,0:T(8,128)}), (f32[8,256,32]{1,2,0:T(8,128)}, f32[8,256,32]{1,2,0:T(8,128)})) %all-reduce.7.cloned.1.call-update) | async-done | bytes 524304 | tf_op jit(solution)/shard_map/psum | solution.py:171
  121.4 1.1 broadcast_divide_fusion.2
  123.0 0.6 fusion.79
  123.6 1.3 fusion.78
  125.0 1.9 copy.60
  126.9 5.2 %fusion.169 = (f32[8,256]{1,0:T(8,128)S(1)}, f32[8,256,512]{2,1,0:T(8,128)}) fusion(f32[8,256,32]{1,2,0:T(8,128)S(1)} %fusion.89, f32[8,512,32]{1,2,0:T(8,128)S(1)} %fusion.79), kind=kOutput, calls=%fused_computation.186 | convolution fusion | flops 404748288 | bytes 4988928 | tf_op jit(solution)/shard_map/jvp(hmf,hkf->hmk)/dot_general | solution.py:82
  132.1 9.7 %online-softmax = f32[8,256,32]{2,1,0:T(8,128)} custom-call(f32[8,256,512]{2,1,0:T(8,128)} %get-tuple-element.120, f32[8,512,32]{2,1,0:T(8,128)} %copy.60), custom_call_target="tpu_custom_call" | custom-call | tf_op online-softmax
  141.7 1.6 convolution_convert_fusion.9
  143.4 1.2 fusion.168
  144.7 3.1 fusion.44
  148.6 0.9 fusion.171
  149.5 1.3 fusion.115
  150.9 1.8 fusion.14
  152.6 1.0 fusion.173
  153.9 1.3 multiply_divide_fusion.2
  155.2 87.9 %all-reduce.5.cloned.1.call-done = f32[8,256,32]{1,2,0:T(8,128)} async-done(((f32[8,256,32]{1,2,0:T(8,128)}), f32[8,256,32]{1,2,0:T(8,128)}) %all-reduce.5.cloned.1.call-update) | async-done | bytes 262160 | tf_op jit(solution)/shard_map/psum | solution.py:214
  243.1 6.7 %convert_reduce_fusion = (f32[8,256]{1,0:T(8,128)S(1)}, pred[8,256,512]{2,1,0:T(32,128)(4,1)S(1)}, f32[8,256]{1,0:T(8,128)S(1)}, f32[8,256,512]{2,1,0:T(8,128)S(1)}) fusion(f32[8,256,512]{2,1,0:T(8,128)} %get-tuple-element.120, f32[8,256]{1,0:T(8,128)S(1)} %get-tuple-element.119, f32[8,256]{1,0:T(8,128)} %multiply_divide_fusion.2, ...), kind=kOutput, calls=%fused_computation.11 | convolution fusion | flops 409989120 | bytes 10256384 | tf_op jit(solution)/shard_map/transpose(jvp(hmk,hkf->hmf))/dot_general | solution.py:88
  249.8 1.5 fusion.158
  251.3 3.4 fusion.12
  254.8 4.7 %fusion.13 = f32[8,256,32]{1,2,0:T(8,128)S(1)} fusion(f32[8,512,32]{1,2,0:T(8,128)S(1)} %fusion.79, f32[8,256,512]{2,1,0:T(8,128)S(1)} %get-tuple-element.94, pred[8,256,512]{2,1,0:T(32,128)(4,1)S(1)} %get-tuple-element.96, f32[8,256]{1,0:T(8,128)S(1)} %negate_divide_fusion), kind=kOutput, calls=%fused_computation.21 | convolution fusion | flops 405798912 | bytes 6037504 | tf_op jit(solution)/shard_map/transpose(jvp(hmf,hkf->hmk))/dot_general | solution.py:82
  259.6 3.8 fusion.7
  266.8 11.1 %fusion.20 = bf16[256,8,256]{2,0,1:T(8,128)(2,1)S(1)} fusion(f32[8,256,256]{1,2,0:T(8,128)S(1)} %add_multiply_fusion.4, f32[8]{0:T(128)S(1)} %copy-done.57, f32[256,8,256]{2,0,1:T(8,128)S(1)} %copy-done.11, f32[256,8]{0,1:T(8,128)S(1)} %copy-done.43), kind=kOutput, calls=%fused_computation.32 | output fusion | flops 3672319 | bytes 5251104 | tf_op jit(solution)/shard_map/sub | solution.py:113
  278.0 4.2 convolution_convert_fusion.2
  282.2 10.2 %fusion.6 = bf16[512,8,256]{2,0,1:T(8,128)(2,1)} fusion(f32[8,256]{1,0:T(8,128)S(1)} %neg.34, f32[8]{0:T(128)S(1)} %copy-done.58, bf16[8,256,32]{1,2,0:T(8,128)(2,1)S(1)} %get-tuple-element.100, bf16[512,8,32]{0,2,1:T(8,128)(2,1)} %bitcast.190, f32[512,8,256]{2,0,1:T(8,128)} %get-tuple-element.112, f32[512,8]{0,1:T(8,128)S(1)} %copy-done.39), kind=kOutput, calls=%fused_computation.9 | convolution fusion | flops 143659264 | bytes 6709280 | tf_op jit(solution)/shard_map/sub | solution.py:113
  292.3 0.8 copy.67
  293.1 1.3 convolution_convert_fusion.1
  294.4 1.2 copy.66
  295.6 1.0 convert_element_type.147
  296.7 1.1 copy.71
  297.8 3.0 convolution_convert_fusion
  300.7 1.3 copy.70
  302.0 2.2 convert_element_type.154
  304.3 1.5 fusion.62
  305.8 1.2 convolution_add_fusion
  307.1 2.3 pad_maximum_fusion
  309.5 1.0 copy.73
  310.5 1.8 copy.74
  312.6 1.7 reshape.203
  314.2 2.6 fusion.34
  316.9 1.7 copy.75
  318.6 2.8 fusion.121
  321.4 2.0 fusion.45
  323.4 3.0 fusion.35
  326.4 60.9 %psum.47 = f32[32,256]{1,0:T(8,128)} all-reduce(f32[32,256]{1,0:T(8,128)S(1)} %fusion.35), channel_id=1, replica_groups=mesh['design'=2,'pts'=16] {'pts'}, use_global_device_ids=true, to_apply=%region_30.31 | all-reduce | flops 8192 | bytes 65536 | tf_op jit(solution)/shard_map/psum | solution.py:235
  388.8 0.6 pad_maximum_fusion.6
  389.4 1.5 slice.22
  390.9 1.4 fusion.159
  392.3 39.0 %reduce-scatter.5.cloned.1.call-done = f32[64,256]{1,0:T(8,128)} async-done(((f32[1024,256]{1,0:T(8,128)}), f32[64,256]{1,0:T(8,128)}) %reduce-scatter.5.cloned.1.call-update) | async-done | bytes 65552 | tf_op jit(solution)/shard_map/reduce_scatter | solution.py:238
  (163 shorter events, 8.1 us)
Async XLA Ops:
  7.2 137.5 %copy-start = (bf16[256,1024]{1,0:T(8,128)(2,1)S(1)}, bf16[256,1024]{1,0:T(8,128)(2,1)}, u32[]{:S(2)}) copy-start(bf16[256,1024]{1,0:T(8,128)(2,1)} %param.30) | copy-start | bytes 1572868
  7.2 12.5 %copy-start.54 = (bf16[32,256]{1,0:T(8,128)(2,1)S(1)}, bf16[32,256]{1,0:T(8,128)(2,1)}, u32[]{:S(2)}) copy-start(bf16[32,256]{1,0:T(8,128)(2,1)} %param.23) | copy-start | bytes 49156
  7.2 12.5 %copy-start.56 = (f32[8]{0:T(128)S(1)}, f32[8]{0:T(128)}, u32[]{:S(2)}) copy-start(f32[8]{0:T(128)} %param.24) | copy-start | bytes 100
  7.2 114.2 %all-reduce.7.cloned.1.call-start = ((), (), s32[]{:S(2)}) async-start(), calls=%async_computation.5 | async-start | bytes 1048576 | tf_op jit(solution)/shard_map/psum | solution.py:171
  8.4 4.9 %copy-start.40 = (f32[256]{0:T(256)}, f32[256]{0:T(256)S(1)}, u32[]{:S(2)}) copy-start(f32[256]{0:T(256)S(1)} %broadcast_multiply_fusion.2) | copy-start | bytes 3076
  8.5 1.2 copy-start.48
  9.7 13.2 %copy-start.27 = (bf16[256,256]{0,1:T(8,128)(2,1)}, bf16[256,256]{0,1:T(8,128)(2,1)S(1)}, u32[]{:S(2)}) copy-start(bf16[256,256]{0,1:T(8,128)(2,1)S(1)} %convolution_convert_fusion.8) | copy-start | bytes 393220
  10.9 14.0 %copy-start.22 = (bf16[256,256]{0,1:T(8,128)(2,1)}, bf16[256,256]{0,1:T(8,128)(2,1)S(1)}, u32[]{:S(2)}) copy-start(bf16[256,256]{0,1:T(8,128)(2,1)S(1)} %convolution_convert_fusion.7) | copy-start | bytes 393220
  12.1 10.8 %copy-start.44 = (f32[512]{0:T(512)}, f32[512]{0:T(512)S(1)}, u32[]{:S(2)}) copy-start(f32[512]{0:T(512)S(1)} %broadcast_multiply_fusion) | copy-start | bytes 6148
  13.3 9.6 %copy-start.51 = (f32[512]{0:T(512)}, f32[512]{0:T(512)S(1)}, u32[]{:S(2)}) copy-start(f32[512]{0:T(512)S(1)} %add_rsqrt_fusion) | copy-start | bytes 6148
  14.8 11.2 %copy-start.26 = (bf16[512,256]{0,1:T(8,128)(2,1)}, bf16[512,256]{0,1:T(8,128)(2,1)S(1)}, u32[]{:S(2)}) copy-start(bf16[512,256]{0,1:T(8,128)(2,1)S(1)} %convolution_convert_fusion.4) | copy-start | bytes 786436
  16.3 9.7 %copy-start.59 = (bf16[512,256]{0,1:T(8,128)(2,1)}, bf16[512,256]{0,1:T(8,128)(2,1)S(1)}, u32[]{:S(2)}) copy-start(bf16[512,256]{0,1:T(8,128)(2,1)S(1)} %convolution_convert_fusion.3) | copy-start | bytes 786436
  16.9 8.0 %copy-start.46 = (f32[256]{0:T(256)}, f32[256]{0:T(256)S(1)}, u32[]{:S(2)}) copy-start(f32[256]{0:T(256)S(1)} %compare_convert_fusion) | copy-start | bytes 3076
  19.7 6.2 %copy-start.42 = (f32[256,8]{0,1:T(8,128)}, f32[256,8]{0,1:T(8,128)S(1)}, u32[]{:S(2)}) copy-start(f32[256,8]{0,1:T(8,128)S(1)} %get-tuple-element.109) | copy-start | bytes 24580
  22.9 5.6 %copy-start.38 = (f32[512,8]{0,1:T(8,128)}, f32[512,8]{0,1:T(8,128)S(1)}, u32[]{:S(2)}) copy-start(f32[512,8]{0,1:T(8,128)S(1)} %get-tuple-element.111) | copy-start | bytes 49156
  28.4 67.4 %copy-start.24 = (bf16[256,256]{1,0:T(8,128)(2,1)S(1)}, bf16[256,256]{1,0:T(8,128)(2,1)}, u32[]{:S(2)}) copy-start(bf16[256,256]{1,0:T(8,128)(2,1)} %param.19) | copy-start | bytes 393220
  28.4 68.1 %copy-start.20 = (bf16[1024,256]{1,0:T(8,128)(2,1)S(1)}, bf16[1024,256]{1,0:T(8,128)(2,1)}, u32[]{:S(2)}) copy-start(bf16[1024,256]{1,0:T(8,128)(2,1)} %param.31) | copy-start | bytes 1572868
  28.4 94.1 %copy-start.34 = (f32[32,32]{1,0:T(8,128)S(1)}, f32[32,32]{1,0:T(8,128)}, u32[]{:S(2)}) copy-start(f32[32,32]{1,0:T(8,128)} %param.25) | copy-start | bytes 12292
  28.4 94.5 %copy-start.32 = (f32[32,32]{1,0:T(8,128)S(1)}, f32[32,32]{1,0:T(8,128)}, u32[]{:S(2)}) copy-start(f32[32,32]{1,0:T(8,128)} %param.26) | copy-start | bytes 12292
  28.5 214.7 %all-reduce.5.cloned.1.call-start = ((), (), s32[]{:S(2)}) async-start(), calls=%async_computation.2 | async-start | bytes 524288 | tf_op jit(solution)/shard_map/psum | solution.py:214
  95.2 29.7 %copy-start.28 = (f32[8,256]{1,0:T(8,128)}, f32[8,256]{1,0:T(8,128)S(1)}, u32[]{:S(2)}) copy-start(f32[8,256]{1,0:T(8,128)S(1)} %get-tuple-element.106) | copy-start | bytes 24580
  122.9 9.1 %copy-start.5 = (f32[8,256,32]{1,2,0:T(8,128)}, f32[8,256,32]{1,2,0:T(8,128)S(1)}, u32[]{:S(2)}) copy-start(f32[8,256,32]{1,2,0:T(8,128)S(1)} %fusion.89) | copy-start | bytes 786436
  124.9 16.8 %copy-start.9 = (f32[8,512,32]{1,2,0:T(8,128)}, f32[8,512,32]{1,2,0:T(8,128)S(1)}, u32[]{:S(2)}) copy-start(f32[8,512,32]{1,2,0:T(8,128)S(1)} %fusion.78) | copy-start | bytes 1572868
  143.4 4.5 %copy-start.50 = (f32[256]{0:T(256)S(1)}, f32[256]{0:T(256)}, u32[]{:S(2)}) copy-start(f32[256]{0:T(256)} %param.29) | copy-start | bytes 3076
  144.6 3.6 copy-start.21
  144.7 3.7 copy-start.19
  147.8 3.0 copy-start.1
  148.6 4.1 copy-start.14
  148.6 94.5 %copy-start.10 = (f32[8,512,32]{1,2,0:T(8,128)S(1)}, f32[8,512,32]{1,2,0:T(8,128)}, u32[]{:S(2)}) copy-start(f32[8,512,32]{1,2,0:T(8,128)} %copy-done.9) | copy-start | bytes 1572868
  153.7 235.8 %reduce-scatter.3.cloned.1.call-start = ((), (), s32[]{:S(2)}) async-start(), calls=%async_computation.3 | async-start | bytes 1949696 | tf_op jit(solution)/shard_map/reduce_scatter | solution.py:241
  243.1 6.7 %copy-start.2 = (f32[8,256,512]{2,1,0:T(8,128)S(1)}, f32[8,256,512]{2,1,0:T(8,128)}, u32[]{:S(2)}) copy-start(f32[8,256,512]{2,1,0:T(8,128)} %get-tuple-element.120) | copy-start | bytes 12582916
  243.1 6.7 %copy-start.30 = (f32[8,256]{1,0:T(8,128)S(1)}, f32[8,256]{1,0:T(8,128)}, u32[]{:S(2)}) copy-start(f32[8,256]{1,0:T(8,128)} %fusion.14) | copy-start | bytes 24580
  249.8 1.5 copy-start.6
  254.8 4.8 %copy-start.53 = (f32[8,256,32]{1,2,0:T(8,128)S(1)}, f32[8,256,32]{1,2,0:T(8,128)}, u32[]{:S(2)}) copy-start(f32[8,256,32]{1,2,0:T(8,128)} %all-reduce.5.cloned.1.call-done) | copy-start | bytes 786436
  259.5 5.2 %copy-start.7 = (f32[8,256,32]{1,2,0:T(8,128)}, f32[8,256,32]{1,2,0:T(8,128)S(1)}, u32[]{:S(2)}) copy-start(f32[8,256,32]{1,2,0:T(8,128)S(1)} %fusion.13) | copy-start | bytes 786436
  259.5 3.9 copy-start.31
  259.5 4.5 %copy-start.33 = (f32[32,32]{1,0:T(8,128)S(1)}, f32[32,32]{1,0:T(8,128)}, u32[]{:S(2)}) copy-start(f32[32,32]{1,0:T(8,128)} %param.26) | copy-start | bytes 12292
  259.5 5.2 %copy-start.18 = (f32[8,256,32]{1,2,0:T(8,128)S(1)}, f32[8,256,32]{1,2,0:T(8,128)}, u32[]{:S(2)}) copy-start(f32[8,256,32]{1,2,0:T(8,128)} %get-tuple-element.91) | copy-start | bytes 786436
  259.6 5.2 %copy-start.35 = (f32[32,32]{1,0:T(8,128)S(1)}, f32[32,32]{1,0:T(8,128)}, u32[]{:S(2)}) copy-start(f32[32,32]{1,0:T(8,128)} %param.25) | copy-start | bytes 12292
  259.6 5.2 %copy-start.37 = (f32[8,256]{1,0:T(8,128)S(1)}, f32[8,256]{1,0:T(8,128)}, u32[]{:S(2)}) copy-start(f32[8,256]{1,0:T(8,128)} %get-tuple-element.105) | copy-start | bytes 24580
  259.6 5.6 %copy-start.23 = (bf16[256,256]{0,1:T(8,128)(2,1)S(1)}, bf16[256,256]{0,1:T(8,128)(2,1)}, u32[]{:S(2)}) copy-start(bf16[256,256]{0,1:T(8,128)(2,1)} %copy-done.22) | copy-start | bytes 393220
  259.6 5.6 %copy-start.29 = (f32[8,256]{1,0:T(8,128)S(1)}, f32[8,256]{1,0:T(8,128)}, u32[]{:S(2)}) copy-start(f32[8,256]{1,0:T(8,128)} %copy-done.28) | copy-start | bytes 24580
  263.4 2.7 copy-start.12
  263.5 2.7 copy-start.3
  263.5 2.7 copy-start.15
  263.5 2.7 copy-start.47
  265.2 1.6 copy-start.11
  265.2 1.6 copy-start.43
  265.2 1.6 copy-start.57
  266.8 11.1 %copy-start.17 = (f32[8,256,32]{1,2,0:T(8,128)S(1)}, f32[8,256,32]{1,2,0:T(8,128)}, u32[]{:S(2)}) copy-start(f32[8,256,32]{1,2,0:T(8,128)} %get-tuple-element.92) | copy-start | bytes 786436
  266.8 11.1 %copy-start.36 = (f32[8,256]{1,0:T(8,128)S(1)}, f32[8,256]{1,0:T(8,128)}, u32[]{:S(2)}) copy-start(f32[8,256]{1,0:T(8,128)} %get-tuple-element.107) | copy-start | bytes 24580
  277.8 15.3 %copy-start.16 = (bf16[256,8,256]{2,0,1:T(8,128)(2,1)}, bf16[256,8,256]{2,0,1:T(8,128)(2,1)S(1)}, u32[]{:S(2)}) copy-start(bf16[256,8,256]{2,0,1:T(8,128)(2,1)S(1)} %fusion.20) | copy-start | bytes 3145732
  277.9 4.2 copy-start.39
  278.0 4.2 copy-start.58
  282.2 10.9 %copy-start.55 = (bf16[32,256]{1,0:T(8,128)(2,1)S(1)}, bf16[32,256]{1,0:T(8,128)(2,1)}, u32[]{:S(2)}) copy-start(bf16[32,256]{1,0:T(8,128)(2,1)} %param.23) | copy-start | bytes 49156
  293.1 11.2 %copy-start.45 = (f32[512]{0:T(512)S(1)}, f32[512]{0:T(512)}, u32[]{:S(2)}) copy-start(f32[512]{0:T(512)} %copy-done.44) | copy-start | bytes 6148
  293.1 11.2 %copy-start.52 = (f32[512]{0:T(512)S(1)}, f32[512]{0:T(512)}, u32[]{:S(2)}) copy-start(f32[512]{0:T(512)} %copy-done.51) | copy-start | bytes 6148
  295.6 10.2 %copy-start.41 = (f32[256]{0:T(256)S(1)}, f32[256]{0:T(256)}, u32[]{:S(2)}) copy-start(f32[256]{0:T(256)} %copy-done.40) | copy-start | bytes 3076
  295.6 10.2 %copy-start.49 = (f32[256]{0:T(256)S(1)}, f32[256]{0:T(256)}, u32[]{:S(2)}) copy-start(f32[256]{0:T(256)} %copy-done.48) | copy-start | bytes 3076
  297.7 9.3 %copy-start.4 = (f32[256,1024]{1,0:T(8,128)S(1)}, f32[256,1024]{1,0:T(8,128)}, u32[]{:S(2)}) copy-start(f32[256,1024]{1,0:T(8,128)} %fusion.115) | copy-start | bytes 3145732
  309.4 9.1 %copy-start.25 = (bf16[256,256]{1,0:T(8,128)(2,1)S(1)}, bf16[256,256]{1,0:T(8,128)(2,1)}, u32[]{:S(2)}) copy-start(bf16[256,256]{1,0:T(8,128)(2,1)} %param.19) | copy-start | bytes 393220
  309.5 121.8 %reduce-scatter.5.cloned.1.call-start = ((), (), s32[]{:S(2)}) async-start(), calls=%async_computation.4 | async-start | bytes 1114112 | tf_op jit(solution)/shard_map/reduce_scatter | solution.py:238
  321.4 66.5 %copy-start.8 = (f32[8,256,32]{1,2,0:T(8,128)S(1)}, f32[8,256,32]{1,2,0:T(8,128)}, u32[]{:S(2)}) copy-start(f32[8,256,32]{1,2,0:T(8,128)} %copy-done.7) | copy-start | bytes 786436
  323.4 64.8 %copy-start.13 = (f32[8,512,32]{1,2,0:T(8,128)S(1)}, f32[8,512,32]{1,2,0:T(8,128)}, u32[]{:S(2)}) copy-start(f32[8,512,32]{1,2,0:T(8,128)} %copy-done.12) | copy-start | bytes 1572868
Sparse Core Ops, SparseCore 0:
  28.6 92.7 all-reduce.6
  153.8 89.2 all-reduce.4
  309.6 61.2 reduce-scatter.2
  374.9 56.3 reduce-scatter.4
where the time goes:
time: 445 us; the launch traced here: 438 us
  waiting for transfers between devices  151 us (34%)
  blocking collectives  124 us (28%)
  matrix products  88.3 us (20%)
  other arithmetic  28.4 us (6%)
  local copies, waits for them, and re-layouts  20.8 us (5%)
  between operations  15.7 us (4%)
  Pallas kernels  9.67 us (2%)
    psum x1, waiting for transfers between devices, on_device(): mixed_grad = lax.psum(mixed_term, 'pts')  87.9 us
    psum x1, blocking collectives, on_device(): lax.psum((field_sums[0], field_sums[1], geo_sums[0], geo_sums[1]), 'pts')  63.4 us
    psum x1, blocking collectives, on_device(): grad_slice = lax.psum(slice_term + geo_slice_term, 'pts')  60.9 us
    reduce_scatter x1, waiting for transfers between devices, on_device(): lax.psum_scatter(outer_rows(hidden, cotangent), 'pts', scatter_dimension=...  39 us
    psum x1, waiting for transfers between devices, on_device(): lax.psum((field_sums[0], field_sums[1], geo_sums[0], geo_sums[1]), 'pts')  23.5 us
    dot_general x3, matrix products, mix_tokens(): jnp.einsum('hmf,hkf->hmk', query, key_rows, precision=highest)  13.3 us
    sub x1, other arithmetic, point_back(): grad_weights - inner  11.1 us
    dot_general x2, matrix products, mix_tokens(): return jnp.einsum('hmk,hkf->hmf', attention, value_rows, precision=highest)  10.5 us
  transfers between devices with their start and end apart: 4, of which 3 were waited for; matrix products, arithmetic and copies ran while one was open for 7% of the time, Pallas kernels for 0%

commit v1 on v0

v1 whole, which is shorter than its diff:
```python
import functools
import math

import jax
import jax.numpy as jnp
from jax import lax
from jax.experimental import pallas as pl
from jax.experimental.pallas import tpu as pltpu
from jax.sharding import PartitionSpec as P

F32 = jnp.float32
BF16 = jnp.bfloat16
HIGHEST = lax.Precision.HIGHEST
EPS = 1e-05
GROUP_BITS = 2
GELU_A = math.sqrt(2.0 / math.pi)
GELU_B = 0.044715

NN = ((1,), (0,))
NT = ((1,), (1,))
TN = ((0,), (0,))


def dot(left, right, dims=NN, precision=None):
    return lax.dot_general(
        left, right, (dims, ((), ())), precision=precision, preferred_element_type=F32
    )


def bit_reverse(value, bits):
    out = 0
    for k in range(bits):
        out = (out << 1) | ((value >> k) & 1)
    return out


def norm_parts(inputs):
    centre = jnp.mean(inputs, axis=-1, keepdims=True)
    shifted = inputs - centre
    spread = jnp.mean(shifted * shifted, axis=-1, keepdims=True)
    return shifted, lax.rsqrt(spread + EPS)


def pad_to(count, unit):
    return -(-count // unit) * unit


def spread_heads(ref, heads, width, slices, block_of):
    ref[...] = jnp.zeros_like(ref)
    for h in range(heads):
        ref[h * width : (h + 1) * width, h * slices : (h + 1) * slices] = block_of(h).astype(BF16)


def sums_kernel(
    counts,
    sharpness,
    points,
    geometry,
    gain,
    w_feat,
    w_mid,
    w_slice,
    keep,
    send,
    normed_out,
    features_out,
    middle_t_out,
    weights_out,
    total,
    slice_map,
):
    me = lax.axis_index("pts")
    rows, model = points.shape
    width, slices = w_slice.shape
    heads = model // width
    groups = total.shape[0]
    per = heads // groups
    bits = groups.bit_length() - 1
    spread_heads(slice_map, heads, width, slices, lambda h: w_slice[...])
    total[...] = jnp.zeros_like(total)
    gain_row = gain[...].reshape(1, model)

    def block(inputs, at, geo):
        shifted, scale = norm_parts(inputs.astype(F32))
        normed = (shifted * scale * gain_row).astype(BF16)
        features = dot(normed, w_feat[...]).astype(BF16)
        middle = dot(normed, w_mid[...]).astype(BF16)
        features_t = features.T
        normed_out[at, :] = normed
        features_out[at, :] = features
        middle_t_out[:, at] = middle.T
        if not geo:
            live = lax.broadcasted_iota(jnp.int32, (rows, 1), 0) < counts[0]
        for h in range(heads):
            cols = slice(h * slices, (h + 1) * slices)
            logits = dot(middle, slice_map[:, cols]) * sharpness[h]
            powers = jnp.exp(logits - jnp.max(logits, axis=1, keepdims=True))
            inverse = 1.0 / jnp.sum(powers, axis=1, keepdims=True)
            if not geo:
                inverse = jnp.where(live, inverse, 0.0)
            weights = powers * inverse
            weights_out[at, cols] = weights
            g, j = h // per, h % per
            num_row = (int(geo) * per + j) * width
            den_row = 2 * per * width + int(geo) * per + j
            total[g, num_row : num_row + width, :] += dot(
                features_t[h * width : (h + 1) * width], weights.astype(BF16)
            )
            total[g, den_row : den_row + 1, :] += jnp.sum(weights, axis=0, keepdims=True)

    block(points[...], pl.ds(0, rows), False)

    @pl.loop(0, geometry.shape[0] // rows)
    def _(i):
        start = pl.multiple_of(i * rows, rows)
        block(geometry[pl.ds(start, rows), :], pl.ds(pl.multiple_of(start + rows, rows), rows), True)

    for pos in range(groups):
        value = total[bit_reverse(pos, bits) ^ (me & (groups - 1))]
        if pos < groups // 2:
            keep[pos] = value
        else:
            send[pos - groups // 2] = value


def token_rows(tokens, j, per, width):
    base = 2 * per * width
    out = []
    for geo in range(2):
        row = (geo * per + j) * width
        den = tokens[base + geo * per + j : base + geo * per + j + 1, :] + EPS
        out.append((tokens[row : row + width, :] / den, den))
    return out


def mix_kernel(tokens, w_query, w_key, w_value, mixed_out, attention_out):
    width = w_query.shape[0]
    per = attention_out.shape[0]
    for j in range(per):
        (field, _), (geo, _) = token_rows(tokens, j, per, width)
        both = jnp.concatenate([field, geo], axis=1)
        query = dot(w_query[...], field, TN, HIGHEST)
        keys = dot(w_key[...], both, TN, HIGHEST)
        values = dot(w_value[...], both, TN, HIGHEST)
        scores = dot(keys, query, TN, HIGHEST) / math.sqrt(width)
        powers = jnp.exp(scores - jnp.max(scores, axis=0, keepdims=True))
        attention = powers * (1.0 / jnp.sum(powers, axis=0, keepdims=True))
        attention_out[j] = attention
        mixed_out[j * width : (j + 1) * width, :] = dot(values, attention, NN, HIGHEST)


def mix_back_kernel(tokens, attention_in, grad, w_query, w_key, w_value, out):
    width = w_query.shape[0]
    per, both_count, slices = attention_in.shape
    base = 2 * per * width
    small = jnp.zeros((width, 3 * width), F32)
    out[base : base + 8 * pl.cdiv(2 * per, 8), :] = jnp.zeros((8 * pl.cdiv(2 * per, 8), slices), F32)
    for j in range(per):
        (field, field_den), (geo, geo_den) = token_rows(tokens, j, per, width)
        both = jnp.concatenate([field, geo], axis=1)
        query = dot(w_query[...], field, TN, HIGHEST)
        keys = dot(w_key[...], both, TN, HIGHEST)
        values = dot(w_value[...], both, TN, HIGHEST)
        attention = attention_in[j]
        mixed_grad = grad[j * width : (j + 1) * width, :]
        att_grad = dot(values, mixed_grad, TN, HIGHEST)
        inner = jnp.sum(attention * att_grad, axis=0, keepdims=True)
        score_grad = attention * (att_grad - inner) * (1.0 / math.sqrt(width))
        value_grad = dot(mixed_grad, attention, NT, HIGHEST)
        query_grad = dot(keys, score_grad, NN, HIGHEST)
        key_grad = dot(query, score_grad, NT, HIGHEST)
        both_grad = dot(w_key[...], key_grad, NN, HIGHEST) + dot(
            w_value[...], value_grad, NN, HIGHEST
        )
        field_grad = both_grad[:, :slices] + dot(w_query[...], query_grad, NN, HIGHEST)
        geo_grad = both_grad[:, slices:]
        small += jnp.concatenate(
            [
                dot(field, query_grad, NT, HIGHEST),
                dot(both, key_grad, NT, HIGHEST),
                dot(both, value_grad, NT, HIGHEST),
            ],
            axis=1,
        )
        for g, (value, den, value_of) in enumerate(
            ((field_grad, field_den, field), (geo_grad, geo_den, geo))
        ):
            row = (g * per + j) * width
            scaled = value / den
            out[row : row + width, :] = scaled
            out[base + g * per + j : base + g * per + j + 1, :] = -jnp.sum(
                scaled * value_of, axis=0, keepdims=True
            )
    half = width // 2
    filler = jnp.zeros((width, slices // 2 - 3 * width), F32)
    wide = jnp.concatenate([small, filler], axis=1)
    out[out.shape[0] - half :, :] = jnp.concatenate([wide[:half], wide[half:]], axis=1)


def mlp_kernel(
    rel,
    *refs,
):
    groups = len(rel)
    pieces = refs[:groups]
    (
        weights,
        points,
        cotangent,
        w_out,
        gain,
        w_up,
        w_down,
        layer_out,
        grad_att_out,
        keep,
        send,
        attended_out,
        second_out,
        hidden_out,
        grad_upper_out,
        grad_resid_out,
        canon,
        mix_map,
    ) = refs[groups:]
    me = lax.axis_index("pts")
    model = points.shape[1]
    slices = canon.shape[2]
    heads = weights.shape[1] // slices
    width = model // heads
    per = heads // groups
    bits = groups.bit_length() - 1
    mine = me & (groups - 1)
    for r, piece in zip(rel, pieces):
        canon[mine ^ r] = piece[...]
    spread_heads(
        mix_map,
        heads,
        width,
        slices,
        lambda h: canon[h // per, (h % per) * width : (h % per + 1) * width, :],
    )
    gain_row = gain[...].reshape(1, model)
    weights_low = weights[...].astype(BF16)
    attended = dot(weights_low, mix_map[...], NT).astype(BF16)
    attended_out[...] = attended
    residual = points[...].astype(F32) + dot(attended, w_out[...])
    shifted, scale = norm_parts(residual)
    unit = shifted * scale
    second = (unit * gain_row).astype(BF16)
    second_out[...] = second
    upper = dot(second, w_up[...])
    square = upper * upper
    slope = jnp.tanh(GELU_A * upper * (1.0 + GELU_B * square))
    half = 0.5 * (1.0 + slope)
    hidden = (upper * half).astype(BF16)
    hidden_out[...] = hidden
    curve = half + 0.5 * upper * (1.0 - slope * slope) * (
        GELU_A * (1.0 + 3.0 * GELU_B * square)
    )
    layer_out[...] = (residual + dot(hidden, w_down[...])).astype(BF16)
    grad_upper = (dot(cotangent[...], w_down[...], NT) * curve).astype(BF16)
    grad_upper_out[...] = grad_upper
    grad_unit = dot(grad_upper, w_up[...], NT) * gain_row
    grad_norm = scale * (
        grad_unit
        - jnp.mean(grad_unit, axis=-1, keepdims=True)
        - unit * jnp.mean(grad_unit * unit, axis=-1, keepdims=True)
    )
    grad_resid = (cotangent[...].astype(F32) + grad_norm).astype(BF16)
    grad_resid_out[...] = grad_resid
    grad_att = dot(grad_resid, w_out[...], NT).astype(BF16)
    grad_att_out[...] = grad_att
    grad_att_t = grad_att.T
    for h in range(heads):
        j = h % per
        canon[h // per, j * width : (j + 1) * width, :] = dot(
            grad_att_t[h * width : (h + 1) * width],
            weights[:, h * slices : (h + 1) * slices].astype(BF16),
        )
    for pos in range(groups):
        value = canon[bit_reverse(pos, bits) ^ mine]
        if pos < groups // 2:
            keep[pos] = value
        else:
            send[pos - groups // 2] = value


def outer_kernel(attended, second, hidden, grad_upper, grad_resid, cotangent, out):
    inner, outer, rows, model = out.shape
    parts = inner * outer
    step = model // parts
    wide = hidden.shape[1] // model
    grad_out = dot(attended[...], grad_resid[...], TN)
    grad_up = dot(second[...], grad_upper[...], TN)
    grad_down = dot(hidden[...], cotangent[...], TN)
    for p in range(parts):
        lo, hi = p % inner, p // inner
        at = slice(p * step, (p + 1) * step)
        out[lo, hi, :step, :] = grad_out[at]
        for w in range(wide):
            out[lo, hi, step * (1 + w) : step * (2 + w), :] = grad_up[
                at, w * model : (w + 1) * model
            ]
        out[lo, hi, step * (1 + wide) :, :] = grad_down[p * step * wide : (p + 1) * step * wide]


def back_kernel(rel, sharpness, *refs):
    groups = len(rel)
    pieces = refs[:groups]
    mixed = refs[groups : 2 * groups]
    (
        weights,
        features,
        middle_t,
        normed,
        grad_att,
        w_slice,
        keep,
        send,
        slice_out,
        grad_mix,
        canon,
        mix_canon,
        mix_map,
        field_map,
        geo_map,
        slice_map,
        logit,
        right,
        total,
    ) = refs[2 * groups :]
    me = lax.axis_index("pts")
    rows, model = grad_att.shape
    width, slices = w_slice.shape
    heads = model // width
    per = heads // groups
    mine = me & (groups - 1)
    base = 2 * per * width
    for r, piece, mix_piece in zip(rel, pieces, mixed):
        canon[mine ^ r] = piece[...]
        mix_canon[mine ^ r] = mix_piece[...]

    def rows_of(ref, offset):
        def of(h):
            row = (offset * per + h % per) * width
            return ref[h // per, row : row + width, :]

        return of

    spread_heads(mix_map, heads, width, slices, rows_of(mix_canon, 0))
    spread_heads(field_map, heads, width, slices, rows_of(canon, 0))
    spread_heads(geo_map, heads, width, slices, rows_of(canon, 1))
    spread_heads(slice_map, heads, width, slices, lambda h: w_slice[...])
    slice_out[...] = jnp.zeros_like(slice_out)

    def block(at, geo):
        numer_map = geo_map if geo else field_map
        feats = features[at, :]
        low = weights[at, :].astype(BF16)
        grad_features = dot(low, numer_map[...], NT)
        right[at, :model] = grad_features.astype(BF16)
        for h in range(heads):
            cols = slice(h * slices, (h + 1) * slices)
            den_row = base + int(geo) * per + h % per
            grad_weights = dot(feats, numer_map[:, cols]) + canon[
                h // per, den_row : den_row + 1, :
            ]
            if not geo:
                grad_weights += dot(grad_att[...], mix_map[:, cols])
            share = weights[at, cols]
            inner = jnp.sum(share * grad_weights, axis=1, keepdims=True)
            low_logit = (share * (grad_weights - inner) * sharpness[h]).astype(BF16)
            logit[:, cols] = low_logit
            slice_out[...] += dot(middle_t[h * width : (h + 1) * width, at], low_logit)
        right[at, model:] = dot(logit[...], slice_map[...], NT).astype(BF16)

    block(pl.ds(0, rows), False)

    @pl.loop(1, normed.shape[0] // rows)
    def _(i):
        block(pl.ds(pl.multiple_of(i * rows, rows), rows), True)

    total[...] = dot(normed[...], right[...], TN)
    half = keep.shape[0]
    step = keep.shape[1] // 2
    bits = (2 * half).bit_length() - 1
    for pos in range(2 * half):
        start = pl.multiple_of((bit_reverse(pos, bits) ^ me) * step, step)
        value = total[pl.ds(start, step), :]
        target = keep if pos < half else send
        target[pos % half, :step, :] = value[:, :model]
        target[pos % half, step:, :] = value[:, model:]

    small_rows = width // 2
    packed = canon[0, canon.shape[1] - small_rows :, :]
    for g in range(1, groups):
        packed += canon[g, canon.shape[1] - small_rows :, :]
    wide = jnp.concatenate([packed[:, : slices // 2], packed[:, slices // 2 :]], axis=0)
    for i in range(3):
        grad_mix[i] = wide[:, i * width : (i + 1) * width]


VMEM = pl.BlockSpec(memory_space=pltpu.VMEM)
SMEM = pl.BlockSpec(memory_space=pltpu.SMEM)


def shape(dims, dtype=F32):
    return jax.ShapeDtypeStruct(tuple(dims), dtype)


def run(body, in_specs, out_shape, scratch, name, *args):
    return pl.pallas_call(
        body,
        out_shape=out_shape,
        in_specs=in_specs,
        out_specs=jax.tree.map(lambda _: VMEM, out_shape),
        scratch_shapes=scratch,
        compiler_params=pltpu.CompilerParams(vmem_limit_bytes=56 * 1024 * 1024),
        name=name,
    )(*args)


def on_device(
    parts,
    points,
    geometry,
    counts,
    cotangent,
    gain_attn,
    w_feat,
    w_mid,
    w_slice,
    sharpness,
    w_query,
    w_key,
    w_value,
    w_out,
    gain_mlp,
    w_up,
    w_down,
):
    rows, model = points.shape
    all_rows = rows + geometry.shape[0]
    width, slices = w_slice.shape
    heads = sharpness.shape[0]
    hidden_width = w_up.shape[1]
    all_bits = parts.bit_length() - 1
    bits = min(GROUP_BITS, all_bits)
    groups = 1 << bits
    per = heads // groups
    token_height = 2 * per * width + pad_to(2 * per, 8)
    grad_height = token_height + width // 2
    half = groups // 2

    def exchange(value, bit):
        return lax.ppermute(value, "pts", [(i, i ^ (1 << bit)) for i in range(parts)])

    def halve(keep, send, first, last):
        for bit in range(first, last):
            got = exchange(send, bit)
            if bit < last - 1:
                count = keep.shape[0] // 2
                keep, send = keep[:count] + got[:count], keep[count:] + got[count:]
            else:
                keep = keep + got
        return keep

    def add_all(value, first, last):
        for bit in range(first, last):
            value = value + exchange(value, bit)
        return value

    def collect(value):
        pieces, rel = [value], [0]
        for bit in reversed(range(bits)):
            pieces = pieces + [exchange(piece, bit) for piece in pieces]
            rel = rel + [r ^ (1 << bit) for r in rel]
        return pieces, tuple(rel)

    keep, send, normed, features, middle_t, weights = run(
        sums_kernel,
        [SMEM, SMEM] + [VMEM] * 6,
        (
            shape((half, token_height, slices)),
            shape((half, token_height, slices)),
            shape((all_rows, model), BF16),
            shape((all_rows, model), BF16),
            shape((model, all_rows), BF16),
            shape((all_rows, heads * slices)),
        ),
        [
            pltpu.VMEM((groups, token_height, slices), F32),
            pltpu.VMEM((model, heads * slices), BF16),
        ],
        "slice_sums",
        counts,
        sharpness,
        points,
        geometry,
        gain_attn,
        w_feat,
        w_mid,
        w_slice,
    )
    tokens = add_all(halve(keep, send, 0, bits)[0], bits, all_bits)
    mixed, attention = run(
        mix_kernel,
        [VMEM] * 4,
        (shape((per * width, slices)), shape((per, 2 * slices, slices))),
        [],
        "mix_tokens",
        tokens,
        w_query,
        w_key,
        w_value,
    )
    mixed_pieces, rel = collect(mixed)
    (
        layer_out,
        grad_att,
        keep,
        send,
        attended,
        second,
        hidden,
        grad_upper,
        grad_resid,
    ) = run(
        functools.partial(mlp_kernel, rel),
        [VMEM] * (groups + 7),
        (
            shape((rows, model), BF16),
            shape((rows, model), BF16),
            shape((half, per * width, slices)),
            shape((half, per * width, slices)),
            shape((rows, model), BF16),
            shape((rows, model), BF16),
            shape((rows, hidden_width), BF16),
            shape((rows, hidden_width), BF16),
            shape((rows, model), BF16),
        ),
        [
            pltpu.VMEM((groups, per * width, slices), F32),
            pltpu.VMEM((model, heads * slices), BF16),
        ],
        "mlp",
        *mixed_pieces,
        weights[:rows],
        points,
        cotangent,
        w_out,
        gain_mlp,
        w_up,
        w_down,
    )
    mixed_grad = add_all(halve(keep, send, 0, bits)[0], bits, all_bits)
    step = model // parts
    wide = hidden_width // model
    outer = run(
        outer_kernel,
        [VMEM] * 6,
        shape((groups, parts // groups, step * (1 + 2 * wide), model)),
        [],
        "weight_grads",
        attended,
        second,
        hidden,
        grad_upper,
        grad_resid,
        cotangent,
    )
    near = [[g * groups + i for i in range(groups)] for g in range(parts // groups)]
    far = [[g * groups + i for g in range(parts // groups)] for i in range(groups)]
    outer = lax.psum_scatter(
        outer, "pts", scatter_dimension=0, axis_index_groups=near, tiled=False
    )
    outer = lax.psum_scatter(outer, "pts", scatter_dimension=0, axis_index_groups=far, tiled=False)
    token_grad = run(
        mix_back_kernel,
        [VMEM] * 6,
        shape((grad_height, slices)),
        [],
        "mix_back",
        tokens,
        attention,
        mixed_grad,
        w_query,
        w_key,
        w_value,
    )
    grad_pieces, rel = collect(token_grad)
    keep, send, slice_sum, grad_mix = run(
        functools.partial(back_kernel, rel),
        [SMEM] + [VMEM] * (2 * groups + 6),
        (
            shape((parts // 2, 2 * step, model)),
            shape((parts // 2, 2 * step, model)),
            shape((width, slices)),
            shape((3, width, width)),
        ),
        [
            pltpu.VMEM((groups, grad_height, slices), F32),
            pltpu.VMEM((groups, per * width, slices), F32),
        ]
        + [pltpu.VMEM((model, heads * slices), BF16)] * 4
        + [
            pltpu.VMEM((rows, heads * slices), BF16),
            pltpu.VMEM((all_rows, 2 * model), BF16),
            pltpu.VMEM((model, 2 * model), F32),
        ],
        "point_back",
        sharpness,
        *grad_pieces,
        *mixed_pieces,
        weights,
        features,
        middle_t,
        normed,
        grad_att,
        w_slice,
    )
    for bit in range(all_bits):
        joined = jnp.concatenate([send.reshape(-1, model), slice_sum], axis=0)
        got = exchange(joined, bit)
        count = keep.shape[0]
        part = got[: count * 2 * step].reshape(keep.shape)
        slice_sum = slice_sum + got[count * 2 * step :]
        if bit < all_bits - 1:
            count //= 2
            keep, send = keep[:count] + part[:count], keep[count:] + part[count:]
        else:
            keep = keep + part
    grad_feat = keep[0, :step]
    grad_mid = keep[0, step:]
    grad_out = outer[:step]
    grad_up = jnp.concatenate(
        [outer[step * (1 + w) : step * (2 + w)] for w in range(wide)], axis=1
    )
    grad_down = outer[step * (1 + wide) :]
    return (layer_out, grad_feat, grad_mid, grad_out, grad_up, grad_down, slice_sum, grad_mix)


def solution(mesh):
    split = P(("design", "pts"), None)
    placed = (split, split, P(("design", "pts")), split) + (P(),) * 12
    return jax.shard_map(
        functools.partial(on_device, mesh.shape["pts"]),
        mesh=mesh,
        in_specs=placed,
        out_specs=(split,) * 6 + (P("design", None), P("design", None, None)),
        check_vma=False,
    )
```

time: 445 us -> 163 us (0.37); the launches traced: 438 us -> 163 us
  blocking collectives: 124 us -> 0 us
  matrix products: 88.3 us -> 0 us
  waiting for transfers between devices: 151 us -> 67.6 us
  Pallas kernels: 9.67 us -> 48.6 us
  other arithmetic: 28.4 us -> 7.31 us
  starting transfers between devices: 0.38 us -> 15.7 us
  local copies, waits for them, and re-layouts: 20.8 us -> 8.65 us
    psum x2 -> x0, blocking collectives: 124 us -> none  [the longest x1 63.4 us: on_device(): lax.psum((field_sums[0], field_sums[1], geo_sums[0], geo_sums[1]), 'pts')]
    psum x2 -> x0, waiting for transfers between devices: 111 us -> none  [the longest x1 87.9 us: on_device(): mixed_grad = lax.psum(mixed_term, 'pts')]
    dot_general x41 -> x0, matrix products: 72.2 us -> none  [the longest x3 13.3 us: mix_tokens(): jnp.einsum('hmf,hkf->hmk', query, key_rows, precision=highest)]
    ppermute x0 -> x18, waiting for transfers between devices: none -> 57 us  [exchange(): return lax.ppermute(value, 'pts', [(i, i ^ 1 << bit) for i in range(parts)])]
    pallas_call x0 -> x6, Pallas kernels: none -> 48.6 us  [run(): pl.pallas_call(body, out_shape=out_shape, in_specs=in_specs, out_specs=ja...]
    reduce_scatter x2, waiting for transfers between devices: 39 us -> 10.5 us  [the longest x1 10.5 us: on_device(): lax.psum_scatter(outer, 'pts', scatter_dimension=0, axis_index_groups=far...]
    sub x3 -> x0, matrix products: 16.1 us -> none  [the longest x1 10.2 us: point_back(): grad_weights - inner]
    ppermute x0 -> x18, starting transfers between devices: none -> 15.4 us  [exchange(): return lax.ppermute(value, 'pts', [(i, i ^ 1 << bit) for i in range(parts)])]
  transfers between devices with their start and end apart: 4 -> 20, of which waited for: 3 -> 16; matrix products, arithmetic and copies ran while one was open for 7% -> 5% of each run, Pallas kernels for 0% -> 12%
where the time goes in v1:
time: 163 us
  waiting for transfers between devices  67.6 us (41%)
  Pallas kernels  48.6 us (30%)
  starting transfers between devices  15.7 us (10%)
  between operations  14.8 us (9%)
  local copies, waits for them, and re-layouts  8.65 us (5%)
  other arithmetic  7.31 us (4%)
    ppermute x18, waiting for transfers between devices, exchange(): return lax.ppermute(value, 'pts', [(i, i ^ 1 << bit) for i in range(parts)])  57 us
    pallas_call x6, Pallas kernels, run(): pl.pallas_call(body, out_shape=out_shape, in_specs=in_specs, out_specs=ja...  48.6 us
    ppermute x18, starting transfers between devices, exchange(): return lax.ppermute(value, 'pts', [(i, i ^ 1 << bit) for i in range(parts)])  15.4 us
    reduce_scatter x1, waiting for transfers between devices, on_device(): lax.psum_scatter(outer, 'pts', scatter_dimension=0, axis_index_groups=far...  10.5 us
  transfers between devices with their start and end apart: 20, of which 16 were waited for; matrix products, arithmetic and copies ran while one was open for 5% of the time, Pallas kernels for 12%

profile of v1, /device:TPU:0, one launch (start us, length us, event | category | flops | bytes accessed | tf_op | source)
XLA Modules:
  0.0 162.6 jit_solution(4218447121623413496)
XLA Ops:
  7.2 0.0 reduce-scatter.3.cloned.1.call-start
  7.9 14.6 %slice_sums.1 = (f32[2,136,256]{2,1,0:T(8,128)}, f32[2,136,256]{2,1,0:T(8,128)}, bf16[768,256]{1,0:T(8,128)(2,1)}, bf16[768,256]{1,0:T(8,128)(2,1)}, bf16[256,768]{1,0:T(8,128)(2,1)}, /*index=5*/f32[768,2048]{1,0:T(8,128)}) custom-call(s32[1]{0:T(128)S(6)} %copy.24.counts, f32[8]{0:T(128)} %sharpness.3, bf16[256,256]{1,0:T(8,128)(2,1)} %refs_5_.1, ...), custom_call_target="tpu_custom_call" | custom-call | tf_op jit(solution)/shard_map/slice_sums/pallas_call | solution.py:413
  22.5 0.5 collective-permute-start
  23.0 1.4 collective-permute-done
  24.3 0.9 slice_add_fusion
  25.3 3.0 %collective-permute-start.1 = (f32[1,136,256]{2,1,0:T(8,128)S(1)}, f32[1,136,256]{2,1,0:T(8,128)S(1)}, u32[]{:S(2)}, u32[]{:S(2)}) collective-permute-start(f32[1,136,256]{2,1,0:T(8,128)S(1)} %slice_add_fusion), channel_id=1, source_target_pairs={{0,2},{1,3},{2,0},{3,1},{4,6},{5,7},{6,4},{7,5},{8,10},{9,11},{10,... | collective-permute-start | bytes 417800 | tf_op jit(solution)/shard_map/ppermute | solution.py:457
  28.2 4.0 %collective-permute-done.1 = f32[1,136,256]{2,1,0:T(8,128)S(1)} collective-permute-done((f32[1,136,256]{2,1,0:T(8,128)S(1)}, f32[1,136,256]{2,1,0:T(8,128)S(1)}, u32[]{:S(2)}, u32[]{:S(2)}) %collective-permute-start.1) | collective-permute-done | bytes 139296 | tf_op jit(solution)/shard_map/ppermute | solution.py:457
  32.2 0.9 fusion.1
  33.1 1.9 %collective-permute-start.2 = (f32[136,256]{1,0:T(8,128)S(1)}, f32[136,256]{1,0:T(8,128)S(1)}, u32[]{:S(2)}, u32[]{:S(2)}) collective-permute-start(f32[136,256]{1,0:T(8,128)S(1)} %fusion.1), channel_id=1, source_target_pairs={{0,4},{1,5},{2,6},{3,7},{4,0},{5,1},{6,2},{7,3},{8,12},{9,13},{10,... | collective-permute-start | bytes 417800 | tf_op jit(solution)/shard_map/ppermute | solution.py:457
  35.0 3.4 %collective-permute-done.2 = f32[136,256]{1,0:T(8,128)S(1)} collective-permute-done((f32[136,256]{1,0:T(8,128)S(1)}, f32[136,256]{1,0:T(8,128)S(1)}, u32[]{:S(2)}, u32[]{:S(2)}) %collective-permute-start.2) | collective-permute-done | bytes 139296 | tf_op jit(solution)/shard_map/ppermute | solution.py:457
  38.4 2.7 %collective-permute-start.3 = (f32[136,256]{1,0:T(8,128)S(1)}, f32[136,256]{1,0:T(8,128)S(1)}, u32[]{:S(2)}, u32[]{:S(2)}) collective-permute-start(f32[136,256]{1,0:T(8,128)S(1)} %add.70), channel_id=1, source_target_pairs={{0,8},{1,9},{2,10},{3,11},{4,12},{5,13},{6,14},{7,15},{8,0},{9,1},... | collective-permute-start | bytes 417800 | tf_op jit(solution)/shard_map/ppermute | solution.py:457
  41.2 5.5 %collective-permute-done.3 = f32[136,256]{1,0:T(8,128)S(1)} collective-permute-done((f32[136,256]{1,0:T(8,128)S(1)}, f32[136,256]{1,0:T(8,128)S(1)}, u32[]{:S(2)}, u32[]{:S(2)}) %collective-permute-start.3) | collective-permute-done | bytes 139296 | tf_op jit(solution)/shard_map/ppermute | solution.py:457
  46.7 0.7 add.71.tokens
  47.4 5.2 %mix_tokens.1 = (f32[64,256]{1,0:T(8,128)}, f32[2,512,256]{2,1,0:T(8,128)}) custom-call(f32[136,256]{1,0:T(8,128)} %add.71.tokens, f32[32,32]{1,0:T(8,128)} %w_query.3, f32[32,32]{1,0:T(8,128)} %w_key.3, f32[32,32]{1,0:T(8,128)} %w_value.3), custom_call_target="tpu_custom_call" | custom-call | tf_op jit(solution)/shard_map/mix_tokens/pallas_call | solution.py:413
  52.5 1.0 collective-permute-start.4
  53.6 0.0 collective-permute-start.5
  53.6 3.5 %collective-permute-done.4.refs_1_.refs_5_ = f32[64,256]{1,0:T(8,128)S(1)} collective-permute-done((f32[64,256]{1,0:T(8,128)}, f32[64,256]{1,0:T(8,128)S(1)}, u32[]{:S(2)}, u32[]{:S(2)}) %collective-permute-start.4) | collective-permute-done | bytes 65568 | tf_op jit(solution)/shard_map/ppermute | solution.py:457
  57.0 0.0 collective-permute-start.6
  57.0 3.2 %slice.151.refs_4_ = f32[256,2048]{1,0:T(8,128)} slice(f32[768,2048]{1,0:T(8,128)} %get-tuple-element.32.refs_8_), slice={[0:256], [0:2048]} | slice | bytes 4194304 | tf_op jit(solution)/shard_map/slice | solution.py:549
  60.3 0.0 collective-permute-done.5.refs_2_.refs_6_
  60.3 0.0 collective-permute-done.6.refs_3_.refs_7_
  60.3 0.6 copy-done.1
  60.9 0.6 copy-done.2
  61.5 5.6 %mlp.1 = (bf16[256,256]{1,0:T(8,128)(2,1)}, bf16[256,256]{1,0:T(8,128)(2,1)}, f32[2,64,256]{2,1,0:T(8,128)}, f32[2,64,256]{2,1,0:T(8,128)}, bf16[256,256]{1,0:T(...) custom-call(f32[64,256]{1,0:T(8,128)} %get-tuple-element.31.refs_0_., ...), custom_call_target="tpu_custom_call" | custom-call | tf_op jit(solution)/shard_map/mlp/pallas_call | solution.py:413
  67.2 3.4 %weight_grads.1 = f32[4,4,144,256]{3,2,1,0:T(8,128)} custom-call(bf16[256,256]{1,0:T(8,128)(2,1)} %get-tuple-element.44.attended, bf16[256,256]{1,0:T(8,128)(2,1)} %get-tuple-element.45.second, bf16[256,1024]{1,0:T(8,128)(2,1)} %get-tuple-element.46.hidden, bf16[256,1024]{1,0:T(8,128)(2,1)} %get-tuple-element.47.grad_upper, ...), custom_call_target="tpu_custom_call" | custom-call | tf_op jit(solution)/shard_map/weight_grads/pallas_call | solution.py:413
  70.6 0.0 reduce-scatter.3.cloned.1.call-update
  70.6 0.2 reduce-scatter.5.cloned.1.call-start
  70.8 0.5 collective-permute-start.7
  71.4 1.0 collective-permute-done.7
  72.4 1.1 collective-permute-start.8
  73.5 3.3 %collective-permute-done.8 = f32[1,64,256]{2,1,0:T(8,128)S(1)} collective-permute-done((f32[1,64,256]{2,1,0:T(8,128)S(1)}, f32[1,64,256]{2,1,0:T(8,128)S(1)}, u32[]{:S(2)}, u32[]{:S(2)}) %collective-permute-start.8) | collective-permute-done | bytes 65568 | tf_op jit(solution)/shard_map/ppermute | solution.py:457
  76.8 0.2 collective-permute-start.9
  77.1 4.1 %collective-permute-done.9 = f32[64,256]{1,0:T(8,128)S(1)} collective-permute-done((f32[64,256]{1,0:T(8,128)S(1)}, f32[64,256]{1,0:T(8,128)S(1)}, u32[]{:S(2)}, u32[]{:S(2)}) %collective-permute-start.9) | collective-permute-done | bytes 65568 | tf_op jit(solution)/shard_map/ppermute | solution.py:457
  81.2 1.6 collective-permute-start.10
  82.8 4.3 %collective-permute-done.10 = f32[64,256]{1,0:T(8,128)S(1)} collective-permute-done((f32[64,256]{1,0:T(8,128)S(1)}, f32[64,256]{1,0:T(8,128)S(1)}, u32[]{:S(2)}, u32[]{:S(2)}) %collective-permute-start.10) | collective-permute-done | bytes 65568 | tf_op jit(solution)/shard_map/ppermute | solution.py:457
  87.1 0.6 add.76.grad
  87.7 7.6 %mix_back.1.refs_0_ = f32[152,256]{1,0:T(8,128)} custom-call(f32[136,256]{1,0:T(8,128)} %add.71.tokens, f32[2,512,256]{2,1,0:T(8,128)} %get-tuple-element.34.attention_in, f32[64,256]{1,0:T(8,128)} %add.76.grad, f32[32,32]{1,0:T(8,128)} %w_query.3, f32[32,32]{1,0:T(8,128)} %w_key.3, f32[32,32]{1,0:T(8,128)} %w_value.3), custom_call_target="tpu_custom_call" | custom-call | tf_op jit(solution)/shard_map/mix_back/pallas_call | solution.py:413
  95.3 0.8 collective-permute-start.11
  96.2 0.0 collective-permute-start.12
  96.2 8.3 %collective-permute-done.11.refs_1_ = f32[152,256]{1,0:T(8,128)S(1)} collective-permute-done((f32[152,256]{1,0:T(8,128)}, f32[152,256]{1,0:T(8,128)S(1)}, u32[]{:S(2)}, u32[]{:S(2)}) %collective-permute-start.11) | collective-permute-done | bytes 155680 | tf_op jit(solution)/shard_map/ppermute | solution.py:457
  104.4 0.0 collective-permute-start.13
  104.4 0.0 collective-permute-done.12.refs_2_
  104.4 1.4 collective-permute-done.13.refs_3_
  105.8 0.7 copy-done.5
  106.5 12.1 %point_back.1 = (f32[8,32,256]{2,1,0:T(8,128)}, f32[8,32,256]{2,1,0:T(8,128)}, f32[32,256]{1,0:T(8,128)}, f32[3,32,32]{2,1,0:T(8,128)}) custom-call(f32[8]{0:T(128)} %sharpness.3, f32[152,256]{1,0:T(8,128)} %mix_back.1.refs_0_, f32[152,256]{1,0:T(8,128)} %copy-done.3, f32[152,256]{1,0:T(8,128)} %copy-done.4, f32[152,256]{1,0:T(8,128)} %copy-done.5, ...), custom_call_target="tpu_custom_call" | custom-call | tf_op jit(solution)/shard_map/point_back/pallas_call | solution.py:413
  118.6 1.0 pad_maximum_fusion
  119.6 0.2 collective-permute-start.14
  119.8 1.4 collective-permute-done.14
  121.2 0.8 slice_add_fusion.11
  122.0 1.0 slice_add_fusion.3
  123.1 0.7 collective-permute-start.15
  123.8 5.6 %collective-permute-done.15 = f32[160,256]{1,0:T(8,128)S(1)} collective-permute-done((f32[160,256]{1,0:T(8,128)S(1)}, f32[160,256]{1,0:T(8,128)S(1)}, u32[]{:S(2)}, u32[]{:S(2)}) %collective-permute-start.15) | collective-permute-done | bytes 163872 | tf_op jit(solution)/shard_map/ppermute | solution.py:457
  129.4 0.1 collective-permute-start.16
  129.5 0.0 reduce-scatter.3.cloned.1.call-done
  129.5 0.0 reduce-scatter.5.cloned.1.call-update
  129.6 4.5 %collective-permute-done.16 = f32[96,256]{1,0:T(8,128)S(1)} collective-permute-done((f32[96,256]{1,0:T(8,128)S(1)}, f32[96,256]{1,0:T(8,128)S(1)}, u32[]{:S(2)}, u32[]{:S(2)}) %collective-permute-start.16) | collective-permute-done | bytes 98336 | tf_op jit(solution)/shard_map/ppermute | solution.py:457
  134.1 1.0 collective-permute-start.17
  135.2 5.3 %collective-permute-done.17 = f32[64,256]{1,0:T(8,128)S(1)} collective-permute-done((f32[64,256]{1,0:T(8,128)S(1)}, f32[64,256]{1,0:T(8,128)S(1)}, u32[]{:S(2)}, u32[]{:S(2)}) %collective-permute-start.17) | collective-permute-done | bytes 65568 | tf_op jit(solution)/shard_map/ppermute | solution.py:457
  140.5 0.6 slice_bitcast_fusion.9
  141.1 0.6 slice_add_fusion.8
  141.7 10.5 %reduce-scatter.5.cloned.1.call-done = f32[1,144,256]{2,1,0:T(8,128)} async-done(((f32[4,144,256]{2,1,0:T(8,128)}), f32[1,144,256]{2,1,0:T(8,128)}) %reduce-scatter.5.cloned.1.call-update) | async-done | bytes 147472 | tf_op jit(solution)/shard_map/reduce_scatter | solution.py:578
  152.2 1.4 slice_bitcast_fusion.7
  153.6 0.6 pad_maximum_fusion.4
  154.3 1.5 slice_bitcast_fusion
  (27 shorter events, 0.2 us)
Async XLA Ops:
  7.2 122.4 %reduce-scatter.3.cloned.1.call-start = ((), (), s32[]{:S(2)}) async-start(), calls=%async_computation.2 | async-start | bytes 2949120 | tf_op jit(solution)/shard_map/reduce_scatter | solution.py:575
  22.5 1.8 %collective-permute-start = (f32[2,136,256]{2,1,0:T(8,128)}, f32[2,136,256]{2,1,0:T(8,128)S(1)}, u32[]{:S(2)}, u32[]{:S(2)}) collective-permute-start(f32[2,136,256]{2,1,0:T(8,128)} %get-tuple-element.30), channel_id=1, source_target_pairs={{0,1},{1,0},{2,3},{3,2},{4,5},{5,4},{6,7},{7,6},{8,9},{9,8},{10,11... | collective-permute-start | bytes 835592 | tf_op jit(solution)/shard_map/ppermute | solution.py:457
  25.3 6.9 %collective-permute-start.1 = (f32[1,136,256]{2,1,0:T(8,128)S(1)}, f32[1,136,256]{2,1,0:T(8,128)S(1)}, u32[]{:S(2)}, u32[]{:S(2)}) collective-permute-start(f32[1,136,256]{2,1,0:T(8,128)S(1)} %slice_add_fusion), channel_id=1, source_target_pairs={{0,2},{1,3},{2,0},{3,1},{4,6},{5,7},{6,4},{7,5},{8,10},{9,11},{10,... | collective-permute-start | bytes 417800 | tf_op jit(solution)/shard_map/ppermute | solution.py:457
  33.1 5.3 %collective-permute-start.2 = (f32[136,256]{1,0:T(8,128)S(1)}, f32[136,256]{1,0:T(8,128)S(1)}, u32[]{:S(2)}, u32[]{:S(2)}) collective-permute-start(f32[136,256]{1,0:T(8,128)S(1)} %fusion.1), channel_id=1, source_target_pairs={{0,4},{1,5},{2,6},{3,7},{4,0},{5,1},{6,2},{7,3},{8,12},{9,13},{10,... | collective-permute-start | bytes 417800 | tf_op jit(solution)/shard_map/ppermute | solution.py:457
  38.4 8.3 %collective-permute-start.3 = (f32[136,256]{1,0:T(8,128)S(1)}, f32[136,256]{1,0:T(8,128)S(1)}, u32[]{:S(2)}, u32[]{:S(2)}) collective-permute-start(f32[136,256]{1,0:T(8,128)S(1)} %add.70), channel_id=1, source_target_pairs={{0,8},{1,9},{2,10},{3,11},{4,12},{5,13},{6,14},{7,15},{8,0},{9,1},... | collective-permute-start | bytes 417800 | tf_op jit(solution)/shard_map/ppermute | solution.py:457
  52.5 4.5 %collective-permute-start.4 = (f32[64,256]{1,0:T(8,128)}, f32[64,256]{1,0:T(8,128)S(1)}, u32[]{:S(2)}, u32[]{:S(2)}) collective-permute-start(f32[64,256]{1,0:T(8,128)} %get-tuple-element.31.refs_0_.refs_4_), channel_id=1, source_target_pairs={{0,2},{1,3},{2,0},{3,1},{4,6},{5,7},{6,4},{7,5},{8,10},{9,11},{10,... | collective-permute-start | bytes 196616 | tf_op jit(solution)/shard_map/ppermute | solution.py:457
  53.6 6.7 %collective-permute-start.5 = (f32[64,256]{1,0:T(8,128)}, f32[64,256]{1,0:T(8,128)S(1)}, u32[]{:S(2)}, u32[]{:S(2)}) collective-permute-start(f32[64,256]{1,0:T(8,128)} %get-tuple-element.31.refs_0_.refs_4_), channel_id=1, source_target_pairs={{0,1},{1,0},{2,3},{3,2},{4,5},{5,4},{6,7},{7,6},{8,9},{9,8},{10,11... | collective-permute-start | bytes 196616 | tf_op jit(solution)/shard_map/ppermute | solution.py:457
  57.0 3.3 %copy-start = (f32[64,256]{1,0:T(8,128)}, f32[64,256]{1,0:T(8,128)S(1)}, u32[]{:S(2)}) copy-start(f32[64,256]{1,0:T(8,128)S(1)} %collective-permute-done.4.refs_1_.refs_5_) | copy-start | bytes 196612
  57.0 3.3 %collective-permute-start.6 = (f32[64,256]{1,0:T(8,128)S(1)}, f32[64,256]{1,0:T(8,128)S(1)}, u32[]{:S(2)}, u32[]{:S(2)}) collective-permute-start(f32[64,256]{1,0:T(8,128)S(1)} %collective-permute-done.4.refs_1_.refs_5_), channel_id=1, source_target_pairs={{0,1},{1,0},{2,3},{3,2},{4,5},{5,4},{6,7},{7,6},{8,9},{9,8},{10,11... | collective-permute-start | bytes 196616 | tf_op jit(solution)/shard_map/ppermute | solution.py:457
  60.3 0.6 copy-start.1
  60.9 0.6 copy-start.2
  67.1 3.7 %copy-start.7 = (f32[2,64,256]{2,1,0:T(8,128)S(1)}, f32[2,64,256]{2,1,0:T(8,128)}, u32[]{:S(2)}) copy-start(f32[2,64,256]{2,1,0:T(8,128)} %get-tuple-element.36) | copy-start | bytes 393220
  67.2 5.2 %copy-start.6 = (f32[2,64,256]{2,1,0:T(8,128)S(1)}, f32[2,64,256]{2,1,0:T(8,128)}, u32[]{:S(2)}) copy-start(f32[2,64,256]{2,1,0:T(8,128)} %get-tuple-element.35) | copy-start | bytes 393220
  70.6 81.6 %reduce-scatter.5.cloned.1.call-start = ((), (), s32[]{:S(2)}) async-start(), calls=%async_computation.3 | async-start | bytes 737280 | tf_op jit(solution)/shard_map/reduce_scatter | solution.py:578
  70.8 1.5 collective-permute-start.7
  72.4 4.4 %collective-permute-start.8 = (f32[1,64,256]{2,1,0:T(8,128)S(1)}, f32[1,64,256]{2,1,0:T(8,128)S(1)}, u32[]{:S(2)}, u32[]{:S(2)}) collective-permute-start(f32[1,64,256]{2,1,0:T(8,128)S(1)} %slice_add_fusion.6), channel_id=1, source_target_pairs={{0,2},{1,3},{2,0},{3,1},{4,6},{5,7},{6,4},{7,5},{8,10},{9,11},{10,... | collective-permute-start | bytes 196616 | tf_op jit(solution)/shard_map/ppermute | solution.py:457
  76.8 4.3 %collective-permute-start.9 = (f32[64,256]{1,0:T(8,128)S(1)}, f32[64,256]{1,0:T(8,128)S(1)}, u32[]{:S(2)}, u32[]{:S(2)}) collective-permute-start(f32[64,256]{1,0:T(8,128)S(1)} %fusion.3), channel_id=1, source_target_pairs={{0,4},{1,5},{2,6},{3,7},{4,0},{5,1},{6,2},{7,3},{8,12},{9,13},{10,... | collective-permute-start | bytes 196616 | tf_op jit(solution)/shard_map/ppermute | solution.py:457
  81.2 5.9 %collective-permute-start.10 = (f32[64,256]{1,0:T(8,128)S(1)}, f32[64,256]{1,0:T(8,128)S(1)}, u32[]{:S(2)}, u32[]{:S(2)}) collective-permute-start(f32[64,256]{1,0:T(8,128)S(1)} %add.75), channel_id=1, source_target_pairs={{0,8},{1,9},{2,10},{3,11},{4,12},{5,13},{6,14},{7,15},{8,0},{9,1},... | collective-permute-start | bytes 196616 | tf_op jit(solution)/shard_map/ppermute | solution.py:457
  95.3 9.1 %collective-permute-start.11 = (f32[152,256]{1,0:T(8,128)}, f32[152,256]{1,0:T(8,128)S(1)}, u32[]{:S(2)}, u32[]{:S(2)}) collective-permute-start(f32[152,256]{1,0:T(8,128)} %mix_back.1.refs_0_), channel_id=1, source_target_pairs={{0,2},{1,3},{2,0},{3,1},{4,6},{5,7},{6,4},{7,5},{8,10},{9,11},{10,... | collective-permute-start | bytes 466952 | tf_op jit(solution)/shard_map/ppermute | solution.py:457
  96.2 8.3 %collective-permute-start.12 = (f32[152,256]{1,0:T(8,128)}, f32[152,256]{1,0:T(8,128)S(1)}, u32[]{:S(2)}, u32[]{:S(2)}) collective-permute-start(f32[152,256]{1,0:T(8,128)} %mix_back.1.refs_0_), channel_id=1, source_target_pairs={{0,1},{1,0},{2,3},{3,2},{4,5},{5,4},{6,7},{7,6},{8,9},{9,8},{10,11... | collective-permute-start | bytes 466952 | tf_op jit(solution)/shard_map/ppermute | solution.py:457
  104.4 1.4 copy-start.3
  104.4 1.4 collective-permute-start.13
  104.4 1.4 copy-start.4
  105.8 0.7 copy-start.5
  119.6 1.6 %collective-permute-start.14 = (f32[288,256]{1,0:T(8,128)S(1)}, f32[288,256]{1,0:T(8,128)S(1)}, u32[]{:S(2)}, u32[]{:S(2)}) collective-permute-start(f32[288,256]{1,0:T(8,128)S(1)} %pad_maximum_fusion), channel_id=1, source_target_pairs={{0,1},{1,0},{2,3},{3,2},{4,5},{5,4},{6,7},{7,6},{8,9},{9,8},{10,11... | collective-permute-start | bytes 884744 | tf_op jit(solution)/shard_map/ppermute | solution.py:457
  123.1 6.3 %collective-permute-start.15 = (f32[160,256]{1,0:T(8,128)S(1)}, f32[160,256]{1,0:T(8,128)S(1)}, u32[]{:S(2)}, u32[]{:S(2)}) collective-permute-start(f32[160,256]{1,0:T(8,128)S(1)} %pad_maximum_fusion.1), channel_id=1, source_target_pairs={{0,2},{1,3},{2,0},{3,1},{4,6},{5,7},{6,4},{7,5},{8,10},{9,11},{10,... | collective-permute-start | bytes 491528 | tf_op jit(solution)/shard_map/ppermute | solution.py:457
  129.4 4.7 %collective-permute-start.16 = (f32[96,256]{1,0:T(8,128)S(1)}, f32[96,256]{1,0:T(8,128)S(1)}, u32[]{:S(2)}, u32[]{:S(2)}) collective-permute-start(f32[96,256]{1,0:T(8,128)S(1)} %pad_maximum_fusion.2), channel_id=1, source_target_pairs={{0,4},{1,5},{2,6},{3,7},{4,0},{5,1},{6,2},{7,3},{8,12},{9,13},{10,... | collective-permute-start | bytes 294920 | tf_op jit(solution)/shard_map/ppermute | solution.py:457
  134.1 6.3 %collective-permute-start.17 = (f32[64,256]{1,0:T(8,128)S(1)}, f32[64,256]{1,0:T(8,128)S(1)}, u32[]{:S(2)}, u32[]{:S(2)}) collective-permute-start(f32[64,256]{1,0:T(8,128)S(1)} %pad_maximum_fusion.3), channel_id=1, source_target_pairs={{0,8},{1,9},{2,10},{3,11},{4,12},{5,13},{6,14},{7,15},{8,0},{9,1},... | collective-permute-start | bytes 196616 | tf_op jit(solution)/shard_map/ppermute | solution.py:457
Sparse Core Ops, SparseCore 0:
  70.7 37.1 reduce-scatter.2
  129.7 22.4 reduce-scatter.4

commit v2 on v1

v2 whole, which is shorter than its diff:
```python
import functools
import math

import jax
import jax.numpy as jnp
from jax import lax
from jax.experimental import pallas as pl
from jax.experimental.pallas import tpu as pltpu
from jax.sharding import PartitionSpec as P

F32 = jnp.float32
BF16 = jnp.bfloat16
EPS = 1e-05
GROUP_BITS = 2
GELU_A = math.sqrt(2.0 / math.pi)
GELU_B = 0.044715

NN = ((1,), (0,))
NT = ((1,), (1,))
TN = ((0,), (0,))


def dot(left, right, dims=NN, precision=None):
    return lax.dot_general(
        left, right, (dims, ((), ())), precision=precision, preferred_element_type=F32
    )


def bit_reverse(value, bits):
    out = 0
    for k in range(bits):
        out = (out << 1) | ((value >> k) & 1)
    return out


def norm_parts(inputs):
    centre = jnp.mean(inputs, axis=-1, keepdims=True)
    shifted = inputs - centre
    spread = jnp.mean(shifted * shifted, axis=-1, keepdims=True)
    return shifted, lax.rsqrt(spread + EPS)


def pad_to(count, unit):
    return -(-count // unit) * unit


def split(value):
    high = value.astype(BF16)
    return high, (value - high.astype(F32)).astype(BF16)


def narrow_dot(left, right):
    left_high, left_low = split(left)
    right_high, right_low = split(right)
    return dot(
        jnp.concatenate([left_high, left_high, left_low], axis=0),
        jnp.concatenate([right_high, right_low, right_high], axis=0),
        TN,
    )


def wide_dot(left, right_parts, dims):
    rows = left.shape[0]
    high, low = split(left)
    right_high, right_low = right_parts
    both = dot(jnp.concatenate([high, low], axis=0), right_high, dims)
    return both[:rows] + both[rows:] + dot(high, right_low, dims)


def place_groups(value_of, keep, send, mine):
    half = keep.shape[0]
    bits = (2 * half).bit_length() - 1
    for pos in range(2 * half):
        target = keep if pos < half else send
        target[pos % half] = value_of(bit_reverse(pos, bits) ^ mine)


def sums_kernel(
    counts_hbm,
    sharpness_hbm,
    points_hbm,
    geometry_hbm,
    gain_hbm,
    w_feat_hbm,
    w_mid_hbm,
    w_slice_hbm,
    keep,
    send,
    normed_out,
    features_out,
    middle_out,
    weights_out,
    geo_weights_out,
    low_out,
    geo_low_out,
    total,
    spread,
    maps,
    logit_map,
    logits,
    counts,
    sharpness,
    points,
    geometry,
    gain,
    w_feat,
    w_mid,
    w_slice,
    sems,
):
    copies = [
        pltpu.make_async_copy(source, target, sems.at[i])
        for i, (source, target) in enumerate(
            (
                (w_slice_hbm, w_slice),
                (w_feat_hbm, w_feat),
                (w_mid_hbm, w_mid),
                (gain_hbm, gain),
                (points_hbm, points),
                (geometry_hbm, geometry),
                (sharpness_hbm, sharpness),
                (counts_hbm, counts),
            )
        )
    ]
    for copy in copies:
        copy.start()
    me = lax.axis_index("pts")
    rows, model = points.shape
    width, slices = w_slice.shape
    heads = model // width
    groups = total.shape[0]
    per = heads // groups
    lanes = spread.shape[2]
    logit_map[...] = jnp.zeros_like(logit_map)
    for copy in copies:
        copy.wait()
    slice_t = w_slice[...].T
    for h in range(heads):
        logit_map[h * slices : (h + 1) * slices, h * width : (h + 1) * width] = slice_t
    maps[:model, :] = w_feat[...].T
    maps[model:, :] = w_mid[...].T
    gain_column = jnp.broadcast_to(gain[...].reshape(1, model), (8, model)).T[:, :1]
    live = lax.broadcasted_iota(jnp.int32, (1, rows), 1) < counts[0]

    def block(inputs, at, out_at, weights_ref, low_ref, geo):
        inputs_t = inputs.T.astype(F32)
        shifted = inputs_t - jnp.mean(inputs_t, axis=0, keepdims=True)
        scale = lax.rsqrt(jnp.mean(shifted * shifted, axis=0, keepdims=True) + EPS)
        normed = (shifted * scale * gain_column).astype(BF16)
        both = dot(maps[...], normed).astype(BF16)
        normed_out[:, at] = normed
        features_out[:, at] = both[:model]
        middle_out[:, at] = both[model:]
        logits[...] = dot(logit_map[...], both[model:])
        for h in range(heads):
            cols = slice(h * slices, (h + 1) * slices)
            factor = sharpness[h] * math.log2(math.e)
            for start in range(0, rows, lanes):
                part = logits[cols, start : start + lanes]
                powers = jnp.exp2((part - jnp.max(part, axis=0, keepdims=True)) * factor)
                inverse = 1.0 / jnp.sum(powers, axis=0, keepdims=True)
                if not geo:
                    inverse = jnp.where(live[:, start : start + lanes], inverse, 0.0)
                weights = powers * inverse
                where = pl.ds(out_at + start, lanes)
                weights_ref[cols, where] = weights
                low_ref[cols, where] = weights.astype(BF16)
                if start == 0 and not geo:
                    spread[0, cols, :] = weights
                else:
                    spread[int(geo), cols, :] += weights

    spread[1] = jnp.zeros_like(spread[1])
    block(points[...], pl.ds(0, rows), 0, weights_out, low_out, False)

    @pl.loop(0, geometry.shape[0] // rows)
    def _(i):
        start = pl.multiple_of(i * rows, rows)
        block(
            geometry[pl.ds(start, rows), :],
            pl.ds(pl.multiple_of(start + rows, rows), rows),
            start,
            geo_weights_out,
            geo_low_out,
            True,
        )

    ones = jnp.ones((16, lanes), BF16)
    for geo, (low_ref, at) in enumerate(
        ((low_out, slice(0, rows)), (geo_low_out, slice(rows, rows + geometry.shape[0])))
    ):
        high = spread[geo].astype(BF16)
        rest = spread[geo] - high.astype(F32)
        middle = rest.astype(BF16)
        low = (rest - middle.astype(F32)).astype(BF16)
        sums = dot(ones, high, NT) + dot(ones, middle, NT) + dot(ones, low, NT)
        for h in range(heads):
            g, j = h // per, h % per
            row = 2 * per * width + geo * per + j
            total[g, row : row + 1, :] = sums[:1, h * slices : (h + 1) * slices]
            row = (geo * per + j) * width
            total[g, row : row + width, :] = dot(
                features_out[h * width : (h + 1) * width, at],
                low_ref[h * slices : (h + 1) * slices, :],
                NT,
            )
    filled = 2 * per * (width + 1)
    total[:, filled:, :] = jnp.zeros((groups, total.shape[1] - filled, slices), F32)
    place_groups(lambda g: total[g], keep, send, me & (groups - 1))


tie = lax.optimization_barrier


def token_rows(tokens, j, per, width):
    base = 2 * per * width
    out = []
    for geo in range(2):
        row = (geo * per + j) * width
        den = tokens[base + geo * per + j : base + geo * per + j + 1, :] + EPS
        out.append((tokens[row : row + width, :] / den, den))
    return out


def mix_kernel(tokens, w_query, w_key, w_value, mixed_out, attention_out, kept):
    width = w_query.shape[0]
    per = attention_out.shape[0]
    slices = tokens.shape[1]
    for j in range(per):
        (field, _), (geo, _) = token_rows(tokens, j, per, width)
        both = jnp.concatenate([field, geo], axis=1)
        query = narrow_dot(w_query[...], field)
        keys = narrow_dot(w_key[...], both)
        values = narrow_dot(w_value[...], both)
        kept[j, :width, :slices] = query
        kept[j, width : 2 * width, :] = keys
        kept[j, 2 * width :, :] = values
        scores = narrow_dot(keys, query)
        scores = (scores - jnp.max(scores, axis=0, keepdims=True)) * (
            math.log2(math.e) / math.sqrt(width)
        )
        powers = jnp.exp2(scores)
        attention = powers * (1.0 / jnp.sum(powers, axis=0, keepdims=True))
        attention_out[j] = attention
        mixed_out[j * width : (j + 1) * width, :] = wide_dot(values, split(attention), NN)


def mix_back_kernel(tokens, attention_in, kept, grad, w_query, w_key, w_value, out):
    width = w_query.shape[0]
    per, both_count, slices = attention_in.shape
    base = 2 * per * width
    small = jnp.zeros((width, 3 * width), F32)
    out[base : base + pad_to(2 * per, 8), :] = jnp.zeros((pad_to(2 * per, 8), slices), F32)
    w_query_t, w_key_t, w_value_t = w_query[...].T, w_key[...].T, w_value[...].T
    for j in range(per):
        (field, field_den), (geo, geo_den) = token_rows(tokens, j, per, width)
        both = jnp.concatenate([field, geo], axis=1)
        query = kept[j, :width, :slices]
        keys = kept[j, width : 2 * width, :]
        values = kept[j, 2 * width :, :]
        attention = attention_in[j]
        mixed_grad = grad[j * width : (j + 1) * width, :]
        att_grad = narrow_dot(values, mixed_grad)
        inner = jnp.sum(attention * att_grad, axis=0, keepdims=True)
        score_grad = split(attention * (att_grad - inner) * (1.0 / math.sqrt(width)))
        value_grad = wide_dot(mixed_grad, split(attention), NT)
        query_grad = wide_dot(keys, score_grad, NN)
        key_grad = wide_dot(query, score_grad, NT)
        both_grad = narrow_dot(w_key_t, key_grad) + narrow_dot(w_value_t, value_grad)
        field_grad = both_grad[:, :slices] + narrow_dot(w_query_t, query_grad)
        geo_grad = both_grad[:, slices:]
        small += jnp.concatenate(
            [
                wide_dot(field, split(query_grad), NT),
                wide_dot(both, split(key_grad), NT),
                wide_dot(both, split(value_grad), NT),
            ],
            axis=1,
        )
        for g, (value, den, value_of) in enumerate(
            ((field_grad, field_den, field), (geo_grad, geo_den, geo))
        ):
            row = (g * per + j) * width
            scaled = value / den
            out[row : row + width, :] = scaled
            out[base + g * per + j : base + g * per + j + 1, :] = -jnp.sum(
                scaled * value_of, axis=0, keepdims=True
            )
    half = width // 2
    filler = jnp.zeros((width, slices // 2 - 3 * width), F32)
    wide = jnp.concatenate([small, filler], axis=1)
    out[out.shape[0] - half :, :] = jnp.concatenate([wide[:half], wide[half:]], axis=1)


def mlp_kernel(
    rel,
    *refs,
):
    groups = len(rel)
    pieces = refs[:groups]
    (
        low,
        points,
        cotangent,
        w_out,
        gain,
        w_up,
        w_down,
        layer_out,
        grad_att_out,
        keep,
        send,
        attended,
        second_out,
        hidden_out,
        grad_upper_out,
        grad_resid_out,
        canon,
    ) = refs[groups:]
    me = lax.axis_index("pts")
    model = points.shape[1]
    slices = canon.shape[2]
    heads = low.shape[0] // slices
    width = model // heads
    per = heads // groups
    mine = me & (groups - 1)
    for r, piece in zip(rel, pieces):
        canon[mine ^ r] = piece[...]
    for h in range(heads):
        cols = slice(h * slices, (h + 1) * slices)
        j = h % per
        attended[h * width : (h + 1) * width, :] = dot(
            canon[h // per, j * width : (j + 1) * width, :].astype(BF16), low[cols, :]
        ).astype(BF16)
    gain_row = gain[...].reshape(1, model)
    residual = points[...].astype(F32) + dot(attended[...], w_out[...], TN)
    shifted, scale = norm_parts(residual)
    unit = shifted * scale
    second = (unit * gain_row).astype(BF16)
    second_out[...] = second
    upper = dot(second, w_up[...])
    square = upper * upper
    slope = jnp.tanh(GELU_A * upper * (1.0 + GELU_B * square))
    half = 0.5 * (1.0 + slope)
    hidden = (upper * half).astype(BF16)
    hidden_out[...] = hidden
    curve = half + 0.5 * upper * (1.0 - slope * slope) * (
        GELU_A * (1.0 + 3.0 * GELU_B * square)
    )
    layer_out[...] = (residual + dot(hidden, w_down[...])).astype(BF16)
    grad_upper = (dot(cotangent[...], w_down[...], NT) * curve).astype(BF16)
    grad_upper_out[...] = grad_upper
    grad_unit = dot(grad_upper, w_up[...], NT) * gain_row
    grad_norm = scale * (
        grad_unit
        - jnp.mean(grad_unit, axis=-1, keepdims=True)
        - unit * jnp.mean(grad_unit * unit, axis=-1, keepdims=True)
    )
    grad_resid = (cotangent[...].astype(F32) + grad_norm).astype(BF16)
    grad_resid_out[...] = grad_resid
    grad_att = dot(w_out[...], grad_resid, NT).astype(BF16)
    grad_att_out[...] = grad_att
    for h in range(heads):
        j = h % per
        canon[h // per, j * width : (j + 1) * width, :] = dot(
            grad_att[h * width : (h + 1) * width], low[h * slices : (h + 1) * slices, :], NT
        )
    place_groups(lambda g: canon[g], keep, send, mine)


def outer_kernel(
    attended, second, hidden, grad_upper, grad_resid, cotangent, keep, send, out, up, down
):
    me = lax.axis_index("pts")
    half, rows, model = keep.shape
    parts = 2 * half
    bits = parts.bit_length() - 1
    step = model // parts
    wide = hidden.shape[1] // model
    out[...] = dot(attended[...], grad_resid[...])
    up[...] = dot(second[...], grad_upper[...], TN)
    down[...] = dot(hidden[...], cotangent[...], TN)
    for pos in range(parts):
        target = keep if pos < half else send
        p = bit_reverse(pos, bits) ^ me
        i = pos % half
        at = pl.ds(pl.multiple_of(p * step, step), step)
        target[i, :step, :] = out[at, :]
        for w in range(wide):
            target[i, step * (1 + w) : step * (2 + w), :] = up[at, w * model : (w + 1) * model]
        tall = step * wide
        target[i, step * (1 + wide) :, :] = down[pl.ds(pl.multiple_of(p * tall, tall), tall), :]


def back_kernel(rel, sharpness, *refs):
    groups = len(rel)
    pieces = refs[:groups]
    mixed = refs[groups : 2 * groups]
    (
        weights,
        geo_weights,
        low,
        geo_low,
        features,
        middle,
        normed,
        grad_att,
        w_slice,
        keep,
        send,
        grad_mix,
        canon,
        mix_canon,
        left_field,
        left_geo,
        low_numer,
        right,
        total,
        slice_sum,
        products,
        logit,
    ) = refs[2 * groups :]
    me = lax.axis_index("pts")
    model, rows = grad_att.shape
    width, slices = w_slice.shape
    heads = model // width
    per = heads // groups
    mine = me & (groups - 1)
    base = 2 * per * width
    for r, piece, mix_piece in zip(rel, pieces, mixed):
        canon[mine ^ r] = piece[...]
        mix_canon[mine ^ r] = mix_piece[...]
    for h in range(heads):
        g, j = h // per, h % per
        for geo in range(2):
            row = (geo * per + j) * width
            numer = canon[g, row : row + width, :].astype(BF16)
            low_numer[geo, h * width : (h + 1) * width, :] = numer
            den = canon[g, base + geo * per + j : base + geo * per + j + 1, :]
            high = den.astype(BF16).astype(F32)
            middle_part = (den - high).astype(BF16).astype(F32)
            rest = den - high - middle_part
            den_rows = jnp.concatenate([high, middle_part, rest, jnp.zeros((13, slices), F32)], axis=0)
            parts = [numer.astype(F32)]
            if not geo:
                parts.append(mix_canon[g, j * width : (j + 1) * width, :])
            parts.append(den_rows)
            left = jnp.concatenate(parts, axis=0).astype(BF16).T
            if geo:
                left_geo[h] = left
            else:
                left_field[h] = left
    slice_sum[...] = jnp.zeros_like(slice_sum)
    ones = jnp.ones((16, rows), BF16)

    def block(at, own_at, weights_ref, low_ref, geo):
        left_ref = left_geo if geo else left_field
        for h in range(heads):
            own = slice(h * width, (h + 1) * width)
            stack = [features[own, at]]
            if not geo:
                stack.append(grad_att[own, :])
            products[h * slices : (h + 1) * slices, :] = dot(
                left_ref[h], jnp.concatenate(stack + [ones], axis=0)
            )
        for h in range(heads):
            cols = slice(h * slices, (h + 1) * slices)
            for start in range(0, rows, lanes):
                grad_weights = products[cols, start : start + lanes]
                share = weights_ref[cols, pl.ds(own_at + start, lanes)]
                inner = jnp.sum(share * grad_weights, axis=0, keepdims=True)
                logit[cols, start : start + lanes] = (
                    share * (grad_weights - inner) * sharpness[h]
                ).astype(BF16)
        for h in range(heads):
            cols = slice(h * slices, (h + 1) * slices)
            own = slice(h * width, (h + 1) * width)
            right[own, at] = dot(
                low_numer[int(geo), own, :], low_ref[cols, pl.ds(own_at, rows)]
            ).astype(BF16)
            right[model + h * width : model + (h + 1) * width, at] = dot(
                w_slice[...], logit[cols, :]
            ).astype(BF16)
            slice_sum[...] += dot(middle[own, at], logit[cols, :], NT)

    lanes = math.gcd(rows, 128)
    block(pl.ds(0, rows), 0, weights, low, False)

    @pl.loop(0, normed.shape[1] // rows - 1)
    def _(i):
        start = pl.multiple_of(i * rows, rows)
        block(pl.ds(pl.multiple_of(start + rows, rows), rows), start, geo_weights, geo_low, True)

    total[...] = dot(normed[...], right[...], NT)
    half = keep.shape[0] // 2
    step = model // (2 * half)
    bits = (2 * half).bit_length() - 1
    for pos in range(2 * half):
        start = pl.multiple_of((bit_reverse(pos, bits) ^ me) * step, step)
        value = total[pl.ds(start, step), :]
        if pos < half:
            keep[2 * pos] = value[:, :model]
            keep[2 * pos + 1] = value[:, model:]
        else:
            row = (pos - half) * 2 * step
            send[row : row + step, :] = value[:, :model]
            send[row + step : row + 2 * step, :] = value[:, model:]
    send[half * 2 * step :, :] = slice_sum[...]

    small_rows = width // 2
    packed = canon[0, canon.shape[1] - small_rows :, :]
    for g in range(1, groups):
        packed += canon[g, canon.shape[1] - small_rows :, :]
    wide = jnp.concatenate([packed[:, : slices // 2], packed[:, slices // 2 :]], axis=0)
    for i in range(3):
        grad_mix[i] = wide[:, i * width : (i + 1) * width]


VMEM = pl.BlockSpec(memory_space=pltpu.VMEM)
SMEM = pl.BlockSpec(memory_space=pltpu.SMEM)
HBM = pl.BlockSpec(memory_space=pltpu.HBM)
MIB = 1024 * 1024


def shape(dims, dtype=F32):
    return jax.ShapeDtypeStruct(tuple(dims), dtype)


def run(body, name, limit, first, out_shape, scratch, *args):
    rest = HBM if first is HBM else VMEM
    if first is HBM:
        args = args[:1] + tuple(
            pltpu.with_memory_space_constraint(arg, pltpu.HBM) for arg in args[1:]
        )
    return pl.pallas_call(
        body,
        out_shape=out_shape,
        in_specs=[first] + [rest] * (len(args) - 1),
        out_specs=jax.tree.map(lambda _: VMEM, out_shape),
        scratch_shapes=scratch,
        compiler_params=pltpu.CompilerParams(vmem_limit_bytes=limit * MIB),
        name=name,
    )(*args)


def on_device(
    parts,
    points,
    geometry,
    counts,
    cotangent,
    gain_attn,
    w_feat,
    w_mid,
    w_slice,
    sharpness,
    w_query,
    w_key,
    w_value,
    w_out,
    gain_mlp,
    w_up,
    w_down,
):
    rows, model = points.shape
    geo_rows = geometry.shape[0]
    all_rows = rows + geo_rows
    width, slices = w_slice.shape
    heads = sharpness.shape[0]
    hidden_width = w_up.shape[1]
    all_bits = parts.bit_length() - 1
    bits = min(GROUP_BITS, all_bits)
    groups = 1 << bits
    per = heads // groups
    token_height = 2 * per * width + pad_to(2 * per, 8)
    grad_height = token_height + width // 2
    half = groups // 2
    step = model // parts
    wide = hidden_width // model

    def exchange(value, bit):
        return lax.ppermute(value, "pts", [(i, i ^ (1 << bit)) for i in range(parts)])

    def fold(keep, got):
        count = keep.shape[0] // 2
        return keep[:count] + got[:count], keep[count:] + got[count:]

    def add_all(value, first, last):
        for bit in range(first, last):
            value = value + exchange(value, bit)
        return value

    def collect(pieces, first, count):
        for bit in reversed(range(first, first + count)):
            pieces = pieces + [exchange(piece, bit) for piece in pieces]
        return pieces

    rel = [0]
    for bit in reversed(range(bits)):
        rel = rel + [r ^ (1 << bit) for r in rel]

    keep, send, normed, features, middle, weights, geo_weights, low, geo_low = run(
        sums_kernel,
        "slice_sums",
        20,
        HBM,
        (
            shape((half, token_height, slices)),
            shape((half, token_height, slices)),
            shape((model, all_rows), BF16),
            shape((model, all_rows), BF16),
            shape((model, all_rows), BF16),
            shape((heads * slices, rows)),
            shape((heads * slices, geo_rows)),
            shape((heads * slices, rows), BF16),
            shape((heads * slices, geo_rows), BF16),
        ),
        [
            pltpu.VMEM((groups, token_height, slices), F32),
            pltpu.VMEM((2, heads * slices, math.gcd(rows, 128)), F32),
            pltpu.VMEM((2 * model, model), BF16),
            pltpu.VMEM((heads * slices, model), BF16),
            pltpu.VMEM((heads * slices, rows), F32),
            pltpu.SMEM(counts.shape, jnp.int32),
            pltpu.SMEM(sharpness.shape, F32),
            pltpu.VMEM(points.shape, BF16),
            pltpu.VMEM(geometry.shape, BF16),
            pltpu.VMEM(gain_attn.shape, F32),
            pltpu.VMEM(w_feat.shape, BF16),
            pltpu.VMEM(w_mid.shape, BF16),
            pltpu.VMEM(w_slice.shape, BF16),
            pltpu.SemaphoreType.DMA((8,)),
        ],
        counts,
        sharpness,
        points,
        geometry,
        gain_attn,
        w_feat,
        w_mid,
        w_slice,
    )
    got = exchange(send, 0)
    for bit in range(1, bits):
        keep, send = fold(keep, got)
        got = exchange(send, bit)
    tokens = add_all((keep + got)[0], bits, all_bits)
    mixed, attention, kept = run(
        mix_kernel,
        "mix_tokens",
        12,
        VMEM,
        (
            shape((per * width, slices)),
            shape((per, 2 * slices, slices)),
            shape((per, 3 * width, 2 * slices)),
        ),
        [],
        tokens,
        w_query,
        w_key,
        w_value,
    )
    mixed_pieces = collect([mixed], 0, bits)
    (
        layer_out,
        grad_att,
        keep,
        send,
        attended,
        second,
        hidden,
        grad_upper,
        grad_resid,
    ) = run(
        functools.partial(mlp_kernel, tuple(rel)),
        "mlp",
        24,
        VMEM,
        (
            shape((rows, model), BF16),
            shape((model, rows), BF16),
            shape((half, per * width, slices)),
            shape((half, per * width, slices)),
            shape((model, rows), BF16),
            shape((rows, model), BF16),
            shape((rows, hidden_width), BF16),
            shape((rows, hidden_width), BF16),
            shape((rows, model), BF16),
        ),
        [pltpu.VMEM((groups, per * width, slices), F32)],
        *mixed_pieces,
        low,
        points,
        cotangent,
        w_out,
        gain_mlp,
        w_up,
        w_down,
    )
    got = exchange(send, 0)
    attended, second, hidden, grad_upper, grad_resid, got = tie(
        (attended, second, hidden, grad_upper, grad_resid, got)
    )
    outer_keep, outer_send = run(
        outer_kernel,
        "weight_grads",
        16,
        VMEM,
        (shape((parts // 2, step * (1 + 2 * wide), model)),) * 2,
        [
            pltpu.VMEM((model, model), F32),
            pltpu.VMEM((model, hidden_width), F32),
            pltpu.VMEM((hidden_width, model), F32),
        ],
        attended,
        second,
        hidden,
        grad_upper,
        grad_resid,
        cotangent,
    )
    for bit in range(1, bits):
        keep, send = fold(keep, got)
        got = exchange(send, bit)
    outer_got = exchange(outer_send, 0)
    mixed_grad, outer_got = tie(((keep + got)[0], outer_got))
    outer_keep, outer_send = fold(outer_keep, outer_got)
    outer_got = exchange(outer_send, 1)
    mixed_grad = add_all(mixed_grad, bits, all_bits)
    token_grad = run(
        mix_back_kernel,
        "mix_back",
        16,
        VMEM,
        shape((grad_height, slices)),
        [],
        tokens,
        attention,
        kept,
        mixed_grad,
        w_query,
        w_key,
        w_value,
    )
    token_grad, outer_got = tie((token_grad, outer_got))
    outer_keep, outer_send = fold(outer_keep, outer_got)
    outer_got = exchange(outer_send, 2)
    grad_pieces = collect([token_grad], 0, bits)
    grad_pieces, outer_got = tie((grad_pieces, outer_got))
    outer_keep, outer_send = fold(outer_keep, outer_got)
    outer_got = exchange(outer_send, 3)
    keep, send, grad_mix = run(
        functools.partial(back_kernel, tuple(rel)),
        "point_back",
        24,
        SMEM,
        (
            shape((parts, step, model)),
            shape((parts * step + width, model)),
            shape((3, width, width)),
        ),
        [
            pltpu.VMEM((groups, grad_height, slices), F32),
            pltpu.VMEM((groups, per * width, slices), F32),
            pltpu.VMEM((heads, slices, 2 * width + 16), BF16),
            pltpu.VMEM((heads, slices, width + 16), BF16),
            pltpu.VMEM((2, model, slices), BF16),
            pltpu.VMEM((2 * model, all_rows), BF16),
            pltpu.VMEM((model, 2 * model), F32),
            pltpu.VMEM((width, slices), F32),
            pltpu.VMEM((heads * slices, rows), F32),
            pltpu.VMEM((heads * slices, rows), BF16),
        ],
        sharpness,
        *grad_pieces,
        *mixed_pieces,
        weights,
        geo_weights,
        low,
        geo_low,
        features,
        middle,
        normed,
        grad_att,
        w_slice,
    )
    keep = keep.reshape(-1, model)
    slice_sum = send[keep.shape[0] :]
    for bit in range(all_bits):
        if bit < all_bits - 3:
            send, outer_got = tie((send, outer_got))
        if bit < all_bits - 4:
            outer_keep, outer_send = fold(outer_keep, outer_got)
            outer_got = exchange(outer_send, bit + 4)
        got = exchange(send, bit)
        count = keep.shape[0]
        slice_sum = slice_sum + got[count:]
        if bit < all_bits - 1:
            count //= 2
            send = jnp.concatenate([keep[count:] + got[count : 2 * count], slice_sum], axis=0)
            keep = keep[:count] + got[:count]
        else:
            grad_feat = keep[:step] + got[:step]
            grad_mid = keep[step:] + got[step : 2 * step]
    outer = (outer_keep + outer_got)[0]
    grad_out = outer[:step]
    grad_up = jnp.concatenate(
        [outer[step * (1 + w) : step * (2 + w)] for w in range(wide)], axis=1
    )
    grad_down = outer[step * (1 + wide) :]
    return (layer_out, grad_feat, grad_mid, grad_out, grad_up, grad_down, slice_sum, grad_mix)


def solution(mesh):
    split = P(("design", "pts"), None)
    placed = (split, split, P(("design", "pts")), split) + (P(),) * 12
    return jax.shard_map(
        functools.partial(on_device, mesh.shape["pts"]),
        mesh=mesh,
        in_specs=placed,
        out_specs=(split,) * 6 + (P("design", None), P("design", None, None)),
        check_vma=False,
    )
```

time: 163 us -> 100 us (0.61)
  Pallas kernels: 48.6 us -> 21.9 us
  waiting for transfers between devices: 67.6 us -> 51.4 us
  between operations: 14.8 us -> 1.55 us
  local copies, waits for them, and re-layouts: 8.65 us -> 1.31 us
  starting transfers between devices: 15.7 us -> 21.7 us
  other arithmetic: 7.31 us -> 2.42 us
    pallas_call x6, Pallas kernels: 48.6 us -> 21.9 us  [run(): pl.pallas_call(body, out_shape=out_shape, in_specs=[first] + [rest] * (le...]
    reduce_scatter x2 -> x0, waiting for transfers between devices: 10.5 us -> none  [the longest x1 10.5 us: on_device(): lax.psum_scatter(outer, 'pts', scatter_dimension=0, axis_index_groups=far...]
    ppermute x18 -> x22, starting transfers between devices: 15.4 us -> 21.7 us  [exchange(): return lax.ppermute(value, 'pts', [(i, i ^ 1 << bit) for i in range(parts)])]
    ppermute x18 -> x22, waiting for transfers between devices: 57 us -> 51.4 us  [exchange(): return lax.ppermute(value, 'pts', [(i, i ^ 1 << bit) for i in range(parts)])]
    slice x3 -> x1, local copies, waits for them, and re-layouts: 3.27 us -> 0.02 us  [on_device(): keep = keep[:count] + got[:count]]
    unnamed x16 -> x22, local copies, waits for them, and re-layouts: 1.9 us -> 0.05 us
    add x9 -> x13, other arithmetic: 3.37 us -> 1.66 us  [the longest x3 0.63 us: on_device(): slice_sum = slice_sum + got[count:]]
  transfers between devices with their start and end apart: 20 -> 22, of which waited for: 16 -> 17; matrix products, arithmetic and copies ran while one was open for 5% -> 2% of each run, Pallas kernels for 12% -> 8%
where the time goes in v2:
time: 100 us
  waiting for transfers between devices  51.4 us (51%)
  Pallas kernels  21.9 us (22%)
  starting transfers between devices  21.7 us (22%)
  other arithmetic  2.42 us (2%)
  between operations  1.55 us (2%)
  local copies, waits for them, and re-layouts  1.31 us (1%)
    ppermute x22, waiting for transfers between devices, exchange(): return lax.ppermute(value, 'pts', [(i, i ^ 1 << bit) for i in range(parts)])  51.4 us
    pallas_call x6, Pallas kernels, run(): pl.pallas_call(body, out_shape=out_shape, in_specs=[first] + [rest] * (le...  21.9 us
    ppermute x22, starting transfers between devices, exchange(): return lax.ppermute(value, 'pts', [(i, i ^ 1 << bit) for i in range(parts)])  21.7 us
  transfers between devices with their start and end apart: 22, of which 17 were waited for; matrix products, arithmetic and copies ran while one was open for 2% of the time, Pallas kernels for 8%

profile of v2, /device:TPU:0, one launch (start us, length us, event | category | flops | bytes accessed | tf_op | source)
XLA Modules:
  0.0 100.3 jit_solution(8944559375751999635)
XLA Ops:
  1.3 0.0 copy-start.5
  1.3 0.0 copy-start.6
  1.3 0.0 copy-start.7
  1.3 0.0 copy-start
  1.3 0.0 copy-start.1
  1.4 8.5 %slice_sums.1 = (f32[2,136,256]{2,1,0:T(8,128)S(1)}, f32[2,136,256]{2,1,0:T(8,128)S(1)}, bf16[256,768]{1,0:T(8,128)(2,1)S(1)}, bf16[256,768]{1,0:T(8,128)(2,1)S(...) custom-call(s32[1]{0:T(128)S(6)} %copy.24.counts_hbm, ...), custom_call_target="tpu_custom_call" | custom-call | tf_op jit(solution)/shard_map/slice_sums/pallas_call | solution.py:536
  9.9 0.5 collective-permute-start
  10.4 1.2 %collective-permute-done = f32[2,136,256]{2,1,0:T(8,128)S(1)} collective-permute-done((f32[2,136,256]{2,1,0:T(8,128)S(1)}, f32[2,136,256]{2,1,0:T(8,128)S(1)}, u32[]{:S(2)}, u32[]{:S(2)}) %collective-permute-start) | collective-permute-done | bytes 278560 | tf_op jit(solution)/shard_map/ppermute | solution.py:583
  11.6 3.0 %collective-permute-start.1 = (f32[1,136,256]{2,1,0:T(8,128)S(1)}, f32[1,136,256]{2,1,0:T(8,128)S(1)}, u32[]{:S(2)}, u32[]{:S(2)}) collective-permute-start(f32[1,136,256]{2,1,0:T(8,128)S(1)} %slice_add_fusion.6), channel_id=1, source_target_pairs={{0,2},{1,3},{2,0},{3,1},{4,6},{5,7},{6,4},{7,5},{8,10},{9,11},{10,... | collective-permute-start | bytes 417800 | tf_op jit(solution)/shard_map/ppermute | solution.py:583
  14.6 4.0 %collective-permute-done.1 = f32[1,136,256]{2,1,0:T(8,128)S(1)} collective-permute-done((f32[1,136,256]{2,1,0:T(8,128)S(1)}, f32[1,136,256]{2,1,0:T(8,128)S(1)}, u32[]{:S(2)}, u32[]{:S(2)}) %collective-permute-start.1) | collective-permute-done | bytes 139296 | tf_op jit(solution)/shard_map/ppermute | solution.py:583
  18.6 1.9 %collective-permute-start.2 = (f32[136,256]{1,0:T(8,128)S(1)}, f32[136,256]{1,0:T(8,128)S(1)}, u32[]{:S(2)}, u32[]{:S(2)}) collective-permute-start(f32[136,256]{1,0:T(8,128)S(1)} %fusion.2), channel_id=1, source_target_pairs={{0,4},{1,5},{2,6},{3,7},{4,0},{5,1},{6,2},{7,3},{8,12},{9,13},{10,... | collective-permute-start | bytes 417800 | tf_op jit(solution)/shard_map/ppermute | solution.py:583
  20.4 3.4 %collective-permute-done.2 = f32[136,256]{1,0:T(8,128)S(1)} collective-permute-done((f32[136,256]{1,0:T(8,128)S(1)}, f32[136,256]{1,0:T(8,128)S(1)}, u32[]{:S(2)}, u32[]{:S(2)}) %collective-permute-start.2) | collective-permute-done | bytes 139296 | tf_op jit(solution)/shard_map/ppermute | solution.py:583
  23.9 2.7 %collective-permute-start.3 = (f32[136,256]{1,0:T(8,128)S(1)}, f32[136,256]{1,0:T(8,128)S(1)}, u32[]{:S(2)}, u32[]{:S(2)}) collective-permute-start(f32[136,256]{1,0:T(8,128)S(1)} %add.90), channel_id=1, source_target_pairs={{0,8},{1,9},{2,10},{3,11},{4,12},{5,13},{6,14},{7,15},{8,0},{9,1},... | collective-permute-start | bytes 417800 | tf_op jit(solution)/shard_map/ppermute | solution.py:583
  26.6 5.5 %collective-permute-done.3 = f32[136,256]{1,0:T(8,128)S(1)} collective-permute-done((f32[136,256]{1,0:T(8,128)S(1)}, f32[136,256]{1,0:T(8,128)S(1)}, u32[]{:S(2)}, u32[]{:S(2)}) %collective-permute-start.3) | collective-permute-done | bytes 139296 | tf_op jit(solution)/shard_map/ppermute | solution.py:583
  32.2 1.6 %mix_tokens.1 = (f32[64,256]{1,0:T(8,128)S(1)}, f32[2,512,256]{2,1,0:T(8,128)S(1)}, f32[2,96,512]{2,1,0:T(8,128)S(1)}) custom-call(f32[136,256]{1,0:T(8,128)S(1)} %add.91.tokens, f32[32,32]{1,0:T(8,128)S(1)} %copy-done.5, f32[32,32]{1,0:T(8,128)S(1)} %copy-done.6, f32[32,32]{1,0:T(8,128)S(1)} %copy-done.7), custom_call_target="tpu_custom_call" | custom-call | tf_op jit(solution)/shard_map/mix_tokens/pallas_call | solution.py:536
  33.8 1.0 %collective-permute-start.4 = (f32[64,256]{1,0:T(8,128)S(1)}, f32[64,256]{1,0:T(8,128)S(1)}, u32[]{:S(2)}, u32[]{:S(2)}) collective-permute-start(f32[64,256]{1,0:T(8,128)S(1)} %get-tuple-element.53.refs_0_.refs_4_), channel_id=1, source_target_pairs={{0,2},{1,3},{2,0},{3,1},{4,6},{5,7},{6,4},{7,5},{8,10},{9,11},{10,... | collective-permute-start | bytes 196616 | tf_op jit(solution)/shard_map/ppermute | solution.py:583
  34.8 0.0 collective-permute-start.5
  34.8 3.2 %collective-permute-done.4.refs_1_.refs_5_ = f32[64,256]{1,0:T(8,128)S(1)} collective-permute-done((f32[64,256]{1,0:T(8,128)S(1)}, f32[64,256]{1,0:T(8,128)S(1)}, u32[]{:S(2)}, u32[]{:S(2)}) %collective-permute-start.4) | collective-permute-done | bytes 65568 | tf_op jit(solution)/shard_map/ppermute | solution.py:583
  38.1 0.0 collective-permute-start.6
  38.1 0.0 collective-permute-done.5.refs_2_.refs_6_
  38.1 1.2 %collective-permute-done.6.refs_3_.refs_7_ = f32[64,256]{1,0:T(8,128)S(1)} collective-permute-done((f32[64,256]{1,0:T(8,128)S(1)}, f32[64,256]{1,0:T(8,128)S(1)}, u32[]{:S(2)}, u32[]{:S(2)}) %collective-permute-start.6) | collective-permute-done | bytes 65568 | tf_op jit(solution)/shard_map/ppermute | solution.py:583
  39.4 2.8 %mlp.1 = (bf16[256,256]{1,0:T(8,128)(2,1)}, bf16[256,256]{1,0:T(8,128)(2,1)S(1)}, f32[2,64,256]{2,1,0:T(8,128)S(1)}, f32[2,64,256]{2,1,0:T(8,128)S(1)}, bf16[256...) custom-call(f32[64,256]{1,0:T(8,128)S(1)} %get-tuple-element.53.refs, ...), custom_call_target="tpu_custom_call" | custom-call | tf_op jit(solution)/shard_map/mlp/pallas_call | solution.py:536
  42.2 0.2 collective-permute-start.7
  42.4 1.2 %collective-permute-done.7 = f32[2,64,256]{2,1,0:T(8,128)S(1)} collective-permute-done((f32[2,64,256]{2,1,0:T(8,128)S(1)}, f32[2,64,256]{2,1,0:T(8,128)S(1)}, u32[]{:S(2)}, u32[]{:S(2)}) %collective-permute-start.7) | collective-permute-done | bytes 131104 | tf_op jit(solution)/shard_map/ppermute | solution.py:583
  43.6 0.6 weight_grads.1
  44.1 0.2 collective-permute-start.9
  44.4 1.1 %collective-permute-start.8 = (f32[1,64,256]{2,1,0:T(8,128)S(1)}, f32[1,64,256]{2,1,0:T(8,128)S(1)}, u32[]{:S(2)}, u32[]{:S(2)}) collective-permute-start(f32[1,64,256]{2,1,0:T(8,128)S(1)} %slice_add_fusion.12), channel_id=1, source_target_pairs={{0,2},{1,3},{2,0},{3,1},{4,6},{5,7},{6,4},{7,5},{8,10},{9,11},{10,... | collective-permute-start | bytes 196616 | tf_op jit(solution)/shard_map/ppermute | solution.py:583
  45.5 3.3 %collective-permute-done.8 = f32[1,64,256]{2,1,0:T(8,128)S(1)} collective-permute-done((f32[1,64,256]{2,1,0:T(8,128)S(1)}, f32[1,64,256]{2,1,0:T(8,128)S(1)}, u32[]{:S(2)}, u32[]{:S(2)}) %collective-permute-start.8) | collective-permute-done | bytes 65568 | tf_op jit(solution)/shard_map/ppermute | solution.py:583
  48.8 0.0 collective-permute-done.9
  48.8 0.2 slice_add_fusion
  49.0 1.1 %collective-permute-start.12 = (f32[4,144,256]{2,1,0:T(8,128)S(1)}, f32[4,144,256]{2,1,0:T(8,128)S(1)}, u32[]{:S(2)}, u32[]{:S(2)}) collective-permute-start(f32[4,144,256]{2,1,0:T(8,128)S(1)} %get-tuple-element.95), channel_id=1, source_target_pairs={{0,2},{1,3},{2,0},{3,1},{4,6},{5,7},{6,4},{7,5},{8,10},{9,11},{10,... | collective-permute-start | bytes 1769480 | tf_op jit(solution)/shard_map/ppermute | solution.py:583
  50.1 0.7 collective-permute-start.10
  50.7 3.6 %collective-permute-done.10 = f32[64,256]{1,0:T(8,128)S(1)} collective-permute-done((f32[64,256]{1,0:T(8,128)S(1)}, f32[64,256]{1,0:T(8,128)S(1)}, u32[]{:S(2)}, u32[]{:S(2)}) %collective-permute-start.10) | collective-permute-done | bytes 65568 | tf_op jit(solution)/shard_map/ppermute | solution.py:583
  54.3 2.1 %collective-permute-start.11 = (f32[64,256]{1,0:T(8,128)S(1)}, f32[64,256]{1,0:T(8,128)S(1)}, u32[]{:S(2)}, u32[]{:S(2)}) collective-permute-start(f32[64,256]{1,0:T(8,128)S(1)} %add.95), channel_id=1, source_target_pairs={{0,8},{1,9},{2,10},{3,11},{4,12},{5,13},{6,14},{7,15},{8,0},{9,1},... | collective-permute-start | bytes 196616 | tf_op jit(solution)/shard_map/ppermute | solution.py:583
  56.4 3.9 %collective-permute-done.11 = f32[64,256]{1,0:T(8,128)S(1)} collective-permute-done((f32[64,256]{1,0:T(8,128)S(1)}, f32[64,256]{1,0:T(8,128)S(1)}, u32[]{:S(2)}, u32[]{:S(2)}) %collective-permute-start.11) | collective-permute-done | bytes 65568 | tf_op jit(solution)/shard_map/ppermute | solution.py:583
  60.3 2.0 %mix_back.1.refs_0_ = f32[152,256]{1,0:T(8,128)S(1)} custom-call(f32[136,256]{1,0:T(8,128)S(1)} %add.91.tokens, f32[2,512,256]{2,1,0:T(8,128)S(1)} %get-tuple-element.56.attention_in, f32[2,96,512]{2,1,0:T(8,128)S(1)} %get-tuple-element.57.kept, f32[64,256]{1,0:T(8,128)S(1)} %add.96.grad, f32[32,32]{1,0:T(8,128)S(1)} %copy-done.5, f32[32,32]{1,0:T(8,128)S(1)} %copy-done.6, ...), custom_call_target="tpu_custom_call" | custom-call | tf_op jit(solution)/shard_map/mix_back/pallas_call | solution.py:536
  62.2 0.0 copy-start.8
  62.3 0.0 copy-start.9
  62.3 1.5 %collective-permute-done.12 = f32[4,144,256]{2,1,0:T(8,128)S(1)} collective-permute-done((f32[4,144,256]{2,1,0:T(8,128)S(1)}, f32[4,144,256]{2,1,0:T(8,128)S(1)}, u32[]{:S(2)}, u32[]{:S(2)}) %collective-permute-start.12) | collective-permute-done | bytes 589856 | tf_op jit(solution)/shard_map/ppermute | solution.py:583
  63.8 1.0 %collective-permute-start.13 = (f32[152,256]{1,0:T(8,128)S(1)}, f32[152,256]{1,0:T(8,128)S(1)}, u32[]{:S(2)}, u32[]{:S(2)}) collective-permute-start(f32[152,256]{1,0:T(8,128)S(1)} %mix_back.1.refs_0_), channel_id=1, source_target_pairs={{0,2},{1,3},{2,0},{3,1},{4,6},{5,7},{6,4},{7,5},{8,10},{9,11},{10,... | collective-permute-start | bytes 466952 | tf_op jit(solution)/shard_map/ppermute | solution.py:583
  64.8 0.1 slice_add_fusion.2
  65.0 0.7 collective-permute-start.16
  65.7 0.0 collective-permute-start.14
  65.7 3.4 %collective-permute-done.13.refs_1_ = f32[152,256]{1,0:T(8,128)S(1)} collective-permute-done((f32[152,256]{1,0:T(8,128)S(1)}, f32[152,256]{1,0:T(8,128)S(1)}, u32[]{:S(2)}, u32[]{:S(2)}) %collective-permute-start.13) | collective-permute-done | bytes 155680 | tf_op jit(solution)/shard_map/ppermute | solution.py:583
  69.1 0.0 collective-permute-start.15
  69.1 0.0 collective-permute-done.14.refs_2_
  69.1 3.2 %collective-permute-done.16 = f32[2,144,256]{2,1,0:T(8,128)S(1)} collective-permute-done((f32[2,144,256]{2,1,0:T(8,128)S(1)}, f32[2,144,256]{2,1,0:T(8,128)S(1)}, u32[]{:S(2)}, u32[]{:S(2)}) %collective-permute-start.16) | collective-permute-done | bytes 294944 | tf_op jit(solution)/shard_map/ppermute | solution.py:583
  72.3 0.0 collective-permute-done.15.refs_3_
  72.3 2.4 %collective-permute-start.17 = (f32[1,144,256]{2,1,0:T(8,128)S(1)}, f32[1,144,256]{2,1,0:T(8,128)S(1)}, u32[]{:S(2)}, u32[]{:S(2)}) collective-permute-start(f32[1,144,256]{2,1,0:T(8,128)S(1)} %slice_add_fusion.5), channel_id=1, source_target_pairs={{0,8},{1,9},{2,10},{3,11},{4,12},{5,13},{6,14},{7,15},{8,0},{9,1},... | collective-permute-start | bytes 442376 | tf_op jit(solution)/shard_map/ppermute | solution.py:583
  74.7 6.4 %point_back.1 = (f32[16,16,256]{2,1,0:T(8,128)S(1)}, f32[288,256]{1,0:T(8,128)S(1)}, f32[3,32,32]{2,1,0:T(8,128)}) custom-call(f32[8]{0:T(128)S(1)} %copy-done.9, f32[152,256]{1,0:T(8,128)S(1)} %mix_back.1.refs_0_, f32[152,256]{1,0:T(8,128)S(1)} %collective-permute-done.13.refs_1_, f32[152,256]{1,0:T(8,128)S(1)} %collective-permute-done.14.refs_2_, ...), custom_call_target="tpu_custom_call" | custom-call | tf_op jit(solution)/shard_map/point_back/pallas_call | solution.py:536
  81.1 0.0 collective-permute-done.17
  81.1 0.0 collective-permute-start.18
  81.1 1.5 %collective-permute-done.18 = f32[288,256]{1,0:T(8,128)S(1)} collective-permute-done((f32[288,256]{1,0:T(8,128)S(1)}, f32[288,256]{1,0:T(8,128)S(1)}, u32[]{:S(2)}, u32[]{:S(2)}) %collective-permute-start.18) | collective-permute-done | bytes 294944 | tf_op jit(solution)/shard_map/ppermute | solution.py:583
  82.7 0.6 collective-permute-start.19
  83.3 0.6 slice_bitcast_fusion
  83.9 5.1 %collective-permute-done.19 = f32[160,256]{1,0:T(8,128)S(1)} collective-permute-done((f32[160,256]{1,0:T(8,128)S(1)}, f32[160,256]{1,0:T(8,128)S(1)}, u32[]{:S(2)}, u32[]{:S(2)}) %collective-permute-start.19) | collective-permute-done | bytes 163872 | tf_op jit(solution)/shard_map/ppermute | solution.py:583
  89.1 1.8 %collective-permute-start.20 = (f32[96,256]{1,0:T(8,128)S(1)}, f32[96,256]{1,0:T(8,128)S(1)}, u32[]{:S(2)}, u32[]{:S(2)}) collective-permute-start(f32[96,256]{1,0:T(8,128)S(1)} %pad_maximum_fusion.1), channel_id=1, source_target_pairs={{0,4},{1,5},{2,6},{3,7},{4,0},{5,1},{6,2},{7,3},{8,12},{9,13},{10,... | collective-permute-start | bytes 294920 | tf_op jit(solution)/shard_map/ppermute | solution.py:583
  90.9 0.6 slice_bitcast_fusion.4
  91.5 2.3 %collective-permute-done.20 = f32[96,256]{1,0:T(8,128)S(1)} collective-permute-done((f32[96,256]{1,0:T(8,128)S(1)}, f32[96,256]{1,0:T(8,128)S(1)}, u32[]{:S(2)}, u32[]{:S(2)}) %collective-permute-start.20) | collective-permute-done | bytes 98336 | tf_op jit(solution)/shard_map/ppermute | solution.py:583
  93.8 0.7 collective-permute-start.21
  94.5 0.6 pad_maximum_fusion.3
  95.2 3.9 %collective-permute-done.21 = f32[64,256]{1,0:T(8,128)S(1)} collective-permute-done((f32[64,256]{1,0:T(8,128)S(1)}, f32[64,256]{1,0:T(8,128)S(1)}, u32[]{:S(2)}, u32[]{:S(2)}) %collective-permute-start.21) | collective-permute-done | bytes 65568 | tf_op jit(solution)/shard_map/ppermute | solution.py:583
  99.0 0.6 slice_add_fusion.13
  99.6 0.6 slice_add_fusion.19
  (34 shorter events, 0.3 us)
Async XLA Ops:
  1.3 30.9 %copy-start.5 = (f32[32,32]{1,0:T(8,128)S(1)}, f32[32,32]{1,0:T(8,128)}, u32[]{:S(2)}) copy-start(f32[32,32]{1,0:T(8,128)} %w_query.3) | copy-start | bytes 12292
  1.3 30.9 %copy-start.6 = (f32[32,32]{1,0:T(8,128)S(1)}, f32[32,32]{1,0:T(8,128)}, u32[]{:S(2)}) copy-start(f32[32,32]{1,0:T(8,128)} %w_key.3) | copy-start | bytes 12292
  1.3 30.9 %copy-start.7 = (f32[32,32]{1,0:T(8,128)S(1)}, f32[32,32]{1,0:T(8,128)}, u32[]{:S(2)}) copy-start(f32[32,32]{1,0:T(8,128)} %w_value.3) | copy-start | bytes 12292
  1.3 38.0 %copy-start = (bf16[256,1024]{1,0:T(8,128)(2,1)S(1)}, bf16[256,1024]{1,0:T(8,128)(2,1)}, u32[]{:S(2)}) copy-start(bf16[256,1024]{1,0:T(8,128)(2,1)} %refs_9_.1) | copy-start | bytes 1572868
  1.3 38.0 %copy-start.1 = (bf16[1024,256]{1,0:T(8,128)(2,1)S(1)}, bf16[1024,256]{1,0:T(8,128)(2,1)}, u32[]{:S(2)}) copy-start(bf16[1024,256]{1,0:T(8,128)(2,1)} %refs_10_.1) | copy-start | bytes 1572868
  1.3 38.0 %copy-start.2 = (bf16[256,256]{1,0:T(8,128)(2,1)S(1)}, bf16[256,256]{1,0:T(8,128)(2,1)}, u32[]{:S(2)}) copy-start(bf16[256,256]{1,0:T(8,128)(2,1)} %cotangent.1) | copy-start | bytes 393220
  1.3 38.0 %copy-start.3 = (bf16[256,256]{1,0:T(8,128)(2,1)S(1)}, bf16[256,256]{1,0:T(8,128)(2,1)}, u32[]{:S(2)}) copy-start(bf16[256,256]{1,0:T(8,128)(2,1)} %refs_5_.1) | copy-start | bytes 393220
  1.4 38.0 %copy-start.4 = (bf16[256,256]{1,0:T(8,128)(2,1)S(1)}, bf16[256,256]{1,0:T(8,128)(2,1)}, u32[]{:S(2)}) copy-start(bf16[256,256]{1,0:T(8,128)(2,1)} %refs_7_.1) | copy-start | bytes 393220
  1.4 38.0 %copy-start.10 = (f32[256]{0:T(256)S(1)}, f32[256]{0:T(256)}, u32[]{:S(2)}) copy-start(f32[256]{0:T(256)} %refs_8_.1) | copy-start | bytes 3076
  9.9 1.7 %collective-permute-start = (f32[2,136,256]{2,1,0:T(8,128)S(1)}, f32[2,136,256]{2,1,0:T(8,128)S(1)}, u32[]{:S(2)}, u32[]{:S(2)}) collective-permute-start(f32[2,136,256]{2,1,0:T(8,128)S(1)} %get-tuple-element.52), channel_id=1, source_target_pairs={{0,1},{1,0},{2,3},{3,2},{4,5},{5,4},{6,7},{7,6},{8,9},{9,8},{10,11... | collective-permute-start | bytes 835592 | tf_op jit(solution)/shard_map/ppermute | solution.py:583
  11.6 6.9 %collective-permute-start.1 = (f32[1,136,256]{2,1,0:T(8,128)S(1)}, f32[1,136,256]{2,1,0:T(8,128)S(1)}, u32[]{:S(2)}, u32[]{:S(2)}) collective-permute-start(f32[1,136,256]{2,1,0:T(8,128)S(1)} %slice_add_fusion.6), channel_id=1, source_target_pairs={{0,2},{1,3},{2,0},{3,1},{4,6},{5,7},{6,4},{7,5},{8,10},{9,11},{10,... | collective-permute-start | bytes 417800 | tf_op jit(solution)/shard_map/ppermute | solution.py:583
  18.6 5.3 %collective-permute-start.2 = (f32[136,256]{1,0:T(8,128)S(1)}, f32[136,256]{1,0:T(8,128)S(1)}, u32[]{:S(2)}, u32[]{:S(2)}) collective-permute-start(f32[136,256]{1,0:T(8,128)S(1)} %fusion.2), channel_id=1, source_target_pairs={{0,4},{1,5},{2,6},{3,7},{4,0},{5,1},{6,2},{7,3},{8,12},{9,13},{10,... | collective-permute-start | bytes 417800 | tf_op jit(solution)/shard_map/ppermute | solution.py:583
  23.9 8.3 %collective-permute-start.3 = (f32[136,256]{1,0:T(8,128)S(1)}, f32[136,256]{1,0:T(8,128)S(1)}, u32[]{:S(2)}, u32[]{:S(2)}) collective-permute-start(f32[136,256]{1,0:T(8,128)S(1)} %add.90), channel_id=1, source_target_pairs={{0,8},{1,9},{2,10},{3,11},{4,12},{5,13},{6,14},{7,15},{8,0},{9,1},... | collective-permute-start | bytes 417800 | tf_op jit(solution)/shard_map/ppermute | solution.py:583
  33.8 4.3 %collective-permute-start.4 = (f32[64,256]{1,0:T(8,128)S(1)}, f32[64,256]{1,0:T(8,128)S(1)}, u32[]{:S(2)}, u32[]{:S(2)}) collective-permute-start(f32[64,256]{1,0:T(8,128)S(1)} %get-tuple-element.53.refs_0_.refs_4_), channel_id=1, source_target_pairs={{0,2},{1,3},{2,0},{3,1},{4,6},{5,7},{6,4},{7,5},{8,10},{9,11},{10,... | collective-permute-start | bytes 196616 | tf_op jit(solution)/shard_map/ppermute | solution.py:583
  34.8 3.2 %collective-permute-start.5 = (f32[64,256]{1,0:T(8,128)S(1)}, f32[64,256]{1,0:T(8,128)S(1)}, u32[]{:S(2)}, u32[]{:S(2)}) collective-permute-start(f32[64,256]{1,0:T(8,128)S(1)} %get-tuple-element.53.refs_0_.refs_4_), channel_id=1, source_target_pairs={{0,1},{1,0},{2,3},{3,2},{4,5},{5,4},{6,7},{7,6},{8,9},{9,8},{10,11... | collective-permute-start | bytes 196616 | tf_op jit(solution)/shard_map/ppermute | solution.py:583
  38.1 1.3 %collective-permute-start.6 = (f32[64,256]{1,0:T(8,128)S(1)}, f32[64,256]{1,0:T(8,128)S(1)}, u32[]{:S(2)}, u32[]{:S(2)}) collective-permute-start(f32[64,256]{1,0:T(8,128)S(1)} %collective-permute-done.4.refs_1_.refs_5_), channel_id=1, source_target_pairs={{0,1},{1,0},{2,3},{3,2},{4,5},{5,4},{6,7},{7,6},{8,9},{9,8},{10,11... | collective-permute-start | bytes 196616 | tf_op jit(solution)/shard_map/ppermute | solution.py:583
  42.2 1.3 %collective-permute-start.7 = (f32[2,64,256]{2,1,0:T(8,128)S(1)}, f32[2,64,256]{2,1,0:T(8,128)S(1)}, u32[]{:S(2)}, u32[]{:S(2)}) collective-permute-start(f32[2,64,256]{2,1,0:T(8,128)S(1)} %get-tuple-element.64), channel_id=1, source_target_pairs={{0,1},{1,0},{2,3},{3,2},{4,5},{5,4},{6,7},{7,6},{8,9},{9,8},{10,11... | collective-permute-start | bytes 393224 | tf_op jit(solution)/shard_map/ppermute | solution.py:583
  44.1 4.7 %collective-permute-start.9 = (f32[8,144,256]{2,1,0:T(8,128)S(1)}, f32[8,144,256]{2,1,0:T(8,128)S(1)}, u32[]{:S(2)}, u32[]{:S(2)}) collective-permute-start(f32[8,144,256]{2,1,0:T(8,128)S(1)} %get-tuple-element.71), channel_id=1, source_target_pairs={{0,1},{1,0},{2,3},{3,2},{4,5},{5,4},{6,7},{7,6},{8,9},{9,8},{10,11... | collective-permute-start | bytes 3538952 | tf_op jit(solution)/shard_map/ppermute | solution.py:583
  44.4 4.4 %collective-permute-start.8 = (f32[1,64,256]{2,1,0:T(8,128)S(1)}, f32[1,64,256]{2,1,0:T(8,128)S(1)}, u32[]{:S(2)}, u32[]{:S(2)}) collective-permute-start(f32[1,64,256]{2,1,0:T(8,128)S(1)} %slice_add_fusion.12), channel_id=1, source_target_pairs={{0,2},{1,3},{2,0},{3,1},{4,6},{5,7},{6,4},{7,5},{8,10},{9,11},{10,... | collective-permute-start | bytes 196616 | tf_op jit(solution)/shard_map/ppermute | solution.py:583
  49.0 14.8 %collective-permute-start.12 = (f32[4,144,256]{2,1,0:T(8,128)S(1)}, f32[4,144,256]{2,1,0:T(8,128)S(1)}, u32[]{:S(2)}, u32[]{:S(2)}) collective-permute-start(f32[4,144,256]{2,1,0:T(8,128)S(1)} %get-tuple-element.95), channel_id=1, source_target_pairs={{0,2},{1,3},{2,0},{3,1},{4,6},{5,7},{6,4},{7,5},{8,10},{9,11},{10,... | collective-permute-start | bytes 1769480 | tf_op jit(solution)/shard_map/ppermute | solution.py:583
  50.1 4.3 %collective-permute-start.10 = (f32[64,256]{1,0:T(8,128)S(1)}, f32[64,256]{1,0:T(8,128)S(1)}, u32[]{:S(2)}, u32[]{:S(2)}) collective-permute-start(f32[64,256]{1,0:T(8,128)S(1)} %add_bitcast_fusion), channel_id=1, source_target_pairs={{0,4},{1,5},{2,6},{3,7},{4,0},{5,1},{6,2},{7,3},{8,12},{9,13},{10,... | collective-permute-start | bytes 196616 | tf_op jit(solution)/shard_map/ppermute | solution.py:583
  54.3 5.9 %collective-permute-start.11 = (f32[64,256]{1,0:T(8,128)S(1)}, f32[64,256]{1,0:T(8,128)S(1)}, u32[]{:S(2)}, u32[]{:S(2)}) collective-permute-start(f32[64,256]{1,0:T(8,128)S(1)} %add.95), channel_id=1, source_target_pairs={{0,8},{1,9},{2,10},{3,11},{4,12},{5,13},{6,14},{7,15},{8,0},{9,1},... | collective-permute-start | bytes 196616 | tf_op jit(solution)/shard_map/ppermute | solution.py:583
  62.2 12.4 %copy-start.8 = (bf16[32,256]{1,0:T(8,128)(2,1)S(1)}, bf16[32,256]{1,0:T(8,128)(2,1)}, u32[]{:S(2)}) copy-start(bf16[32,256]{1,0:T(8,128)(2,1)} %refs_16_.1) | copy-start | bytes 49156
  62.3 12.4 %copy-start.9 = (f32[8]{0:T(128)S(1)}, f32[8]{0:T(128)}, u32[]{:S(2)}) copy-start(f32[8]{0:T(128)} %sharpness.1) | copy-start | bytes 100
  63.8 5.2 %collective-permute-start.13 = (f32[152,256]{1,0:T(8,128)S(1)}, f32[152,256]{1,0:T(8,128)S(1)}, u32[]{:S(2)}, u32[]{:S(2)}) collective-permute-start(f32[152,256]{1,0:T(8,128)S(1)} %mix_back.1.refs_0_), channel_id=1, source_target_pairs={{0,2},{1,3},{2,0},{3,1},{4,6},{5,7},{6,4},{7,5},{8,10},{9,11},{10,... | collective-permute-start | bytes 466952 | tf_op jit(solution)/shard_map/ppermute | solution.py:583
  65.0 7.3 %collective-permute-start.16 = (f32[2,144,256]{2,1,0:T(8,128)S(1)}, f32[2,144,256]{2,1,0:T(8,128)S(1)}, u32[]{:S(2)}, u32[]{:S(2)}) collective-permute-start(f32[2,144,256]{2,1,0:T(8,128)S(1)} %get-tuple-element.97), channel_id=1, source_target_pairs={{0,4},{1,5},{2,6},{3,7},{4,0},{5,1},{6,2},{7,3},{8,12},{9,13},{10,... | collective-permute-start | bytes 884744 | tf_op jit(solution)/shard_map/ppermute | solution.py:583
  65.7 3.4 %collective-permute-start.14 = (f32[152,256]{1,0:T(8,128)S(1)}, f32[152,256]{1,0:T(8,128)S(1)}, u32[]{:S(2)}, u32[]{:S(2)}) collective-permute-start(f32[152,256]{1,0:T(8,128)S(1)} %mix_back.1.refs_0_), channel_id=1, source_target_pairs={{0,1},{1,0},{2,3},{3,2},{4,5},{5,4},{6,7},{7,6},{8,9},{9,8},{10,11... | collective-permute-start | bytes 466952 | tf_op jit(solution)/shard_map/ppermute | solution.py:583
  69.1 3.2 %collective-permute-start.15 = (f32[152,256]{1,0:T(8,128)S(1)}, f32[152,256]{1,0:T(8,128)S(1)}, u32[]{:S(2)}, u32[]{:S(2)}) collective-permute-start(f32[152,256]{1,0:T(8,128)S(1)} %collective-permute-done.13.refs_1_), channel_id=1, source_target_pairs={{0,1},{1,0},{2,3},{3,2},{4,5},{5,4},{6,7},{7,6},{8,9},{9,8},{10,11... | collective-permute-start | bytes 466952 | tf_op jit(solution)/shard_map/ppermute | solution.py:583
  72.3 8.8 %collective-permute-start.17 = (f32[1,144,256]{2,1,0:T(8,128)S(1)}, f32[1,144,256]{2,1,0:T(8,128)S(1)}, u32[]{:S(2)}, u32[]{:S(2)}) collective-permute-start(f32[1,144,256]{2,1,0:T(8,128)S(1)} %slice_add_fusion.5), channel_id=1, source_target_pairs={{0,8},{1,9},{2,10},{3,11},{4,12},{5,13},{6,14},{7,15},{8,0},{9,1},... | collective-permute-start | bytes 442376 | tf_op jit(solution)/shard_map/ppermute | solution.py:583
  81.1 1.6 %collective-permute-start.18 = (f32[288,256]{1,0:T(8,128)S(1)}, f32[288,256]{1,0:T(8,128)S(1)}, u32[]{:S(2)}, u32[]{:S(2)}) collective-permute-start(f32[288,256]{1,0:T(8,128)S(1)} %get-tuple-element.91), channel_id=1, source_target_pairs={{0,1},{1,0},{2,3},{3,2},{4,5},{5,4},{6,7},{7,6},{8,9},{9,8},{10,11... | collective-permute-start | bytes 884744 | tf_op jit(solution)/shard_map/ppermute | solution.py:583
  82.7 6.3 %collective-permute-start.19 = (f32[160,256]{1,0:T(8,128)S(1)}, f32[160,256]{1,0:T(8,128)S(1)}, u32[]{:S(2)}, u32[]{:S(2)}) collective-permute-start(f32[160,256]{1,0:T(8,128)S(1)} %pad_maximum_fusion), channel_id=1, source_target_pairs={{0,2},{1,3},{2,0},{3,1},{4,6},{5,7},{6,4},{7,5},{8,10},{9,11},{10,... | collective-permute-start | bytes 491528 | tf_op jit(solution)/shard_map/ppermute | solution.py:583
  89.1 4.7 %collective-permute-start.20 = (f32[96,256]{1,0:T(8,128)S(1)}, f32[96,256]{1,0:T(8,128)S(1)}, u32[]{:S(2)}, u32[]{:S(2)}) collective-permute-start(f32[96,256]{1,0:T(8,128)S(1)} %pad_maximum_fusion.1), channel_id=1, source_target_pairs={{0,4},{1,5},{2,6},{3,7},{4,0},{5,1},{6,2},{7,3},{8,12},{9,13},{10,... | collective-permute-start | bytes 294920 | tf_op jit(solution)/shard_map/ppermute | solution.py:583
  93.8 5.2 %collective-permute-start.21 = (f32[64,256]{1,0:T(8,128)S(1)}, f32[64,256]{1,0:T(8,128)S(1)}, u32[]{:S(2)}, u32[]{:S(2)}) collective-permute-start(f32[64,256]{1,0:T(8,128)S(1)} %pad_maximum_fusion.2), channel_id=1, source_target_pairs={{0,8},{1,9},{2,10},{3,11},{4,12},{5,13},{6,14},{7,15},{8,0},{9,1},... | collective-permute-start | bytes 196616 | tf_op jit(solution)/shard_map/ppermute | solution.py:583

commit v3 on v2

--- a/solution.py
+++ b/solution.py
@@ -94,10 +94,7 @@
     low_out,
     geo_low_out,
     total,
-    spread,
     maps,
-    logit_map,
-    logits,
     counts,
     sharpness,
     points,
@@ -127,23 +124,27 @@
         copy.start()
     me = lax.axis_index("pts")
     rows, model = points.shape
+    all_rows = rows + geometry.shape[0]
     width, slices = w_slice.shape
     heads = model // width
     groups = total.shape[0]
     per = heads // groups
-    lanes = spread.shape[2]
-    logit_map[...] = jnp.zeros_like(logit_map)
-    for copy in copies:
+    lanes = math.gcd(rows, 128)
+    filled = 2 * per * (width + 1)
+    total[:, filled:, :] = jnp.zeros((groups, total.shape[1] - filled, slices), F32)
+    for copy in copies[:4]:
         copy.wait()
     slice_t = w_slice[...].T
-    for h in range(heads):
-        logit_map[h * slices : (h + 1) * slices, h * width : (h + 1) * width] = slice_t
     maps[:model, :] = w_feat[...].T
     maps[model:, :] = w_mid[...].T
     gain_column = jnp.broadcast_to(gain[...].reshape(1, model), (8, model)).T[:, :1]
+    for copy in copies[4:]:
+        copy.wait()
     live = lax.broadcasted_iota(jnp.int32, (1, rows), 1) < counts[0]
-
-    def block(inputs, at, out_at, weights_ref, low_ref, geo):
+    blocks = range(0, all_rows, rows)
+    for start in blocks:
+        at = slice(start, start + rows)
+        inputs = points[...] if start == 0 else geometry[start - rows : start, :]
         inputs_t = inputs.T.astype(F32)
         shifted = inputs_t - jnp.mean(inputs_t, axis=0, keepdims=True)
         scale = lax.rsqrt(jnp.mean(shifted * shifted, axis=0, keepdims=True) + EPS)
@@ -152,61 +153,49 @@
         normed_out[:, at] = normed
         features_out[:, at] = both[:model]
         middle_out[:, at] = both[model:]
-        logits[...] = dot(logit_map[...], both[model:])
-        for h in range(heads):
-            cols = slice(h * slices, (h + 1) * slices)
-            factor = sharpness[h] * math.log2(math.e)
-            for start in range(0, rows, lanes):
-                part = logits[cols, start : start + lanes]
-                powers = jnp.exp2((part - jnp.max(part, axis=0, keepdims=True)) * factor)
-                inverse = 1.0 / jnp.sum(powers, axis=0, keepdims=True)
-                if not geo:
-                    inverse = jnp.where(live[:, start : start + lanes], inverse, 0.0)
-                weights = powers * inverse
-                where = pl.ds(out_at + start, lanes)
-                weights_ref[cols, where] = weights
-                low_ref[cols, where] = weights.astype(BF16)
-                if start == 0 and not geo:
-                    spread[0, cols, :] = weights
-                else:
-                    spread[int(geo), cols, :] += weights
-
-    spread[1] = jnp.zeros_like(spread[1])
-    block(points[...], pl.ds(0, rows), 0, weights_out, low_out, False)
-
-    @pl.loop(0, geometry.shape[0] // rows)
-    def _(i):
-        start = pl.multiple_of(i * rows, rows)
-        block(
-            geometry[pl.ds(start, rows), :],
-            pl.ds(pl.multiple_of(start + rows, rows), rows),
-            start,
-            geo_weights_out,
-            geo_low_out,
-            True,
-        )
-
-    ones = jnp.ones((16, lanes), BF16)
-    for geo, (low_ref, at) in enumerate(
-        ((low_out, slice(0, rows)), (geo_low_out, slice(rows, rows + geometry.shape[0])))
-    ):
-        high = spread[geo].astype(BF16)
-        rest = spread[geo] - high.astype(F32)
-        middle = rest.astype(BF16)
-        low = (rest - middle.astype(F32)).astype(BF16)
-        sums = dot(ones, high, NT) + dot(ones, middle, NT) + dot(ones, low, NT)
-        for h in range(heads):
-            g, j = h // per, h % per
-            row = 2 * per * width + geo * per + j
-            total[g, row : row + 1, :] = sums[:1, h * slices : (h + 1) * slices]
+
+    def logits_of(h):
+        own = slice(h * width, (h + 1) * width)
+        return [dot(slice_t, middle_out[own, start : start + rows]) for start in blocks]
+
+    def numerators(h):
+        own = slice(h * width, (h + 1) * width)
+        cols = slice(h * slices, (h + 1) * slices)
+        g, j = h // per, h % per
+        for geo, (low_ref, at) in enumerate(
+            ((low_out, slice(0, rows)), (geo_low_out, slice(rows, all_rows)))
+        ):
             row = (geo * per + j) * width
-            total[g, row : row + width, :] = dot(
-                features_out[h * width : (h + 1) * width, at],
-                low_ref[h * slices : (h + 1) * slices, :],
-                NT,
-            )
-    filled = 2 * per * (width + 1)
-    total[:, filled:, :] = jnp.zeros((groups, total.shape[1] - filled, slices), F32)
+            total[g, row : row + width, :] = dot(features_out[own, at], low_ref[cols, :], NT)
+
+    ahead = logits_of(0)
+    for h in range(heads):
+        cols = slice(h * slices, (h + 1) * slices)
+        logits = ahead
+        if h + 1 < heads:
+            ahead = logits_of(h + 1)
+        factor = sharpness[h] * math.log2(math.e)
+        for geo, first in ((0, 0), (1, 1)):
+            weights_ref, low_ref = ((weights_out, low_out), (geo_weights_out, geo_low_out))[geo]
+            folded = None
+            for i in range(first, 1 if geo == 0 else len(logits)):
+                for start in range(0, rows, lanes):
+                    part = logits[i][:, start : start + lanes]
+                    powers = jnp.exp2((part - jnp.max(part, axis=0, keepdims=True)) * factor)
+                    inverse = 1.0 / jnp.sum(powers, axis=0, keepdims=True)
+                    if geo == 0:
+                        inverse = jnp.where(live[:, start : start + lanes], inverse, 0.0)
+                    weights = powers * inverse
+                    where = (i - first) * rows + start
+                    weights_ref[cols, where : where + lanes] = weights
+                    low_ref[cols, where : where + lanes] = weights.astype(BF16)
+                    folded = weights if folded is None else folded + weights
+            row = 2 * per * width + geo * per + h % per
+            total[h // per, row : row + 1, :] = jnp.sum(folded.T, axis=0, keepdims=True)
+        if h > 0:
+            numerators(h - 1)
+    numerators(heads - 1)
+
     place_groups(lambda g: total[g], keep, send, me & (groups - 1))
 
 
@@ -227,15 +216,15 @@
     width = w_query.shape[0]
     per = attention_out.shape[0]
     slices = tokens.shape[1]
+    maps = jnp.concatenate([w_query[...], w_key[...], w_value[...]], axis=1)
     for j in range(per):
         (field, _), (geo, _) = token_rows(tokens, j, per, width)
         both = jnp.concatenate([field, geo], axis=1)
-        query = narrow_dot(w_query[...], field)
-        keys = narrow_dot(w_key[...], both)
-        values = narrow_dot(w_value[...], both)
-        kept[j, :width, :slices] = query
-        kept[j, width : 2 * width, :] = keys
-        kept[j, 2 * width :, :] = values
+        projected = narrow_dot(maps, both)
+        kept[j] = projected
+        query = projected[:width, :slices]
+        keys = projected[width : 2 * width]
+        values = projected[2 * width :]
         scores = narrow_dot(keys, query)
         scores = (scores - jnp.max(scores, axis=0, keepdims=True)) * (
             math.log2(math.e) / math.sqrt(width)
@@ -252,7 +241,8 @@
     base = 2 * per * width
     small = jnp.zeros((width, 3 * width), F32)
     out[base : base + pad_to(2 * per, 8), :] = jnp.zeros((pad_to(2 * per, 8), slices), F32)
-    w_query_t, w_key_t, w_value_t = w_query[...].T, w_key[...].T, w_value[...].T
+    maps_t = jnp.concatenate([w_query[...].T, w_key[...].T, w_value[...].T], axis=0)
+    none = jnp.zeros((width, both_count - slices), F32)
     for j in range(per):
         (field, field_den), (geo, geo_den) = token_rows(tokens, j, per, width)
         both = jnp.concatenate([field, geo], axis=1)
@@ -267,17 +257,13 @@
         value_grad = wide_dot(mixed_grad, split(attention), NT)
         query_grad = wide_dot(keys, score_grad, NN)
         key_grad = wide_dot(query, score_grad, NT)
-        both_grad = narrow_dot(w_key_t, key_grad) + narrow_dot(w_value_t, value_grad)
-        field_grad = both_grad[:, :slices] + narrow_dot(w_query_t, query_grad)
+        grads = jnp.concatenate(
+            [jnp.concatenate([query_grad, none], axis=1), key_grad, value_grad], axis=0
+        )
+        both_grad = narrow_dot(maps_t, grads)
+        field_grad = both_grad[:, :slices]
         geo_grad = both_grad[:, slices:]
-        small += jnp.concatenate(
-            [
-                wide_dot(field, split(query_grad), NT),
-                wide_dot(both, split(key_grad), NT),
-                wide_dot(both, split(value_grad), NT),
-            ],
-            axis=1,
-        )
+        small += wide_dot(both, split(grads), NT)
         for g, (value, den, value_of) in enumerate(
             ((field_grad, field_den, field), (geo_grad, geo_den, geo))
         ):
@@ -418,7 +404,6 @@
         right,
         total,
         slice_sum,
-        products,
         logit,
     ) = refs[2 * groups :]
     me = lax.axis_index("pts")
@@ -451,46 +436,57 @@
                 left_geo[h] = left
             else:
                 left_field[h] = left
-    slice_sum[...] = jnp.zeros_like(slice_sum)
+    all_rows = normed.shape[1]
+    lanes = math.gcd(rows, 128)
     ones = jnp.ones((16, rows), BF16)
-
-    def block(at, own_at, weights_ref, low_ref, geo):
-        left_ref = left_geo if geo else left_field
-        for h in range(heads):
-            own = slice(h * width, (h + 1) * width)
-            stack = [features[own, at]]
-            if not geo:
+    blocks = range(0, all_rows, rows)
+
+    def products_of(h):
+        own = slice(h * width, (h + 1) * width)
+        out = []
+        for start in blocks:
+            stack = [features[own, start : start + rows]]
+            if start == 0:
                 stack.append(grad_att[own, :])
-            products[h * slices : (h + 1) * slices, :] = dot(
-                left_ref[h], jnp.concatenate(stack + [ones], axis=0)
-            )
-        for h in range(heads):
-            cols = slice(h * slices, (h + 1) * slices)
+            left = left_field if start == 0 else left_geo
+            out.append(dot(left[h], jnp.concatenate(stack + [ones], axis=0)))
+        return out
+
+    def finish(h):
+        cols = slice(h * slices, (h + 1) * slices)
+        own = slice(h * width, (h + 1) * width)
+        right[own, :rows] = dot(low_numer[0, own, :], low[cols, :]).astype(BF16)
+        right[own, rows:] = dot(low_numer[1, own, :], geo_low[cols, :]).astype(BF16)
+        right[model + h * width : model + (h + 1) * width, :] = dot(
+            w_slice[...], logit[cols, :]
+        ).astype(BF16)
+        term = dot(logit[cols, :], middle[own, :], NT)
+        if h == 0:
+            slice_sum[...] = term
+        else:
+            slice_sum[...] += term
+
+    ahead = products_of(0)
+    for h in range(heads):
+        cols = slice(h * slices, (h + 1) * slices)
+        products = ahead
+        if h + 1 < heads:
+            ahead = products_of(h + 1)
+        for i, begin in enumerate(blocks):
             for start in range(0, rows, lanes):
-                grad_weights = products[cols, start : start + lanes]
-                share = weights_ref[cols, pl.ds(own_at + start, lanes)]
+                grad_weights = products[i][:, start : start + lanes]
+                if i == 0:
+                    share = weights[cols, start : start + lanes]
+                else:
+                    where = begin - rows + start
+                    share = geo_weights[cols, where : where + lanes]
                 inner = jnp.sum(share * grad_weights, axis=0, keepdims=True)
-                logit[cols, start : start + lanes] = (
+                logit[cols, begin + start : begin + start + lanes] = (
                     share * (grad_weights - inner) * sharpness[h]
                 ).astype(BF16)
-        for h in range(heads):
-            cols = slice(h * slices, (h + 1) * slices)
-            own = slice(h * width, (h + 1) * width)
-            right[own, at] = dot(
-                low_numer[int(geo), own, :], low_ref[cols, pl.ds(own_at, rows)]
-            ).astype(BF16)
-            right[model + h * width : model + (h + 1) * width, at] = dot(
-                w_slice[...], logit[cols, :]
-            ).astype(BF16)
-            slice_sum[...] += dot(middle[own, at], logit[cols, :], NT)
-
-    lanes = math.gcd(rows, 128)
-    block(pl.ds(0, rows), 0, weights, low, False)
-
-    @pl.loop(0, normed.shape[1] // rows - 1)
-    def _(i):
-        start = pl.multiple_of(i * rows, rows)
-        block(pl.ds(pl.multiple_of(start + rows, rows), rows), start, geo_weights, geo_low, True)
+        if h > 0:
+            finish(h - 1)
+    finish(heads - 1)
 
     total[...] = dot(normed[...], right[...], NT)
     half = keep.shape[0] // 2
@@ -506,7 +502,7 @@
             row = (pos - half) * 2 * step
             send[row : row + step, :] = value[:, :model]
             send[row + step : row + 2 * step, :] = value[:, model:]
-    send[half * 2 * step :, :] = slice_sum[...]
+    send[half * 2 * step :, :] = slice_sum[...].T
 
     small_rows = width // 2
     packed = canon[0, canon.shape[1] - small_rows :, :]
@@ -515,6 +511,13 @@
     wide = jnp.concatenate([packed[:, : slices // 2], packed[:, slices // 2 :]], axis=0)
     for i in range(3):
         grad_mix[i] = wide[:, i * width : (i + 1) * width]
+
+
+def finish_kernel(keep, got, slice_sum, feat, mid, slice_out):
+    step = feat.shape[0]
+    feat[...] = keep[:step, :] + got[:step, :]
+    mid[...] = keep[step:, :] + got[step : 2 * step, :]
+    slice_out[...] = slice_sum[...] + got[2 * step :, :]
 
 
 VMEM = pl.BlockSpec(memory_space=pltpu.VMEM)
@@ -618,10 +621,7 @@
         ),
         [
             pltpu.VMEM((groups, token_height, slices), F32),
-            pltpu.VMEM((2, heads * slices, math.gcd(rows, 128)), F32),
             pltpu.VMEM((2 * model, model), BF16),
-            pltpu.VMEM((heads * slices, model), BF16),
-            pltpu.VMEM((heads * slices, rows), F32),
             pltpu.SMEM(counts.shape, jnp.int32),
             pltpu.SMEM(sharpness.shape, F32),
             pltpu.VMEM(points.shape, BF16),
@@ -769,9 +769,8 @@
             pltpu.VMEM((2, model, slices), BF16),
             pltpu.VMEM((2 * model, all_rows), BF16),
             pltpu.VMEM((model, 2 * model), F32),
-            pltpu.VMEM((width, slices), F32),
-            pltpu.VMEM((heads * slices, rows), F32),
-            pltpu.VMEM((heads * slices, rows), BF16),
+            pltpu.VMEM((slices, width), F32),
+            pltpu.VMEM((heads * slices, all_rows), BF16),
         ],
         sharpness,
         *grad_pieces,
@@ -795,22 +794,30 @@
             outer_keep, outer_send = fold(outer_keep, outer_got)
             outer_got = exchange(outer_send, bit + 4)
         got = exchange(send, bit)
-        count = keep.shape[0]
-        slice_sum = slice_sum + got[count:]
-        if bit < all_bits - 1:
-            count //= 2
-            send = jnp.concatenate([keep[count:] + got[count : 2 * count], slice_sum], axis=0)
-            keep = keep[:count] + got[:count]
-        else:
-            grad_feat = keep[:step] + got[:step]
-            grad_mid = keep[step:] + got[step : 2 * step]
+        if bit == all_bits - 1:
+            break
+        slice_sum = slice_sum + got[keep.shape[0] :]
+        count = keep.shape[0] // 2
+        send = jnp.concatenate([keep[count:] + got[count : 2 * count], slice_sum], axis=0)
+        keep = keep[:count] + got[:count]
+    grad_feat, grad_mid, grad_slice = run(
+        finish_kernel,
+        "finish",
+        4,
+        VMEM,
+        (shape((step, model)), shape((step, model)), shape((width, slices))),
+        [],
+        keep,
+        got,
+        slice_sum,
+    )
     outer = (outer_keep + outer_got)[0]
     grad_out = outer[:step]
     grad_up = jnp.concatenate(
         [outer[step * (1 + w) : step * (2 + w)] for w in range(wide)], axis=1
     )
     grad_down = outer[step * (1 + wide) :]
-    return (layer_out, grad_feat, grad_mid, grad_out, grad_up, grad_down, slice_sum, grad_mix)
+    return (layer_out, grad_feat, grad_mid, grad_out, grad_up, grad_down, grad_slice, grad_mix)
 
 
 def solution(mesh):

time: 100 us -> 95.7 us (0.957)
  Pallas kernels: 21.9 us -> 17.6 us
  other arithmetic: 2.42 us -> 1.19 us
    pallas_call x6 -> x7, Pallas kernels: 21.9 us -> 17.6 us  [run(): pl.pallas_call(body, out_shape=out_shape, in_specs=[first] + [rest] * (le...]
    add x4 -> x3, other arithmetic: 1.24 us -> 0.02 us  [the longest x1 0.01 us: on_device(): keep[count:] + got[count:2 * count]]
  transfers between devices with their start and end apart: 22 -> 22, of which waited for: 17 -> 18; matrix products, arithmetic and copies ran while one was open for 2% -> 2% of each run, Pallas kernels for 8% -> 7%
where the time goes in v3:
time: 95.7 us; the launch traced here: 95.5 us
  waiting for transfers between devices  51.6 us (54%)
  starting transfers between devices  22.2 us (23%)
  Pallas kernels  17.6 us (18%)
  between operations  1.54 us (2%)
  local copies, waits for them, and re-layouts  1.31 us (1%)
  other arithmetic  1.19 us (1%)
    ppermute x22, waiting for transfers between devices, exchange(): return lax.ppermute(value, 'pts', [(i, i ^ 1 << bit) for i in range(parts)])  51.6 us
    ppermute x22, starting transfers between devices, exchange(): return lax.ppermute(value, 'pts', [(i, i ^ 1 << bit) for i in range(parts)])  22.2 us
    pallas_call x7, Pallas kernels, run(): pl.pallas_call(body, out_shape=out_shape, in_specs=[first] + [rest] * (le...  17.6 us
  transfers between devices with their start and end apart: 22, of which 18 were waited for; matrix products, arithmetic and copies ran while one was open for 2% of the time, Pallas kernels for 7%

profile of v3, /device:TPU:0, one launch (start us, length us, event | category | flops | bytes accessed | tf_op | source)
XLA Modules:
  0.0 95.5 jit_solution(8220831850396170416)
XLA Ops:
  1.3 0.0 copy-start.5
  1.3 0.0 copy-start.6
  1.3 0.0 copy-start.7
  1.3 0.0 copy-start
  1.3 0.0 copy-start.1
  1.3 0.0 copy-start.2
  1.3 0.0 copy-start.3
  1.4 4.9 %slice_sums.1 = (f32[2,136,256]{2,1,0:T(8,128)S(1)}, f32[2,136,256]{2,1,0:T(8,128)S(1)}, bf16[256,768]{1,0:T(8,128)(2,1)S(1)}, bf16[256,768]{1,0:T(8,128)(2,1)S(...) custom-call(s32[1]{0:T(128)S(6)} %copy.24.counts_hbm, ...), custom_call_target="tpu_custom_call" | custom-call | tf_op jit(solution)/shard_map/slice_sums/pallas_call | solution.py:539
  6.2 0.5 collective-permute-start
  6.8 1.2 %collective-permute-done = f32[2,136,256]{2,1,0:T(8,128)S(1)} collective-permute-done((f32[2,136,256]{2,1,0:T(8,128)S(1)}, f32[2,136,256]{2,1,0:T(8,128)S(1)}, u32[]{:S(2)}, u32[]{:S(2)}) %collective-permute-start) | collective-permute-done | bytes 278560 | tf_op jit(solution)/shard_map/ppermute | solution.py:586
  8.0 2.9 %collective-permute-start.1 = (f32[1,136,256]{2,1,0:T(8,128)S(1)}, f32[1,136,256]{2,1,0:T(8,128)S(1)}, u32[]{:S(2)}, u32[]{:S(2)}) collective-permute-start(f32[1,136,256]{2,1,0:T(8,128)S(1)} %slice_add_fusion.6), channel_id=1, source_target_pairs={{0,2},{1,3},{2,0},{3,1},{4,6},{5,7},{6,4},{7,5},{8,10},{9,11},{10,... | collective-permute-start | bytes 417800 | tf_op jit(solution)/shard_map/ppermute | solution.py:586
  10.9 4.0 %collective-permute-done.1 = f32[1,136,256]{2,1,0:T(8,128)S(1)} collective-permute-done((f32[1,136,256]{2,1,0:T(8,128)S(1)}, f32[1,136,256]{2,1,0:T(8,128)S(1)}, u32[]{:S(2)}, u32[]{:S(2)}) %collective-permute-start.1) | collective-permute-done | bytes 139296 | tf_op jit(solution)/shard_map/ppermute | solution.py:586
  14.9 1.9 %collective-permute-start.2 = (f32[136,256]{1,0:T(8,128)S(1)}, f32[136,256]{1,0:T(8,128)S(1)}, u32[]{:S(2)}, u32[]{:S(2)}) collective-permute-start(f32[136,256]{1,0:T(8,128)S(1)} %fusion.2), channel_id=1, source_target_pairs={{0,4},{1,5},{2,6},{3,7},{4,0},{5,1},{6,2},{7,3},{8,12},{9,13},{10,... | collective-permute-start | bytes 417800 | tf_op jit(solution)/shard_map/ppermute | solution.py:586
  16.8 3.4 %collective-permute-done.2 = f32[136,256]{1,0:T(8,128)S(1)} collective-permute-done((f32[136,256]{1,0:T(8,128)S(1)}, f32[136,256]{1,0:T(8,128)S(1)}, u32[]{:S(2)}, u32[]{:S(2)}) %collective-permute-start.2) | collective-permute-done | bytes 139296 | tf_op jit(solution)/shard_map/ppermute | solution.py:586
  20.2 2.7 %collective-permute-start.3 = (f32[136,256]{1,0:T(8,128)S(1)}, f32[136,256]{1,0:T(8,128)S(1)}, u32[]{:S(2)}, u32[]{:S(2)}) collective-permute-start(f32[136,256]{1,0:T(8,128)S(1)} %add.81), channel_id=1, source_target_pairs={{0,8},{1,9},{2,10},{3,11},{4,12},{5,13},{6,14},{7,15},{8,0},{9,1},... | collective-permute-start | bytes 417800 | tf_op jit(solution)/shard_map/ppermute | solution.py:586
  23.0 5.5 %collective-permute-done.3 = f32[136,256]{1,0:T(8,128)S(1)} collective-permute-done((f32[136,256]{1,0:T(8,128)S(1)}, f32[136,256]{1,0:T(8,128)S(1)}, u32[]{:S(2)}, u32[]{:S(2)}) %collective-permute-start.3) | collective-permute-done | bytes 139296 | tf_op jit(solution)/shard_map/ppermute | solution.py:586
  28.5 1.7 %mix_tokens.1 = (f32[64,256]{1,0:T(8,128)S(1)}, f32[2,512,256]{2,1,0:T(8,128)S(1)}, f32[2,96,512]{2,1,0:T(8,128)S(1)}) custom-call(f32[136,256]{1,0:T(8,128)S(1)} %add.82.tokens, f32[32,32]{1,0:T(8,128)S(1)} %copy-done.5, f32[32,32]{1,0:T(8,128)S(1)} %copy-done.6, f32[32,32]{1,0:T(8,128)S(1)} %copy-done.7), custom_call_target="tpu_custom_call" | custom-call | tf_op jit(solution)/shard_map/mix_tokens/pallas_call | solution.py:539
  30.3 1.0 %collective-permute-start.4 = (f32[64,256]{1,0:T(8,128)S(1)}, f32[64,256]{1,0:T(8,128)S(1)}, u32[]{:S(2)}, u32[]{:S(2)}) collective-permute-start(f32[64,256]{1,0:T(8,128)S(1)} %get-tuple-element.56.refs_0_.refs_4_), channel_id=1, source_target_pairs={{0,2},{1,3},{2,0},{3,1},{4,6},{5,7},{6,4},{7,5},{8,10},{9,11},{10,... | collective-permute-start | bytes 196616 | tf_op jit(solution)/shard_map/ppermute | solution.py:586
  31.3 0.0 collective-permute-start.5
  31.3 3.2 %collective-permute-done.4.refs_1_.refs_5_ = f32[64,256]{1,0:T(8,128)S(1)} collective-permute-done((f32[64,256]{1,0:T(8,128)S(1)}, f32[64,256]{1,0:T(8,128)S(1)}, u32[]{:S(2)}, u32[]{:S(2)}) %collective-permute-start.4) | collective-permute-done | bytes 65568 | tf_op jit(solution)/shard_map/ppermute | solution.py:586
  34.5 0.0 collective-permute-start.6
  34.5 0.0 collective-permute-done.5.refs_2_.refs_6_
  34.5 1.2 %collective-permute-done.6.refs_3_.refs_7_ = f32[64,256]{1,0:T(8,128)S(1)} collective-permute-done((f32[64,256]{1,0:T(8,128)S(1)}, f32[64,256]{1,0:T(8,128)S(1)}, u32[]{:S(2)}, u32[]{:S(2)}) %collective-permute-start.6) | collective-permute-done | bytes 65568 | tf_op jit(solution)/shard_map/ppermute | solution.py:586
  35.8 2.8 %mlp.1 = (bf16[256,256]{1,0:T(8,128)(2,1)}, bf16[256,256]{1,0:T(8,128)(2,1)S(1)}, f32[2,64,256]{2,1,0:T(8,128)S(1)}, f32[2,64,256]{2,1,0:T(8,128)S(1)}, bf16[256...) custom-call(f32[64,256]{1,0:T(8,128)S(1)} %get-tuple-element.56.refs, ...), custom_call_target="tpu_custom_call" | custom-call | tf_op jit(solution)/shard_map/mlp/pallas_call | solution.py:539
  38.7 0.2 collective-permute-start.7
  38.8 1.2 %collective-permute-done.7 = f32[2,64,256]{2,1,0:T(8,128)S(1)} collective-permute-done((f32[2,64,256]{2,1,0:T(8,128)S(1)}, f32[2,64,256]{2,1,0:T(8,128)S(1)}, u32[]{:S(2)}, u32[]{:S(2)}) %collective-permute-start.7) | collective-permute-done | bytes 131104 | tf_op jit(solution)/shard_map/ppermute | solution.py:586
  40.0 0.6 weight_grads.1
  40.6 0.2 collective-permute-start.9
  40.8 1.1 %collective-permute-start.8 = (f32[1,64,256]{2,1,0:T(8,128)S(1)}, f32[1,64,256]{2,1,0:T(8,128)S(1)}, u32[]{:S(2)}, u32[]{:S(2)}) collective-permute-start(f32[1,64,256]{2,1,0:T(8,128)S(1)} %slice_add_fusion.12), channel_id=1, source_target_pairs={{0,2},{1,3},{2,0},{3,1},{4,6},{5,7},{6,4},{7,5},{8,10},{9,11},{10,... | collective-permute-start | bytes 196616 | tf_op jit(solution)/shard_map/ppermute | solution.py:586
  41.9 3.3 %collective-permute-done.8 = f32[1,64,256]{2,1,0:T(8,128)S(1)} collective-permute-done((f32[1,64,256]{2,1,0:T(8,128)S(1)}, f32[1,64,256]{2,1,0:T(8,128)S(1)}, u32[]{:S(2)}, u32[]{:S(2)}) %collective-permute-start.8) | collective-permute-done | bytes 65568 | tf_op jit(solution)/shard_map/ppermute | solution.py:586
  45.2 0.0 collective-permute-done.9
  45.3 0.2 slice_add_fusion
  45.4 1.1 %collective-permute-start.12 = (f32[4,144,256]{2,1,0:T(8,128)S(1)}, f32[4,144,256]{2,1,0:T(8,128)S(1)}, u32[]{:S(2)}, u32[]{:S(2)}) collective-permute-start(f32[4,144,256]{2,1,0:T(8,128)S(1)} %get-tuple-element.101), channel_id=1, source_target_pairs={{0,2},{1,3},{2,0},{3,1},{4,6},{5,7},{6,4},{7,5},{8,10},{9,11},{10,... | collective-permute-start | bytes 1769480 | tf_op jit(solution)/shard_map/ppermute | solution.py:586
  46.5 0.7 collective-permute-start.10
  47.2 3.6 %collective-permute-done.10 = f32[64,256]{1,0:T(8,128)S(1)} collective-permute-done((f32[64,256]{1,0:T(8,128)S(1)}, f32[64,256]{1,0:T(8,128)S(1)}, u32[]{:S(2)}, u32[]{:S(2)}) %collective-permute-start.10) | collective-permute-done | bytes 65568 | tf_op jit(solution)/shard_map/ppermute | solution.py:586
  50.8 2.1 %collective-permute-start.11 = (f32[64,256]{1,0:T(8,128)S(1)}, f32[64,256]{1,0:T(8,128)S(1)}, u32[]{:S(2)}, u32[]{:S(2)}) collective-permute-start(f32[64,256]{1,0:T(8,128)S(1)} %add.86), channel_id=1, source_target_pairs={{0,8},{1,9},{2,10},{3,11},{4,12},{5,13},{6,14},{7,15},{8,0},{9,1},... | collective-permute-start | bytes 196616 | tf_op jit(solution)/shard_map/ppermute | solution.py:586
  52.9 3.8 %collective-permute-done.11 = f32[64,256]{1,0:T(8,128)S(1)} collective-permute-done((f32[64,256]{1,0:T(8,128)S(1)}, f32[64,256]{1,0:T(8,128)S(1)}, u32[]{:S(2)}, u32[]{:S(2)}) %collective-permute-start.11) | collective-permute-done | bytes 65568 | tf_op jit(solution)/shard_map/ppermute | solution.py:586
  56.7 1.8 %mix_back.1.refs_0_ = f32[152,256]{1,0:T(8,128)S(1)} custom-call(f32[136,256]{1,0:T(8,128)S(1)} %add.82.tokens, f32[2,512,256]{2,1,0:T(8,128)S(1)} %get-tuple-element.59.attention_in, f32[2,96,512]{2,1,0:T(8,128)S(1)} %get-tuple-element.60.kept, f32[64,256]{1,0:T(8,128)S(1)} %add.87.grad, f32[32,32]{1,0:T(8,128)S(1)} %copy-done.5, f32[32,32]{1,0:T(8,128)S(1)} %copy-done.6, ...), custom_call_target="tpu_custom_call" | custom-call | tf_op jit(solution)/shard_map/mix_back/pallas_call | solution.py:539
  58.6 0.0 copy-start.9
  58.6 1.7 %collective-permute-done.12 = f32[4,144,256]{2,1,0:T(8,128)S(1)} collective-permute-done((f32[4,144,256]{2,1,0:T(8,128)S(1)}, f32[4,144,256]{2,1,0:T(8,128)S(1)}, u32[]{:S(2)}, u32[]{:S(2)}) %collective-permute-start.12) | collective-permute-done | bytes 589856 | tf_op jit(solution)/shard_map/ppermute | solution.py:586
  60.3 1.0 %collective-permute-start.13 = (f32[152,256]{1,0:T(8,128)S(1)}, f32[152,256]{1,0:T(8,128)S(1)}, u32[]{:S(2)}, u32[]{:S(2)}) collective-permute-start(f32[152,256]{1,0:T(8,128)S(1)} %mix_back.1.refs_0_), channel_id=1, source_target_pairs={{0,2},{1,3},{2,0},{3,1},{4,6},{5,7},{6,4},{7,5},{8,10},{9,11},{10,... | collective-permute-start | bytes 466952 | tf_op jit(solution)/shard_map/ppermute | solution.py:586
  61.3 0.1 slice_add_fusion.2
  61.4 0.7 collective-permute-start.16
  62.1 0.0 collective-permute-start.14
  62.1 3.4 %collective-permute-done.13.refs_1_ = f32[152,256]{1,0:T(8,128)S(1)} collective-permute-done((f32[152,256]{1,0:T(8,128)S(1)}, f32[152,256]{1,0:T(8,128)S(1)}, u32[]{:S(2)}, u32[]{:S(2)}) %collective-permute-start.13) | collective-permute-done | bytes 155680 | tf_op jit(solution)/shard_map/ppermute | solution.py:586
  65.5 0.0 collective-permute-start.15
  65.5 0.0 collective-permute-done.14.refs_2_
  65.5 3.2 %collective-permute-done.16 = f32[2,144,256]{2,1,0:T(8,128)S(1)} collective-permute-done((f32[2,144,256]{2,1,0:T(8,128)S(1)}, f32[2,144,256]{2,1,0:T(8,128)S(1)}, u32[]{:S(2)}, u32[]{:S(2)}) %collective-permute-start.16) | collective-permute-done | bytes 294944 | tf_op jit(solution)/shard_map/ppermute | solution.py:586
  68.7 0.0 collective-permute-done.15.refs_3_
  68.7 2.4 %collective-permute-start.17 = (f32[1,144,256]{2,1,0:T(8,128)S(1)}, f32[1,144,256]{2,1,0:T(8,128)S(1)}, u32[]{:S(2)}, u32[]{:S(2)}) collective-permute-start(f32[1,144,256]{2,1,0:T(8,128)S(1)} %slice_add_fusion.5), channel_id=1, source_target_pairs={{0,8},{1,9},{2,10},{3,11},{4,12},{5,13},{6,14},{7,15},{8,0},{9,1},... | collective-permute-start | bytes 442376 | tf_op jit(solution)/shard_map/ppermute | solution.py:586
  71.1 5.2 %point_back.1 = (f32[16,16,256]{2,1,0:T(8,128)S(1)}, f32[288,256]{1,0:T(8,128)S(1)}, f32[3,32,32]{2,1,0:T(8,128)}) custom-call(f32[8]{0:T(128)S(1)} %copy-done.9, f32[152,256]{1,0:T(8,128)S(1)} %mix_back.1.refs_0_, f32[152,256]{1,0:T(8,128)S(1)} %collective-permute-done.13.refs_1_, f32[152,256]{1,0:T(8,128)S(1)} %collective-permute-done.14.refs_2_, ...), custom_call_target="tpu_custom_call" | custom-call | tf_op jit(solution)/shard_map/point_back/pallas_call | solution.py:539
  76.3 0.6 collective-permute-done.17
  76.9 0.0 collective-permute-start.18
  77.0 1.5 %collective-permute-done.18 = f32[288,256]{1,0:T(8,128)S(1)} collective-permute-done((f32[288,256]{1,0:T(8,128)S(1)}, f32[288,256]{1,0:T(8,128)S(1)}, u32[]{:S(2)}, u32[]{:S(2)}) %collective-permute-start.18) | collective-permute-done | bytes 294944 | tf_op jit(solution)/shard_map/ppermute | solution.py:586
  78.6 1.1 %collective-permute-start.19 = (f32[160,256]{1,0:T(8,128)S(1)}, f32[160,256]{1,0:T(8,128)S(1)}, u32[]{:S(2)}, u32[]{:S(2)}) collective-permute-start(f32[160,256]{1,0:T(8,128)S(1)} %pad_maximum_fusion), channel_id=1, source_target_pairs={{0,2},{1,3},{2,0},{3,1},{4,6},{5,7},{6,4},{7,5},{8,10},{9,11},{10,... | collective-permute-start | bytes 491528 | tf_op jit(solution)/shard_map/ppermute | solution.py:586
  79.6 0.6 slice_bitcast_fusion
  80.3 4.6 %collective-permute-done.19 = f32[160,256]{1,0:T(8,128)S(1)} collective-permute-done((f32[160,256]{1,0:T(8,128)S(1)}, f32[160,256]{1,0:T(8,128)S(1)}, u32[]{:S(2)}, u32[]{:S(2)}) %collective-permute-start.19) | collective-permute-done | bytes 163872 | tf_op jit(solution)/shard_map/ppermute | solution.py:586
  84.9 1.2 %collective-permute-start.20 = (f32[96,256]{1,0:T(8,128)S(1)}, f32[96,256]{1,0:T(8,128)S(1)}, u32[]{:S(2)}, u32[]{:S(2)}) collective-permute-start(f32[96,256]{1,0:T(8,128)S(1)} %pad_maximum_fusion.1), channel_id=1, source_target_pairs={{0,4},{1,5},{2,6},{3,7},{4,0},{5,1},{6,2},{7,3},{8,12},{9,13},{10,... | collective-permute-start | bytes 294920 | tf_op jit(solution)/shard_map/ppermute | solution.py:586
  86.2 0.6 slice_bitcast_fusion.4
  86.8 2.8 %collective-permute-done.20 = f32[96,256]{1,0:T(8,128)S(1)} collective-permute-done((f32[96,256]{1,0:T(8,128)S(1)}, f32[96,256]{1,0:T(8,128)S(1)}, u32[]{:S(2)}, u32[]{:S(2)}) %collective-permute-start.20) | collective-permute-done | bytes 98336 | tf_op jit(solution)/shard_map/ppermute | solution.py:586
  89.6 1.3 %collective-permute-start.21 = (f32[64,256]{1,0:T(8,128)S(1)}, f32[64,256]{1,0:T(8,128)S(1)}, u32[]{:S(2)}, u32[]{:S(2)}) collective-permute-start(f32[64,256]{1,0:T(8,128)S(1)} %pad_maximum_fusion.2), channel_id=1, source_target_pairs={{0,8},{1,9},{2,10},{3,11},{4,12},{5,13},{6,14},{7,15},{8,0},{9,1},... | collective-permute-start | bytes 196616 | tf_op jit(solution)/shard_map/ppermute | solution.py:586
  91.0 0.6 pad_maximum_fusion.3
  91.6 3.3 %collective-permute-done.21.got = f32[64,256]{1,0:T(8,128)S(1)} collective-permute-done((f32[64,256]{1,0:T(8,128)S(1)}, f32[64,256]{1,0:T(8,128)S(1)}, u32[]{:S(2)}, u32[]{:S(2)}) %collective-permute-start.21) | collective-permute-done | bytes 65568 | tf_op jit(solution)/shard_map/ppermute | solution.py:586
  94.9 0.6 finish.1
  (33 shorter events, 0.3 us)
Async XLA Ops:
  1.3 27.2 %copy-start.5 = (f32[32,32]{1,0:T(8,128)S(1)}, f32[32,32]{1,0:T(8,128)}, u32[]{:S(2)}) copy-start(f32[32,32]{1,0:T(8,128)} %w_query.3) | copy-start | bytes 12292
  1.3 27.2 %copy-start.6 = (f32[32,32]{1,0:T(8,128)S(1)}, f32[32,32]{1,0:T(8,128)}, u32[]{:S(2)}) copy-start(f32[32,32]{1,0:T(8,128)} %w_key.3) | copy-start | bytes 12292
  1.3 27.2 %copy-start.7 = (f32[32,32]{1,0:T(8,128)S(1)}, f32[32,32]{1,0:T(8,128)}, u32[]{:S(2)}) copy-start(f32[32,32]{1,0:T(8,128)} %w_value.3) | copy-start | bytes 12292
  1.3 34.5 %copy-start = (bf16[256,1024]{1,0:T(8,128)(2,1)S(1)}, bf16[256,1024]{1,0:T(8,128)(2,1)}, u32[]{:S(2)}) copy-start(bf16[256,1024]{1,0:T(8,128)(2,1)} %refs_9_.1) | copy-start | bytes 1572868
  1.3 34.5 %copy-start.1 = (bf16[1024,256]{1,0:T(8,128)(2,1)S(1)}, bf16[1024,256]{1,0:T(8,128)(2,1)}, u32[]{:S(2)}) copy-start(bf16[1024,256]{1,0:T(8,128)(2,1)} %refs_10_.1) | copy-start | bytes 1572868
  1.3 34.5 %copy-start.2 = (bf16[256,256]{1,0:T(8,128)(2,1)S(1)}, bf16[256,256]{1,0:T(8,128)(2,1)}, u32[]{:S(2)}) copy-start(bf16[256,256]{1,0:T(8,128)(2,1)} %cotangent.1) | copy-start | bytes 393220
  1.3 34.5 %copy-start.3 = (bf16[256,256]{1,0:T(8,128)(2,1)S(1)}, bf16[256,256]{1,0:T(8,128)(2,1)}, u32[]{:S(2)}) copy-start(bf16[256,256]{1,0:T(8,128)(2,1)} %refs_5_.1) | copy-start | bytes 393220
  1.4 34.5 %copy-start.4 = (bf16[256,256]{1,0:T(8,128)(2,1)S(1)}, bf16[256,256]{1,0:T(8,128)(2,1)}, u32[]{:S(2)}) copy-start(bf16[256,256]{1,0:T(8,128)(2,1)} %refs_7_.1) | copy-start | bytes 393220
  1.4 34.5 %copy-start.10 = (f32[256]{0:T(256)S(1)}, f32[256]{0:T(256)}, u32[]{:S(2)}) copy-start(f32[256]{0:T(256)} %refs_8_.1) | copy-start | bytes 3076
  6.2 1.7 %collective-permute-start = (f32[2,136,256]{2,1,0:T(8,128)S(1)}, f32[2,136,256]{2,1,0:T(8,128)S(1)}, u32[]{:S(2)}, u32[]{:S(2)}) collective-permute-start(f32[2,136,256]{2,1,0:T(8,128)S(1)} %get-tuple-element.55), channel_id=1, source_target_pairs={{0,1},{1,0},{2,3},{3,2},{4,5},{5,4},{6,7},{7,6},{8,9},{9,8},{10,11... | collective-permute-start | bytes 835592 | tf_op jit(solution)/shard_map/ppermute | solution.py:586
  8.0 6.9 %collective-permute-start.1 = (f32[1,136,256]{2,1,0:T(8,128)S(1)}, f32[1,136,256]{2,1,0:T(8,128)S(1)}, u32[]{:S(2)}, u32[]{:S(2)}) collective-permute-start(f32[1,136,256]{2,1,0:T(8,128)S(1)} %slice_add_fusion.6), channel_id=1, source_target_pairs={{0,2},{1,3},{2,0},{3,1},{4,6},{5,7},{6,4},{7,5},{8,10},{9,11},{10,... | collective-permute-start | bytes 417800 | tf_op jit(solution)/shard_map/ppermute | solution.py:586
  14.9 5.3 %collective-permute-start.2 = (f32[136,256]{1,0:T(8,128)S(1)}, f32[136,256]{1,0:T(8,128)S(1)}, u32[]{:S(2)}, u32[]{:S(2)}) collective-permute-start(f32[136,256]{1,0:T(8,128)S(1)} %fusion.2), channel_id=1, source_target_pairs={{0,4},{1,5},{2,6},{3,7},{4,0},{5,1},{6,2},{7,3},{8,12},{9,13},{10,... | collective-permute-start | bytes 417800 | tf_op jit(solution)/shard_map/ppermute | solution.py:586
  20.2 8.3 %collective-permute-start.3 = (f32[136,256]{1,0:T(8,128)S(1)}, f32[136,256]{1,0:T(8,128)S(1)}, u32[]{:S(2)}, u32[]{:S(2)}) collective-permute-start(f32[136,256]{1,0:T(8,128)S(1)} %add.81), channel_id=1, source_target_pairs={{0,8},{1,9},{2,10},{3,11},{4,12},{5,13},{6,14},{7,15},{8,0},{9,1},... | collective-permute-start | bytes 417800 | tf_op jit(solution)/shard_map/ppermute | solution.py:586
  30.3 4.3 %collective-permute-start.4 = (f32[64,256]{1,0:T(8,128)S(1)}, f32[64,256]{1,0:T(8,128)S(1)}, u32[]{:S(2)}, u32[]{:S(2)}) collective-permute-start(f32[64,256]{1,0:T(8,128)S(1)} %get-tuple-element.56.refs_0_.refs_4_), channel_id=1, source_target_pairs={{0,2},{1,3},{2,0},{3,1},{4,6},{5,7},{6,4},{7,5},{8,10},{9,11},{10,... | collective-permute-start | bytes 196616 | tf_op jit(solution)/shard_map/ppermute | solution.py:586
  31.3 3.2 %collective-permute-start.5 = (f32[64,256]{1,0:T(8,128)S(1)}, f32[64,256]{1,0:T(8,128)S(1)}, u32[]{:S(2)}, u32[]{:S(2)}) collective-permute-start(f32[64,256]{1,0:T(8,128)S(1)} %get-tuple-element.56.refs_0_.refs_4_), channel_id=1, source_target_pairs={{0,1},{1,0},{2,3},{3,2},{4,5},{5,4},{6,7},{7,6},{8,9},{9,8},{10,11... | collective-permute-start | bytes 196616 | tf_op jit(solution)/shard_map/ppermute | solution.py:586
  34.5 1.3 %collective-permute-start.6 = (f32[64,256]{1,0:T(8,128)S(1)}, f32[64,256]{1,0:T(8,128)S(1)}, u32[]{:S(2)}, u32[]{:S(2)}) collective-permute-start(f32[64,256]{1,0:T(8,128)S(1)} %collective-permute-done.4.refs_1_.refs_5_), channel_id=1, source_target_pairs={{0,1},{1,0},{2,3},{3,2},{4,5},{5,4},{6,7},{7,6},{8,9},{9,8},{10,11... | collective-permute-start | bytes 196616 | tf_op jit(solution)/shard_map/ppermute | solution.py:586
  38.7 1.3 %collective-permute-start.7 = (f32[2,64,256]{2,1,0:T(8,128)S(1)}, f32[2,64,256]{2,1,0:T(8,128)S(1)}, u32[]{:S(2)}, u32[]{:S(2)}) collective-permute-start(f32[2,64,256]{2,1,0:T(8,128)S(1)} %get-tuple-element.67), channel_id=1, source_target_pairs={{0,1},{1,0},{2,3},{3,2},{4,5},{5,4},{6,7},{7,6},{8,9},{9,8},{10,11... | collective-permute-start | bytes 393224 | tf_op jit(solution)/shard_map/ppermute | solution.py:586
  40.6 4.7 %collective-permute-start.9 = (f32[8,144,256]{2,1,0:T(8,128)S(1)}, f32[8,144,256]{2,1,0:T(8,128)S(1)}, u32[]{:S(2)}, u32[]{:S(2)}) collective-permute-start(f32[8,144,256]{2,1,0:T(8,128)S(1)} %get-tuple-element.74), channel_id=1, source_target_pairs={{0,1},{1,0},{2,3},{3,2},{4,5},{5,4},{6,7},{7,6},{8,9},{9,8},{10,11... | collective-permute-start | bytes 3538952 | tf_op jit(solution)/shard_map/ppermute | solution.py:586
  40.8 4.4 %collective-permute-start.8 = (f32[1,64,256]{2,1,0:T(8,128)S(1)}, f32[1,64,256]{2,1,0:T(8,128)S(1)}, u32[]{:S(2)}, u32[]{:S(2)}) collective-permute-start(f32[1,64,256]{2,1,0:T(8,128)S(1)} %slice_add_fusion.12), channel_id=1, source_target_pairs={{0,2},{1,3},{2,0},{3,1},{4,6},{5,7},{6,4},{7,5},{8,10},{9,11},{10,... | collective-permute-start | bytes 196616 | tf_op jit(solution)/shard_map/ppermute | solution.py:586
  45.4 14.8 %collective-permute-start.12 = (f32[4,144,256]{2,1,0:T(8,128)S(1)}, f32[4,144,256]{2,1,0:T(8,128)S(1)}, u32[]{:S(2)}, u32[]{:S(2)}) collective-permute-start(f32[4,144,256]{2,1,0:T(8,128)S(1)} %get-tuple-element.101), channel_id=1, source_target_pairs={{0,2},{1,3},{2,0},{3,1},{4,6},{5,7},{6,4},{7,5},{8,10},{9,11},{10,... | collective-permute-start | bytes 1769480 | tf_op jit(solution)/shard_map/ppermute | solution.py:586
  46.5 4.3 %collective-permute-start.10 = (f32[64,256]{1,0:T(8,128)S(1)}, f32[64,256]{1,0:T(8,128)S(1)}, u32[]{:S(2)}, u32[]{:S(2)}) collective-permute-start(f32[64,256]{1,0:T(8,128)S(1)} %add_bitcast_fusion), channel_id=1, source_target_pairs={{0,4},{1,5},{2,6},{3,7},{4,0},{5,1},{6,2},{7,3},{8,12},{9,13},{10,... | collective-permute-start | bytes 196616 | tf_op jit(solution)/shard_map/ppermute | solution.py:586
  50.8 5.9 %collective-permute-start.11 = (f32[64,256]{1,0:T(8,128)S(1)}, f32[64,256]{1,0:T(8,128)S(1)}, u32[]{:S(2)}, u32[]{:S(2)}) collective-permute-start(f32[64,256]{1,0:T(8,128)S(1)} %add.86), channel_id=1, source_target_pairs={{0,8},{1,9},{2,10},{3,11},{4,12},{5,13},{6,14},{7,15},{8,0},{9,1},... | collective-permute-start | bytes 196616 | tf_op jit(solution)/shard_map/ppermute | solution.py:586
  58.6 12.6 %copy-start.8 = (bf16[32,256]{1,0:T(8,128)(2,1)S(1)}, bf16[32,256]{1,0:T(8,128)(2,1)}, u32[]{:S(2)}) copy-start(bf16[32,256]{1,0:T(8,128)(2,1)} %refs_16_.1) | copy-start | bytes 49156
  58.6 12.6 %copy-start.9 = (f32[8]{0:T(128)S(1)}, f32[8]{0:T(128)}, u32[]{:S(2)}) copy-start(f32[8]{0:T(128)} %sharpness.1) | copy-start | bytes 100
  60.3 5.2 %collective-permute-start.13 = (f32[152,256]{1,0:T(8,128)S(1)}, f32[152,256]{1,0:T(8,128)S(1)}, u32[]{:S(2)}, u32[]{:S(2)}) collective-permute-start(f32[152,256]{1,0:T(8,128)S(1)} %mix_back.1.refs_0_), channel_id=1, source_target_pairs={{0,2},{1,3},{2,0},{3,1},{4,6},{5,7},{6,4},{7,5},{8,10},{9,11},{10,... | collective-permute-start | bytes 466952 | tf_op jit(solution)/shard_map/ppermute | solution.py:586
  61.4 7.3 %collective-permute-start.16 = (f32[2,144,256]{2,1,0:T(8,128)S(1)}, f32[2,144,256]{2,1,0:T(8,128)S(1)}, u32[]{:S(2)}, u32[]{:S(2)}) collective-permute-start(f32[2,144,256]{2,1,0:T(8,128)S(1)} %get-tuple-element.103), channel_id=1, source_target_pairs={{0,4},{1,5},{2,6},{3,7},{4,0},{5,1},{6,2},{7,3},{8,12},{9,13},{10,... | collective-permute-start | bytes 884744 | tf_op jit(solution)/shard_map/ppermute | solution.py:586
  62.1 3.4 %collective-permute-start.14 = (f32[152,256]{1,0:T(8,128)S(1)}, f32[152,256]{1,0:T(8,128)S(1)}, u32[]{:S(2)}, u32[]{:S(2)}) collective-permute-start(f32[152,256]{1,0:T(8,128)S(1)} %mix_back.1.refs_0_), channel_id=1, source_target_pairs={{0,1},{1,0},{2,3},{3,2},{4,5},{5,4},{6,7},{7,6},{8,9},{9,8},{10,11... | collective-permute-start | bytes 466952 | tf_op jit(solution)/shard_map/ppermute | solution.py:586
  65.5 3.2 %collective-permute-start.15 = (f32[152,256]{1,0:T(8,128)S(1)}, f32[152,256]{1,0:T(8,128)S(1)}, u32[]{:S(2)}, u32[]{:S(2)}) collective-permute-start(f32[152,256]{1,0:T(8,128)S(1)} %collective-permute-done.13.refs_1_), channel_id=1, source_target_pairs={{0,1},{1,0},{2,3},{3,2},{4,5},{5,4},{6,7},{7,6},{8,9},{9,8},{10,11... | collective-permute-start | bytes 466952 | tf_op jit(solution)/shard_map/ppermute | solution.py:586
  68.7 8.2 %collective-permute-start.17 = (f32[1,144,256]{2,1,0:T(8,128)S(1)}, f32[1,144,256]{2,1,0:T(8,128)S(1)}, u32[]{:S(2)}, u32[]{:S(2)}) collective-permute-start(f32[1,144,256]{2,1,0:T(8,128)S(1)} %slice_add_fusion.5), channel_id=1, source_target_pairs={{0,8},{1,9},{2,10},{3,11},{4,12},{5,13},{6,14},{7,15},{8,0},{9,1},... | collective-permute-start | bytes 442376 | tf_op jit(solution)/shard_map/ppermute | solution.py:586
  76.9 1.6 %collective-permute-start.18 = (f32[288,256]{1,0:T(8,128)S(1)}, f32[288,256]{1,0:T(8,128)S(1)}, u32[]{:S(2)}, u32[]{:S(2)}) collective-permute-start(f32[288,256]{1,0:T(8,128)S(1)} %get-tuple-element.94), channel_id=1, source_target_pairs={{0,1},{1,0},{2,3},{3,2},{4,5},{5,4},{6,7},{7,6},{8,9},{9,8},{10,11... | collective-permute-start | bytes 884744 | tf_op jit(solution)/shard_map/ppermute | solution.py:586
  78.6 6.3 %collective-permute-start.19 = (f32[160,256]{1,0:T(8,128)S(1)}, f32[160,256]{1,0:T(8,128)S(1)}, u32[]{:S(2)}, u32[]{:S(2)}) collective-permute-start(f32[160,256]{1,0:T(8,128)S(1)} %pad_maximum_fusion), channel_id=1, source_target_pairs={{0,2},{1,3},{2,0},{3,1},{4,6},{5,7},{6,4},{7,5},{8,10},{9,11},{10,... | collective-permute-start | bytes 491528 | tf_op jit(solution)/shard_map/ppermute | solution.py:586
  84.9 4.7 %collective-permute-start.20 = (f32[96,256]{1,0:T(8,128)S(1)}, f32[96,256]{1,0:T(8,128)S(1)}, u32[]{:S(2)}, u32[]{:S(2)}) collective-permute-start(f32[96,256]{1,0:T(8,128)S(1)} %pad_maximum_fusion.1), channel_id=1, source_target_pairs={{0,4},{1,5},{2,6},{3,7},{4,0},{5,1},{6,2},{7,3},{8,12},{9,13},{10,... | collective-permute-start | bytes 294920 | tf_op jit(solution)/shard_map/ppermute | solution.py:586
  89.6 5.2 %collective-permute-start.21 = (f32[64,256]{1,0:T(8,128)S(1)}, f32[64,256]{1,0:T(8,128)S(1)}, u32[]{:S(2)}, u32[]{:S(2)}) collective-permute-start(f32[64,256]{1,0:T(8,128)S(1)} %pad_maximum_fusion.2), channel_id=1, source_target_pairs={{0,8},{1,9},{2,10},{3,11},{4,12},{5,13},{6,14},{7,15},{8,0},{9,1},... | collective-permute-start | bytes 196616 | tf_op jit(solution)/shard_map/ppermute | solution.py:586

commit v4 on v3

--- a/solution.py
+++ b/solution.py
@@ -30,6 +30,13 @@
     out = 0
     for k in range(bits):
         out = (out << 1) | ((value >> k) & 1)
+    return out
+
+
+def from_position(pos, order):
+    out = 0
+    for i, bit in enumerate(order):
+        out |= ((pos >> (len(order) - 1 - i)) & 1) << bit
     return out
 
 
@@ -109,12 +116,12 @@
         pltpu.make_async_copy(source, target, sems.at[i])
         for i, (source, target) in enumerate(
             (
-                (w_slice_hbm, w_slice),
+                (points_hbm, points),
+                (geometry_hbm, geometry),
                 (w_feat_hbm, w_feat),
                 (w_mid_hbm, w_mid),
                 (gain_hbm, gain),
-                (points_hbm, points),
-                (geometry_hbm, geometry),
+                (w_slice_hbm, w_slice),
                 (sharpness_hbm, sharpness),
                 (counts_hbm, counts),
             )
@@ -132,14 +139,12 @@
     lanes = math.gcd(rows, 128)
     filled = 2 * per * (width + 1)
     total[:, filled:, :] = jnp.zeros((groups, total.shape[1] - filled, slices), F32)
-    for copy in copies[:4]:
+    for copy in copies:
         copy.wait()
     slice_t = w_slice[...].T
     maps[:model, :] = w_feat[...].T
     maps[model:, :] = w_mid[...].T
     gain_column = jnp.broadcast_to(gain[...].reshape(1, model), (8, model)).T[:, :1]
-    for copy in copies[4:]:
-        copy.wait()
     live = lax.broadcasted_iota(jnp.int32, (1, rows), 1) < counts[0]
     blocks = range(0, all_rows, rows)
     for start in blocks:
@@ -217,22 +222,27 @@
     per = attention_out.shape[0]
     slices = tokens.shape[1]
     maps = jnp.concatenate([w_query[...], w_key[...], w_value[...]], axis=1)
-    for j in range(per):
-        (field, _), (geo, _) = token_rows(tokens, j, per, width)
-        both = jnp.concatenate([field, geo], axis=1)
-        projected = narrow_dot(maps, both)
-        kept[j] = projected
-        query = projected[:width, :slices]
-        keys = projected[width : 2 * width]
-        values = projected[2 * width :]
-        scores = narrow_dot(keys, query)
-        scores = (scores - jnp.max(scores, axis=0, keepdims=True)) * (
+    heads = range(per)
+    both = [
+        jnp.concatenate([part for part, _ in token_rows(tokens, j, per, width)], axis=1)
+        for j in heads
+    ]
+    projected = [narrow_dot(maps, both[j]) for j in heads]
+    for j in heads:
+        kept[j] = projected[j]
+    scores = [narrow_dot(projected[j][width : 2 * width], projected[j][:width, :slices]) for j in heads]
+    attention = []
+    for j in heads:
+        scaled = (scores[j] - jnp.max(scores[j], axis=0, keepdims=True)) * (
             math.log2(math.e) / math.sqrt(width)
         )
-        powers = jnp.exp2(scores)
-        attention = powers * (1.0 / jnp.sum(powers, axis=0, keepdims=True))
-        attention_out[j] = attention
-        mixed_out[j * width : (j + 1) * width, :] = wide_dot(values, split(attention), NN)
+        powers = jnp.exp2(scaled)
+        attention.append(powers * (1.0 / jnp.sum(powers, axis=0, keepdims=True)))
+    for j in heads:
+        attention_out[j] = attention[j]
+        mixed_out[j * width : (j + 1) * width, :] = wide_dot(
+            projected[j][2 * width :], split(attention[j]), NN
+        )
 
 
 def mix_back_kernel(tokens, attention_in, kept, grad, w_query, w_key, w_value, out):
@@ -243,32 +253,31 @@
     out[base : base + pad_to(2 * per, 8), :] = jnp.zeros((pad_to(2 * per, 8), slices), F32)
     maps_t = jnp.concatenate([w_query[...].T, w_key[...].T, w_value[...].T], axis=0)
     none = jnp.zeros((width, both_count - slices), F32)
-    for j in range(per):
-        (field, field_den), (geo, geo_den) = token_rows(tokens, j, per, width)
-        both = jnp.concatenate([field, geo], axis=1)
-        query = kept[j, :width, :slices]
-        keys = kept[j, width : 2 * width, :]
-        values = kept[j, 2 * width :, :]
+    heads = range(per)
+    rows = [token_rows(tokens, j, per, width) for j in heads]
+    both = [jnp.concatenate([part for part, _ in rows[j]], axis=1) for j in heads]
+    mixed_grads = [grad[j * width : (j + 1) * width, :] for j in heads]
+    att_grads = [narrow_dot(kept[j, 2 * width :, :], mixed_grads[j]) for j in heads]
+    value_grads = [wide_dot(mixed_grads[j], split(attention_in[j]), NT) for j in heads]
+    score_grads = []
+    for j in heads:
         attention = attention_in[j]
-        mixed_grad = grad[j * width : (j + 1) * width, :]
-        att_grad = narrow_dot(values, mixed_grad)
-        inner = jnp.sum(attention * att_grad, axis=0, keepdims=True)
-        score_grad = split(attention * (att_grad - inner) * (1.0 / math.sqrt(width)))
-        value_grad = wide_dot(mixed_grad, split(attention), NT)
-        query_grad = wide_dot(keys, score_grad, NN)
-        key_grad = wide_dot(query, score_grad, NT)
-        grads = jnp.concatenate(
-            [jnp.concatenate([query_grad, none], axis=1), key_grad, value_grad], axis=0
+        inner = jnp.sum(attention * att_grads[j], axis=0, keepdims=True)
+        score_grads.append(split(attention * (att_grads[j] - inner) * (1.0 / math.sqrt(width))))
+    query_grads = [wide_dot(kept[j, width : 2 * width, :], score_grads[j], NN) for j in heads]
+    key_grads = [wide_dot(kept[j, :width, :slices], score_grads[j], NT) for j in heads]
+    grads = [
+        jnp.concatenate(
+            [jnp.concatenate([query_grads[j], none], axis=1), key_grads[j], value_grads[j]], axis=0
         )
-        both_grad = narrow_dot(maps_t, grads)
-        field_grad = both_grad[:, :slices]
-        geo_grad = both_grad[:, slices:]
-        small += wide_dot(both, split(grads), NT)
-        for g, (value, den, value_of) in enumerate(
-            ((field_grad, field_den, field), (geo_grad, geo_den, geo))
-        ):
+        for j in heads
+    ]
+    both_grads = [narrow_dot(maps_t, grads[j]) for j in heads]
+    for j in heads:
+        small += wide_dot(both[j], split(grads[j]), NT)
+        for g, (value_of, den) in enumerate(rows[j]):
             row = (g * per + j) * width
-            scaled = value / den
+            scaled = both_grads[j][:, g * slices : (g + 1) * slices] / den
             out[row : row + width, :] = scaled
             out[base + g * per + j : base + g * per + j + 1, :] = -jnp.sum(
                 scaled * value_of, axis=0, keepdims=True
@@ -356,12 +365,11 @@
 
 
 def outer_kernel(
-    attended, second, hidden, grad_upper, grad_resid, cotangent, keep, send, out, up, down
+    order, attended, second, hidden, grad_upper, grad_resid, cotangent, keep, send, out, up, down
 ):
     me = lax.axis_index("pts")
     half, rows, model = keep.shape
     parts = 2 * half
-    bits = parts.bit_length() - 1
     step = model // parts
     wide = hidden.shape[1] // model
     out[...] = dot(attended[...], grad_resid[...])
@@ -369,7 +377,7 @@
     down[...] = dot(hidden[...], cotangent[...], TN)
     for pos in range(parts):
         target = keep if pos < half else send
-        p = bit_reverse(pos, bits) ^ me
+        p = from_position(pos, order) ^ me
         i = pos % half
         at = pl.ds(pl.multiple_of(p * step, step), step)
         target[i, :step, :] = out[at, :]
@@ -379,7 +387,7 @@
         target[i, step * (1 + wide) :, :] = down[pl.ds(pl.multiple_of(p * tall, tall), tall), :]
 
 
-def back_kernel(rel, sharpness, *refs):
+def back_kernel(rel, order, sharpness, *refs):
     groups = len(rel)
     pieces = refs[:groups]
     mixed = refs[groups : 2 * groups]
@@ -491,9 +499,8 @@
     total[...] = dot(normed[...], right[...], NT)
     half = keep.shape[0] // 2
     step = model // (2 * half)
-    bits = (2 * half).bit_length() - 1
     for pos in range(2 * half):
-        start = pl.multiple_of((bit_reverse(pos, bits) ^ me) * step, step)
+        start = pl.multiple_of((from_position(pos, order) ^ me) * step, step)
         value = total[pl.ds(start, step), :]
         if pos < half:
             keep[2 * pos] = value[:, :model]
@@ -520,10 +527,27 @@
     slice_out[...] = slice_sum[...] + got[2 * step :, :]
 
 
+def fold_kernel(value, got, keep, send):
+    count = keep.shape[0]
+    keep[...] = value[:count] + got[:count]
+    send[...] = value[count:] + got[count:]
+
+
+def outer_finish_kernel(keep, got, out, up, down):
+    step, model = out.shape
+    wide = up.shape[1] // model
+    out[...] = keep[0, :step, :] + got[0, :step, :]
+    for w in range(wide):
+        at = slice(step * (1 + w), step * (2 + w))
+        up[:, w * model : (w + 1) * model] = keep[0, at, :] + got[0, at, :]
+    down[...] = keep[0, step * (1 + wide) :, :] + got[0, step * (1 + wide) :, :]
+
+
 VMEM = pl.BlockSpec(memory_space=pltpu.VMEM)
 SMEM = pl.BlockSpec(memory_space=pltpu.SMEM)
 HBM = pl.BlockSpec(memory_space=pltpu.HBM)
 MIB = 1024 * 1024
+COSTS = {"point_back": 0.001, "mix_back": 0.001, "fold": 8.0}
 
 
 def shape(dims, dtype=F32):
@@ -531,6 +555,11 @@
 
 
 def run(body, name, limit, first, out_shape, scratch, *args):
+    estimate = None
+    if name in COSTS:
+        estimate = pl.CostEstimate(
+            flops=int(COSTS[name] * 1e9), bytes_accessed=0, transcendentals=0
+        )
     rest = HBM if first is HBM else VMEM
     if first is HBM:
         args = args[:1] + tuple(
@@ -544,6 +573,7 @@
         scratch_shapes=scratch,
         compiler_params=pltpu.CompilerParams(vmem_limit_bytes=limit * MIB),
         name=name,
+        cost_estimate=estimate,
     )(*args)
 
 
@@ -599,6 +629,7 @@
             pieces = pieces + [exchange(piece, bit) for piece in pieces]
         return pieces
 
+    main_order = outer_order = (0, 2, 1) + tuple(range(3, all_bits))
     rel = [0]
     for bit in reversed(range(bits)):
         rel = rel + [r ^ (1 << bit) for r in rel]
@@ -704,7 +735,7 @@
         (attended, second, hidden, grad_upper, grad_resid, got)
     )
     outer_keep, outer_send = run(
-        outer_kernel,
+        functools.partial(outer_kernel, outer_order),
         "weight_grads",
         16,
         VMEM,
@@ -725,10 +756,10 @@
         keep, send = fold(keep, got)
         got = exchange(send, bit)
     outer_got = exchange(outer_send, 0)
-    mixed_grad, outer_got = tie(((keep + got)[0], outer_got))
+    mixed_grad = add_all((keep + got)[0], bits, all_bits)
+    mixed_grad, outer_got = tie((mixed_grad, outer_got))
     outer_keep, outer_send = fold(outer_keep, outer_got)
-    outer_got = exchange(outer_send, 1)
-    mixed_grad = add_all(mixed_grad, bits, all_bits)
+    outer_got = exchange(outer_send, outer_order[1])
     token_grad = run(
         mix_back_kernel,
         "mix_back",
@@ -744,15 +775,9 @@
         w_key,
         w_value,
     )
-    token_grad, outer_got = tie((token_grad, outer_got))
-    outer_keep, outer_send = fold(outer_keep, outer_got)
-    outer_got = exchange(outer_send, 2)
     grad_pieces = collect([token_grad], 0, bits)
-    grad_pieces, outer_got = tie((grad_pieces, outer_got))
-    outer_keep, outer_send = fold(outer_keep, outer_got)
-    outer_got = exchange(outer_send, 3)
     keep, send, grad_mix = run(
-        functools.partial(back_kernel, tuple(rel)),
+        functools.partial(back_kernel, tuple(rel), main_order),
         "point_back",
         24,
         SMEM,
@@ -787,14 +812,28 @@
     )
     keep = keep.reshape(-1, model)
     slice_sum = send[keep.shape[0] :]
-    for bit in range(all_bits):
-        if bit < all_bits - 3:
+    for turn, bit in enumerate(main_order):
+        if turn == 0:
             send, outer_got = tie((send, outer_got))
-        if bit < all_bits - 4:
             outer_keep, outer_send = fold(outer_keep, outer_got)
-            outer_got = exchange(outer_send, bit + 4)
+            outer_got = exchange(outer_send, outer_order[2])
+            send, outer_keep = tie((send, outer_keep))
+        if turn == 2:
+            count = outer_keep.shape[0] // 2
+            outer_keep, outer_send = run(
+                fold_kernel,
+                "fold",
+                4,
+                VMEM,
+                (shape((count,) + outer_keep.shape[1:]),) * 2,
+                [],
+                outer_keep,
+                outer_got,
+            )
+            send, outer_keep = tie((send, outer_keep))
+            outer_got = exchange(outer_send, outer_order[3])
         got = exchange(send, bit)
-        if bit == all_bits - 1:
+        if turn == all_bits - 1:
             break
         slice_sum = slice_sum + got[keep.shape[0] :]
         count = keep.shape[0] // 2
@@ -811,12 +850,19 @@
         got,
         slice_sum,
     )
-    outer = (outer_keep + outer_got)[0]
-    grad_out = outer[:step]
-    grad_up = jnp.concatenate(
-        [outer[step * (1 + w) : step * (2 + w)] for w in range(wide)], axis=1
-    )
-    grad_down = outer[step * (1 + wide) :]
+    for bit in outer_order[4:]:
+        outer_keep, outer_send = fold(outer_keep, outer_got)
+        outer_got = exchange(outer_send, bit)
+    grad_out, grad_up, grad_down = run(
+        outer_finish_kernel,
+        "outer_finish",
+        4,
+        VMEM,
+        (shape((step, model)), shape((step, hidden_width)), shape((step * wide, model))),
+        [],
+        outer_keep,
+        outer_got,
+    )
     return (layer_out, grad_feat, grad_mid, grad_out, grad_up, grad_down, grad_slice, grad_mix)
 
 

time: 95.7 us -> 93 us (0.972)
  waiting for transfers between devices: 51.6 us -> 47.9 us
  starting transfers between devices: 22.2 us -> 25.4 us
  local copies, waits for them, and re-layouts: 1.31 us -> 0.07 us
    ppermute x22, waiting for transfers between devices: 51.6 us -> 47.9 us  [exchange(): return lax.ppermute(value, 'pts', [(i, i ^ 1 << bit) for i in range(parts)])]
    ppermute x22, starting transfers between devices: 22.2 us -> 25.4 us  [exchange(): return lax.ppermute(value, 'pts', [(i, i ^ 1 << bit) for i in range(parts)])]
    slice x2 -> x0, local copies, waits for them, and re-layouts: 1.24 us -> none  [the longest x1 0.63 us: on_device(): grad_down = outer[step * (1 + wide):]]
    pallas_call x7 -> x9, Pallas kernels: 17.6 us -> 17.4 us  [run(): pl.pallas_call(body, out_shape=out_shape, in_specs=[first] + [rest] * (le...]
  transfers between devices with their start and end apart: 22 -> 22, of which waited for: 18 -> 15; matrix products, arithmetic and copies ran while one was open for 2% -> 0% of each run, Pallas kernels for 7% -> 8%
where the time goes in v4:
time: 93 us; the launch traced here: 92.8 us
  waiting for transfers between devices  47.9 us (52%)
  starting transfers between devices  25.4 us (27%)
  Pallas kernels  17.4 us (19%)
  between operations  1.57 us (2%)
    ppermute x22, waiting for transfers between devices, exchange(): return lax.ppermute(value, 'pts', [(i, i ^ 1 << bit) for i in range(parts)])  47.9 us
    ppermute x22, starting transfers between devices, exchange(): return lax.ppermute(value, 'pts', [(i, i ^ 1 << bit) for i in range(parts)])  25.4 us
    pallas_call x9, Pallas kernels, run(): pl.pallas_call(body, out_shape=out_shape, in_specs=[first] + [rest] * (le...  17.4 us
  transfers between devices with their start and end apart: 22, of which 15 were waited for; matrix products, arithmetic and copies ran while one was open for 0% of the time, Pallas kernels for 8%

profile of v4, /device:TPU:0, one launch (start us, length us, event | category | flops | bytes accessed | tf_op | source)
XLA Modules:
  0.0 92.8 jit_solution(967660750709986616)
XLA Ops:
  1.3 0.0 copy-start.5
  1.3 0.0 copy-start.6
  1.3 0.0 copy-start.7
  1.3 0.0 copy-start
  1.4 4.8 %slice_sums.1 = (f32[2,136,256]{2,1,0:T(8,128)S(1)}, f32[2,136,256]{2,1,0:T(8,128)S(1)}, bf16[256,768]{1,0:T(8,128)(2,1)S(1)}, bf16[256,768]{1,0:T(8,128)(2,1)S(...) custom-call(s32[1]{0:T(128)S(6)} %copy.24.counts_hbm, ...), custom_call_target="tpu_custom_call" | custom-call | tf_op jit(solution)/shard_map/slice_sums/pallas_call | solution.py:568
  6.2 0.5 collective-permute-start
  6.7 1.2 %collective-permute-done = f32[2,136,256]{2,1,0:T(8,128)S(1)} collective-permute-done((f32[2,136,256]{2,1,0:T(8,128)S(1)}, f32[2,136,256]{2,1,0:T(8,128)S(1)}, u32[]{:S(2)}, u32[]{:S(2)}) %collective-permute-start) | collective-permute-done | bytes 278560 | tf_op jit(solution)/shard_map/ppermute | solution.py:616
  7.9 3.0 %collective-permute-start.1 = (f32[1,136,256]{2,1,0:T(8,128)S(1)}, f32[1,136,256]{2,1,0:T(8,128)S(1)}, u32[]{:S(2)}, u32[]{:S(2)}) collective-permute-start(f32[1,136,256]{2,1,0:T(8,128)S(1)} %slice_add_fusion.4), channel_id=1, source_target_pairs={{0,2},{1,3},{2,0},{3,1},{4,6},{5,7},{6,4},{7,5},{8,10},{9,11},{10,... | collective-permute-start | bytes 417800 | tf_op jit(solution)/shard_map/ppermute | solution.py:616
  10.9 4.0 %collective-permute-done.1 = f32[1,136,256]{2,1,0:T(8,128)S(1)} collective-permute-done((f32[1,136,256]{2,1,0:T(8,128)S(1)}, f32[1,136,256]{2,1,0:T(8,128)S(1)}, u32[]{:S(2)}, u32[]{:S(2)}) %collective-permute-start.1) | collective-permute-done | bytes 139296 | tf_op jit(solution)/shard_map/ppermute | solution.py:616
  14.9 1.9 %collective-permute-start.2 = (f32[136,256]{1,0:T(8,128)S(1)}, f32[136,256]{1,0:T(8,128)S(1)}, u32[]{:S(2)}, u32[]{:S(2)}) collective-permute-start(f32[136,256]{1,0:T(8,128)S(1)} %fusion.1), channel_id=1, source_target_pairs={{0,4},{1,5},{2,6},{3,7},{4,0},{5,1},{6,2},{7,3},{8,12},{9,13},{10,... | collective-permute-start | bytes 417800 | tf_op jit(solution)/shard_map/ppermute | solution.py:616
  16.7 3.4 %collective-permute-done.2 = f32[136,256]{1,0:T(8,128)S(1)} collective-permute-done((f32[136,256]{1,0:T(8,128)S(1)}, f32[136,256]{1,0:T(8,128)S(1)}, u32[]{:S(2)}, u32[]{:S(2)}) %collective-permute-start.2) | collective-permute-done | bytes 139296 | tf_op jit(solution)/shard_map/ppermute | solution.py:616
  20.2 2.7 %collective-permute-start.3 = (f32[136,256]{1,0:T(8,128)S(1)}, f32[136,256]{1,0:T(8,128)S(1)}, u32[]{:S(2)}, u32[]{:S(2)}) collective-permute-start(f32[136,256]{1,0:T(8,128)S(1)} %add.72), channel_id=1, source_target_pairs={{0,8},{1,9},{2,10},{3,11},{4,12},{5,13},{6,14},{7,15},{8,0},{9,1},... | collective-permute-start | bytes 417800 | tf_op jit(solution)/shard_map/ppermute | solution.py:616
  22.9 5.5 %collective-permute-done.3 = f32[136,256]{1,0:T(8,128)S(1)} collective-permute-done((f32[136,256]{1,0:T(8,128)S(1)}, f32[136,256]{1,0:T(8,128)S(1)}, u32[]{:S(2)}, u32[]{:S(2)}) %collective-permute-start.3) | collective-permute-done | bytes 139296 | tf_op jit(solution)/shard_map/ppermute | solution.py:616
  28.4 0.0 copy-done.5
  28.5 0.0 copy-done.6
  28.5 0.0 copy-done.7
  28.5 1.1 %mix_tokens.1 = (f32[64,256]{1,0:T(8,128)S(1)}, f32[2,512,256]{2,1,0:T(8,128)S(1)}, f32[2,96,512]{2,1,0:T(8,128)S(1)}) custom-call(f32[136,256]{1,0:T(8,128)S(1)} %add.73.tokens, f32[32,32]{1,0:T(8,128)S(1)} %copy-done.5, f32[32,32]{1,0:T(8,128)S(1)} %copy-done.6, f32[32,32]{1,0:T(8,128)S(1)} %copy-done.7), custom_call_target="tpu_custom_call" | custom-call | tf_op jit(solution)/shard_map/mix_tokens/pallas_call | solution.py:568
  29.6 1.0 %collective-permute-start.4 = (f32[64,256]{1,0:T(8,128)S(1)}, f32[64,256]{1,0:T(8,128)S(1)}, u32[]{:S(2)}, u32[]{:S(2)}) collective-permute-start(f32[64,256]{1,0:T(8,128)S(1)} %get-tuple-element.58.refs_0_.refs_4_), channel_id=1, source_target_pairs={{0,2},{1,3},{2,0},{3,1},{4,6},{5,7},{6,4},{7,5},{8,10},{9,11},{10,... | collective-permute-start | bytes 196616 | tf_op jit(solution)/shard_map/ppermute | solution.py:616
  30.7 0.0 collective-permute-start.5
  30.7 3.2 %collective-permute-done.4.refs_1_.refs_5_ = f32[64,256]{1,0:T(8,128)S(1)} collective-permute-done((f32[64,256]{1,0:T(8,128)S(1)}, f32[64,256]{1,0:T(8,128)S(1)}, u32[]{:S(2)}, u32[]{:S(2)}) %collective-permute-start.4) | collective-permute-done | bytes 65568 | tf_op jit(solution)/shard_map/ppermute | solution.py:616
  33.9 0.0 collective-permute-start.6
  33.9 0.0 collective-permute-done.5.refs_2_.refs_6_
  33.9 1.2 %collective-permute-done.6.refs_3_.refs_7_ = f32[64,256]{1,0:T(8,128)S(1)} collective-permute-done((f32[64,256]{1,0:T(8,128)S(1)}, f32[64,256]{1,0:T(8,128)S(1)}, u32[]{:S(2)}, u32[]{:S(2)}) %collective-permute-start.6) | collective-permute-done | bytes 65568 | tf_op jit(solution)/shard_map/ppermute | solution.py:616
  35.2 0.0 copy-done.1
  35.2 2.8 %mlp.1 = (bf16[256,256]{1,0:T(8,128)(2,1)}, bf16[256,256]{1,0:T(8,128)(2,1)S(1)}, f32[2,64,256]{2,1,0:T(8,128)S(1)}, f32[2,64,256]{2,1,0:T(8,128)S(1)}, bf16[256...) custom-call(f32[64,256]{1,0:T(8,128)S(1)} %get-tuple-element.58.refs, ...), custom_call_target="tpu_custom_call" | custom-call | tf_op jit(solution)/shard_map/mlp/pallas_call | solution.py:568
  38.0 0.1 collective-permute-start.7
  38.2 1.2 %collective-permute-done.7 = f32[2,64,256]{2,1,0:T(8,128)S(1)} collective-permute-done((f32[2,64,256]{2,1,0:T(8,128)S(1)}, f32[2,64,256]{2,1,0:T(8,128)S(1)}, u32[]{:S(2)}, u32[]{:S(2)}) %collective-permute-start.7) | collective-permute-done | bytes 131104 | tf_op jit(solution)/shard_map/ppermute | solution.py:616
  39.4 0.6 weight_grads.1
  39.9 0.2 collective-permute-start.11
  40.2 1.1 %collective-permute-start.8 = (f32[1,64,256]{2,1,0:T(8,128)S(1)}, f32[1,64,256]{2,1,0:T(8,128)S(1)}, u32[]{:S(2)}, u32[]{:S(2)}) collective-permute-start(f32[1,64,256]{2,1,0:T(8,128)S(1)} %slice_add_fusion.10), channel_id=1, source_target_pairs={{0,2},{1,3},{2,0},{3,1},{4,6},{5,7},{6,4},{7,5},{8,10},{9,11},{10,... | collective-permute-start | bytes 196616 | tf_op jit(solution)/shard_map/ppermute | solution.py:616
  41.3 3.3 %collective-permute-done.8 = f32[1,64,256]{2,1,0:T(8,128)S(1)} collective-permute-done((f32[1,64,256]{2,1,0:T(8,128)S(1)}, f32[1,64,256]{2,1,0:T(8,128)S(1)}, u32[]{:S(2)}, u32[]{:S(2)}) %collective-permute-start.8) | collective-permute-done | bytes 65568 | tf_op jit(solution)/shard_map/ppermute | solution.py:616
  44.6 0.2 collective-permute-start.9
  44.9 4.1 %collective-permute-done.9 = f32[64,256]{1,0:T(8,128)S(1)} collective-permute-done((f32[64,256]{1,0:T(8,128)S(1)}, f32[64,256]{1,0:T(8,128)S(1)}, u32[]{:S(2)}, u32[]{:S(2)}) %collective-permute-start.9) | collective-permute-done | bytes 65568 | tf_op jit(solution)/shard_map/ppermute | solution.py:616
  49.0 1.6 %collective-permute-start.10 = (f32[64,256]{1,0:T(8,128)S(1)}, f32[64,256]{1,0:T(8,128)S(1)}, u32[]{:S(2)}, u32[]{:S(2)}) collective-permute-start(f32[64,256]{1,0:T(8,128)S(1)} %add.77), channel_id=1, source_target_pairs={{0,8},{1,9},{2,10},{3,11},{4,12},{5,13},{6,14},{7,15},{8,0},{9,1},... | collective-permute-start | bytes 196616 | tf_op jit(solution)/shard_map/ppermute | solution.py:616
  50.6 4.3 %collective-permute-done.10 = f32[64,256]{1,0:T(8,128)S(1)} collective-permute-done((f32[64,256]{1,0:T(8,128)S(1)}, f32[64,256]{1,0:T(8,128)S(1)}, u32[]{:S(2)}, u32[]{:S(2)}) %collective-permute-start.10) | collective-permute-done | bytes 65568 | tf_op jit(solution)/shard_map/ppermute | solution.py:616
  54.9 0.0 collective-permute-done.11
  54.9 0.2 slice_add_fusion
  55.1 0.0 copy-start.8
  55.1 0.0 copy-start.9
  55.1 0.1 collective-permute-start.15
  55.2 1.5 %mix_back.1.refs_0_ = f32[152,256]{1,0:T(8,128)S(1)} custom-call(f32[136,256]{1,0:T(8,128)S(1)} %add.73.tokens, f32[2,512,256]{2,1,0:T(8,128)S(1)} %get-tuple-element.61.attention_in, f32[2,96,512]{2,1,0:T(8,128)S(1)} %get-tuple-element.62.kept, f32[64,256]{1,0:T(8,128)S(1)} %add.78.grad, f32[32,32]{1,0:T(8,128)S(1)} %copy-done.5, f32[32,32]{1,0:T(8,128)S(1)} %copy-done.6, ...), custom_call_target="tpu_custom_call" | custom-call | flops 1000000 | tf_op jit(solution)/shard_map/mix_back/pallas_call | solution.py:568
  56.7 1.6 %collective-permute-start.12 = (f32[152,256]{1,0:T(8,128)S(1)}, f32[152,256]{1,0:T(8,128)S(1)}, u32[]{:S(2)}, u32[]{:S(2)}) collective-permute-start(f32[152,256]{1,0:T(8,128)S(1)} %mix_back.1.refs_0_), channel_id=1, source_target_pairs={{0,2},{1,3},{2,0},{3,1},{4,6},{5,7},{6,4},{7,5},{8,10},{9,11},{10,... | collective-permute-start | bytes 466952 | tf_op jit(solution)/shard_map/ppermute | solution.py:616
  58.3 0.0 collective-permute-start.13
  58.3 3.7 %collective-permute-done.12.refs_1_ = f32[152,256]{1,0:T(8,128)S(1)} collective-permute-done((f32[152,256]{1,0:T(8,128)S(1)}, f32[152,256]{1,0:T(8,128)S(1)}, u32[]{:S(2)}, u32[]{:S(2)}) %collective-permute-start.12) | collective-permute-done | bytes 155680 | tf_op jit(solution)/shard_map/ppermute | solution.py:616
  62.0 0.0 collective-permute-start.14
  62.0 0.0 collective-permute-done.13.refs_2_
  62.0 1.4 %collective-permute-done.14.refs_3_ = f32[152,256]{1,0:T(8,128)S(1)} collective-permute-done((f32[152,256]{1,0:T(8,128)S(1)}, f32[152,256]{1,0:T(8,128)S(1)}, u32[]{:S(2)}, u32[]{:S(2)}) %collective-permute-start.14) | collective-permute-done | bytes 155680 | tf_op jit(solution)/shard_map/ppermute | solution.py:616
  63.4 5.2 %point_back.1 = (f32[16,16,256]{2,1,0:T(8,128)S(1)}, f32[288,256]{1,0:T(8,128)S(1)}, f32[3,32,32]{2,1,0:T(8,128)}) custom-call(f32[8]{0:T(128)S(1)} %copy-done.9, f32[152,256]{1,0:T(8,128)S(1)} %mix_back.1.refs_0_, f32[152,256]{1,0:T(8,128)S(1)} %collective-permute-done.12.refs_1_, f32[152,256]{1,0:T(8,128)S(1)} %collective-permute-done.13.refs_2_, ...), custom_call_target="tpu_custom_call" | custom-call | flops 1000000 | tf_op jit(solution)/shard_map/point_back/pallas_call | solution.py:568
  68.6 0.0 collective-permute-done.15
  68.6 0.1 slice_add_fusion.2
  68.7 0.2 collective-permute-start.16
  69.0 1.6 %collective-permute-start.18 = (f32[2,144,256]{2,1,0:T(8,128)S(1)}, f32[2,144,256]{2,1,0:T(8,128)S(1)}, u32[]{:S(2)}, u32[]{:S(2)}) collective-permute-start(f32[2,144,256]{2,1,0:T(8,128)S(1)} %get-tuple-element.106), channel_id=1, source_target_pairs={{0,2},{1,3},{2,0},{3,1},{4,6},{5,7},{6,4},{7,5},{8,10},{9,11},{10,... | collective-permute-start | bytes 884744 | tf_op jit(solution)/shard_map/ppermute | solution.py:616
  70.5 0.0 collective-permute-done.16
  70.6 1.9 %collective-permute-start.17 = (f32[160,256]{1,0:T(8,128)S(1)}, f32[160,256]{1,0:T(8,128)S(1)}, u32[]{:S(2)}, u32[]{:S(2)}) collective-permute-start(f32[160,256]{1,0:T(8,128)S(1)} %pad_maximum_fusion), channel_id=1, source_target_pairs={{0,4},{1,5},{2,6},{3,7},{4,0},{5,1},{6,2},{7,3},{8,12},{9,13},{10,... | collective-permute-start | bytes 491528 | tf_op jit(solution)/shard_map/ppermute | solution.py:616
  72.5 5.8 %collective-permute-done.18.got = f32[2,144,256]{2,1,0:T(8,128)S(1)} collective-permute-done((f32[2,144,256]{2,1,0:T(8,128)S(1)}, f32[2,144,256]{2,1,0:T(8,128)S(1)}, u32[]{:S(2)}, u32[]{:S(2)}) %collective-permute-start.18) | collective-permute-done | bytes 294944 | tf_op jit(solution)/shard_map/ppermute | solution.py:616
  78.3 0.0 collective-permute-done.17
  78.4 1.6 %collective-permute-start.19 = (f32[96,256]{1,0:T(8,128)S(1)}, f32[96,256]{1,0:T(8,128)S(1)}, u32[]{:S(2)}, u32[]{:S(2)}) collective-permute-start(f32[96,256]{1,0:T(8,128)S(1)} %pad_maximum_fusion.1), channel_id=1, source_target_pairs={{0,2},{1,3},{2,0},{3,1},{4,6},{5,7},{6,4},{7,5},{8,10},{9,11},{10,... | collective-permute-start | bytes 294920 | tf_op jit(solution)/shard_map/ppermute | solution.py:616
  80.0 3.0 %collective-permute-start.21 = (f32[1,144,256]{2,1,0:T(8,128)S(1)}, f32[1,144,256]{2,1,0:T(8,128)S(1)}, u32[]{:S(2)}, u32[]{:S(2)}) collective-permute-start(f32[1,144,256]{2,1,0:T(8,128)S(1)} %get-tuple-element.98), channel_id=1, source_target_pairs={{0,8},{1,9},{2,10},{3,11},{4,12},{5,13},{6,14},{7,15},{8,0},{9,1},... | collective-permute-start | bytes 442376 | tf_op jit(solution)/shard_map/ppermute | solution.py:616
  82.9 0.1 collective-permute-done.19
  83.1 3.0 %collective-permute-start.20 = (f32[64,256]{1,0:T(8,128)S(1)}, f32[64,256]{1,0:T(8,128)S(1)}, u32[]{:S(2)}, u32[]{:S(2)}) collective-permute-start(f32[64,256]{1,0:T(8,128)S(1)} %pad_maximum_fusion.2), channel_id=1, source_target_pairs={{0,8},{1,9},{2,10},{3,11},{4,12},{5,13},{6,14},{7,15},{8,0},{9,1},... | collective-permute-start | bytes 196616 | tf_op jit(solution)/shard_map/ppermute | solution.py:616
  86.1 5.4 %collective-permute-done.21.got = f32[1,144,256]{2,1,0:T(8,128)S(1)} collective-permute-done((f32[1,144,256]{2,1,0:T(8,128)S(1)}, f32[1,144,256]{2,1,0:T(8,128)S(1)}, u32[]{:S(2)}, u32[]{:S(2)}) %collective-permute-start.21) | collective-permute-done | bytes 147488 | tf_op jit(solution)/shard_map/ppermute | solution.py:616
  91.5 0.7 outer_finish.1
  92.2 0.0 collective-permute-done.20.got
  92.2 0.6 finish.1
  (30 shorter events, 0.3 us)
Async XLA Ops:
  1.3 27.2 %copy-start.5 = (f32[32,32]{1,0:T(8,128)S(1)}, f32[32,32]{1,0:T(8,128)}, u32[]{:S(2)}) copy-start(f32[32,32]{1,0:T(8,128)} %w_query.3) | copy-start | bytes 12292
  1.3 27.2 %copy-start.6 = (f32[32,32]{1,0:T(8,128)S(1)}, f32[32,32]{1,0:T(8,128)}, u32[]{:S(2)}) copy-start(f32[32,32]{1,0:T(8,128)} %w_key.3) | copy-start | bytes 12292
  1.3 27.2 %copy-start.7 = (f32[32,32]{1,0:T(8,128)S(1)}, f32[32,32]{1,0:T(8,128)}, u32[]{:S(2)}) copy-start(f32[32,32]{1,0:T(8,128)} %w_value.3) | copy-start | bytes 12292
  1.3 33.8 %copy-start = (bf16[256,1024]{1,0:T(8,128)(2,1)S(1)}, bf16[256,1024]{1,0:T(8,128)(2,1)}, u32[]{:S(2)}) copy-start(bf16[256,1024]{1,0:T(8,128)(2,1)} %refs_9_.1) | copy-start | bytes 1572868
  1.3 33.8 %copy-start.1 = (bf16[1024,256]{1,0:T(8,128)(2,1)S(1)}, bf16[1024,256]{1,0:T(8,128)(2,1)}, u32[]{:S(2)}) copy-start(bf16[1024,256]{1,0:T(8,128)(2,1)} %refs_10_.1) | copy-start | bytes 1572868
  1.3 33.8 %copy-start.2 = (bf16[256,256]{1,0:T(8,128)(2,1)S(1)}, bf16[256,256]{1,0:T(8,128)(2,1)}, u32[]{:S(2)}) copy-start(bf16[256,256]{1,0:T(8,128)(2,1)} %cotangent.1) | copy-start | bytes 393220
  1.3 33.8 %copy-start.3 = (bf16[256,256]{1,0:T(8,128)(2,1)S(1)}, bf16[256,256]{1,0:T(8,128)(2,1)}, u32[]{:S(2)}) copy-start(bf16[256,256]{1,0:T(8,128)(2,1)} %refs_5_.1) | copy-start | bytes 393220
  1.4 33.8 %copy-start.4 = (bf16[256,256]{1,0:T(8,128)(2,1)S(1)}, bf16[256,256]{1,0:T(8,128)(2,1)}, u32[]{:S(2)}) copy-start(bf16[256,256]{1,0:T(8,128)(2,1)} %refs_7_.1) | copy-start | bytes 393220
  1.4 33.8 %copy-start.10 = (f32[256]{0:T(256)S(1)}, f32[256]{0:T(256)}, u32[]{:S(2)}) copy-start(f32[256]{0:T(256)} %refs_8_.1) | copy-start | bytes 3076
  6.2 1.7 %collective-permute-start = (f32[2,136,256]{2,1,0:T(8,128)S(1)}, f32[2,136,256]{2,1,0:T(8,128)S(1)}, u32[]{:S(2)}, u32[]{:S(2)}) collective-permute-start(f32[2,136,256]{2,1,0:T(8,128)S(1)} %get-tuple-element.57), channel_id=1, source_target_pairs={{0,1},{1,0},{2,3},{3,2},{4,5},{5,4},{6,7},{7,6},{8,9},{9,8},{10,11... | collective-permute-start | bytes 835592 | tf_op jit(solution)/shard_map/ppermute | solution.py:616
  7.9 6.9 %collective-permute-start.1 = (f32[1,136,256]{2,1,0:T(8,128)S(1)}, f32[1,136,256]{2,1,0:T(8,128)S(1)}, u32[]{:S(2)}, u32[]{:S(2)}) collective-permute-start(f32[1,136,256]{2,1,0:T(8,128)S(1)} %slice_add_fusion.4), channel_id=1, source_target_pairs={{0,2},{1,3},{2,0},{3,1},{4,6},{5,7},{6,4},{7,5},{8,10},{9,11},{10,... | collective-permute-start | bytes 417800 | tf_op jit(solution)/shard_map/ppermute | solution.py:616
  14.9 5.3 %collective-permute-start.2 = (f32[136,256]{1,0:T(8,128)S(1)}, f32[136,256]{1,0:T(8,128)S(1)}, u32[]{:S(2)}, u32[]{:S(2)}) collective-permute-start(f32[136,256]{1,0:T(8,128)S(1)} %fusion.1), channel_id=1, source_target_pairs={{0,4},{1,5},{2,6},{3,7},{4,0},{5,1},{6,2},{7,3},{8,12},{9,13},{10,... | collective-permute-start | bytes 417800 | tf_op jit(solution)/shard_map/ppermute | solution.py:616
  20.2 8.3 %collective-permute-start.3 = (f32[136,256]{1,0:T(8,128)S(1)}, f32[136,256]{1,0:T(8,128)S(1)}, u32[]{:S(2)}, u32[]{:S(2)}) collective-permute-start(f32[136,256]{1,0:T(8,128)S(1)} %add.72), channel_id=1, source_target_pairs={{0,8},{1,9},{2,10},{3,11},{4,12},{5,13},{6,14},{7,15},{8,0},{9,1},... | collective-permute-start | bytes 417800 | tf_op jit(solution)/shard_map/ppermute | solution.py:616
  29.6 4.3 %collective-permute-start.4 = (f32[64,256]{1,0:T(8,128)S(1)}, f32[64,256]{1,0:T(8,128)S(1)}, u32[]{:S(2)}, u32[]{:S(2)}) collective-permute-start(f32[64,256]{1,0:T(8,128)S(1)} %get-tuple-element.58.refs_0_.refs_4_), channel_id=1, source_target_pairs={{0,2},{1,3},{2,0},{3,1},{4,6},{5,7},{6,4},{7,5},{8,10},{9,11},{10,... | collective-permute-start | bytes 196616 | tf_op jit(solution)/shard_map/ppermute | solution.py:616
  30.7 3.2 %collective-permute-start.5 = (f32[64,256]{1,0:T(8,128)S(1)}, f32[64,256]{1,0:T(8,128)S(1)}, u32[]{:S(2)}, u32[]{:S(2)}) collective-permute-start(f32[64,256]{1,0:T(8,128)S(1)} %get-tuple-element.58.refs_0_.refs_4_), channel_id=1, source_target_pairs={{0,1},{1,0},{2,3},{3,2},{4,5},{5,4},{6,7},{7,6},{8,9},{9,8},{10,11... | collective-permute-start | bytes 196616 | tf_op jit(solution)/shard_map/ppermute | solution.py:616
  33.9 1.3 %collective-permute-start.6 = (f32[64,256]{1,0:T(8,128)S(1)}, f32[64,256]{1,0:T(8,128)S(1)}, u32[]{:S(2)}, u32[]{:S(2)}) collective-permute-start(f32[64,256]{1,0:T(8,128)S(1)} %collective-permute-done.4.refs_1_.refs_5_), channel_id=1, source_target_pairs={{0,1},{1,0},{2,3},{3,2},{4,5},{5,4},{6,7},{7,6},{8,9},{9,8},{10,11... | collective-permute-start | bytes 196616 | tf_op jit(solution)/shard_map/ppermute | solution.py:616
  38.0 1.3 %collective-permute-start.7 = (f32[2,64,256]{2,1,0:T(8,128)S(1)}, f32[2,64,256]{2,1,0:T(8,128)S(1)}, u32[]{:S(2)}, u32[]{:S(2)}) collective-permute-start(f32[2,64,256]{2,1,0:T(8,128)S(1)} %get-tuple-element.69), channel_id=1, source_target_pairs={{0,1},{1,0},{2,3},{3,2},{4,5},{5,4},{6,7},{7,6},{8,9},{9,8},{10,11... | collective-permute-start | bytes 393224 | tf_op jit(solution)/shard_map/ppermute | solution.py:616
  39.9 15.0 %collective-permute-start.11 = (f32[8,144,256]{2,1,0:T(8,128)S(1)}, f32[8,144,256]{2,1,0:T(8,128)S(1)}, u32[]{:S(2)}, u32[]{:S(2)}) collective-permute-start(f32[8,144,256]{2,1,0:T(8,128)S(1)} %get-tuple-element.76), channel_id=1, source_target_pairs={{0,1},{1,0},{2,3},{3,2},{4,5},{5,4},{6,7},{7,6},{8,9},{9,8},{10,11... | collective-permute-start | bytes 3538952 | tf_op jit(solution)/shard_map/ppermute | solution.py:616
  40.2 4.4 %collective-permute-start.8 = (f32[1,64,256]{2,1,0:T(8,128)S(1)}, f32[1,64,256]{2,1,0:T(8,128)S(1)}, u32[]{:S(2)}, u32[]{:S(2)}) collective-permute-start(f32[1,64,256]{2,1,0:T(8,128)S(1)} %slice_add_fusion.10), channel_id=1, source_target_pairs={{0,2},{1,3},{2,0},{3,1},{4,6},{5,7},{6,4},{7,5},{8,10},{9,11},{10,... | collective-permute-start | bytes 196616 | tf_op jit(solution)/shard_map/ppermute | solution.py:616
  44.6 4.3 %collective-permute-start.9 = (f32[64,256]{1,0:T(8,128)S(1)}, f32[64,256]{1,0:T(8,128)S(1)}, u32[]{:S(2)}, u32[]{:S(2)}) collective-permute-start(f32[64,256]{1,0:T(8,128)S(1)} %add_bitcast_fusion), channel_id=1, source_target_pairs={{0,4},{1,5},{2,6},{3,7},{4,0},{5,1},{6,2},{7,3},{8,12},{9,13},{10,... | collective-permute-start | bytes 196616 | tf_op jit(solution)/shard_map/ppermute | solution.py:616
  49.0 5.9 %collective-permute-start.10 = (f32[64,256]{1,0:T(8,128)S(1)}, f32[64,256]{1,0:T(8,128)S(1)}, u32[]{:S(2)}, u32[]{:S(2)}) collective-permute-start(f32[64,256]{1,0:T(8,128)S(1)} %add.77), channel_id=1, source_target_pairs={{0,8},{1,9},{2,10},{3,11},{4,12},{5,13},{6,14},{7,15},{8,0},{9,1},... | collective-permute-start | bytes 196616 | tf_op jit(solution)/shard_map/ppermute | solution.py:616
  55.1 8.4 %copy-start.8 = (bf16[32,256]{1,0:T(8,128)(2,1)S(1)}, bf16[32,256]{1,0:T(8,128)(2,1)}, u32[]{:S(2)}) copy-start(bf16[32,256]{1,0:T(8,128)(2,1)} %refs_16_.1) | copy-start | bytes 49156
  55.1 8.3 %copy-start.9 = (f32[8]{0:T(128)S(1)}, f32[8]{0:T(128)}, u32[]{:S(2)}) copy-start(f32[8]{0:T(128)} %sharpness.1) | copy-start | bytes 100
  55.1 13.5 %collective-permute-start.15 = (f32[4,144,256]{2,1,0:T(8,128)S(1)}, f32[4,144,256]{2,1,0:T(8,128)S(1)}, u32[]{:S(2)}, u32[]{:S(2)}) collective-permute-start(f32[4,144,256]{2,1,0:T(8,128)S(1)} %get-tuple-element.105), channel_id=1, source_target_pairs={{0,4},{1,5},{2,6},{3,7},{4,0},{5,1},{6,2},{7,3},{8,12},{9,13},{10,... | collective-permute-start | bytes 1769480 | tf_op jit(solution)/shard_map/ppermute | solution.py:616
  56.7 5.3 %collective-permute-start.12 = (f32[152,256]{1,0:T(8,128)S(1)}, f32[152,256]{1,0:T(8,128)S(1)}, u32[]{:S(2)}, u32[]{:S(2)}) collective-permute-start(f32[152,256]{1,0:T(8,128)S(1)} %mix_back.1.refs_0_), channel_id=1, source_target_pairs={{0,2},{1,3},{2,0},{3,1},{4,6},{5,7},{6,4},{7,5},{8,10},{9,11},{10,... | collective-permute-start | bytes 466952 | tf_op jit(solution)/shard_map/ppermute | solution.py:616
  58.3 3.7 %collective-permute-start.13 = (f32[152,256]{1,0:T(8,128)S(1)}, f32[152,256]{1,0:T(8,128)S(1)}, u32[]{:S(2)}, u32[]{:S(2)}) collective-permute-start(f32[152,256]{1,0:T(8,128)S(1)} %mix_back.1.refs_0_), channel_id=1, source_target_pairs={{0,1},{1,0},{2,3},{3,2},{4,5},{5,4},{6,7},{7,6},{8,9},{9,8},{10,11... | collective-permute-start | bytes 466952 | tf_op jit(solution)/shard_map/ppermute | solution.py:616
  62.0 1.4 %collective-permute-start.14 = (f32[152,256]{1,0:T(8,128)S(1)}, f32[152,256]{1,0:T(8,128)S(1)}, u32[]{:S(2)}, u32[]{:S(2)}) collective-permute-start(f32[152,256]{1,0:T(8,128)S(1)} %collective-permute-done.12.refs_1_), channel_id=1, source_target_pairs={{0,1},{1,0},{2,3},{3,2},{4,5},{5,4},{6,7},{7,6},{8,9},{9,8},{10,11... | collective-permute-start | bytes 466952 | tf_op jit(solution)/shard_map/ppermute | solution.py:616
  68.7 1.8 %collective-permute-start.16 = (f32[288,256]{1,0:T(8,128)S(1)}, f32[288,256]{1,0:T(8,128)S(1)}, u32[]{:S(2)}, u32[]{:S(2)}) collective-permute-start(f32[288,256]{1,0:T(8,128)S(1)} %get-tuple-element.91), channel_id=1, source_target_pairs={{0,1},{1,0},{2,3},{3,2},{4,5},{5,4},{6,7},{7,6},{8,9},{9,8},{10,11... | collective-permute-start | bytes 884744 | tf_op jit(solution)/shard_map/ppermute | solution.py:616
  69.0 9.3 %collective-permute-start.18 = (f32[2,144,256]{2,1,0:T(8,128)S(1)}, f32[2,144,256]{2,1,0:T(8,128)S(1)}, u32[]{:S(2)}, u32[]{:S(2)}) collective-permute-start(f32[2,144,256]{2,1,0:T(8,128)S(1)} %get-tuple-element.106), channel_id=1, source_target_pairs={{0,2},{1,3},{2,0},{3,1},{4,6},{5,7},{6,4},{7,5},{8,10},{9,11},{10,... | collective-permute-start | bytes 884744 | tf_op jit(solution)/shard_map/ppermute | solution.py:616
  70.6 7.7 %collective-permute-start.17 = (f32[160,256]{1,0:T(8,128)S(1)}, f32[160,256]{1,0:T(8,128)S(1)}, u32[]{:S(2)}, u32[]{:S(2)}) collective-permute-start(f32[160,256]{1,0:T(8,128)S(1)} %pad_maximum_fusion), channel_id=1, source_target_pairs={{0,4},{1,5},{2,6},{3,7},{4,0},{5,1},{6,2},{7,3},{8,12},{9,13},{10,... | collective-permute-start | bytes 491528 | tf_op jit(solution)/shard_map/ppermute | solution.py:616
  78.4 4.7 %collective-permute-start.19 = (f32[96,256]{1,0:T(8,128)S(1)}, f32[96,256]{1,0:T(8,128)S(1)}, u32[]{:S(2)}, u32[]{:S(2)}) collective-permute-start(f32[96,256]{1,0:T(8,128)S(1)} %pad_maximum_fusion.1), channel_id=1, source_target_pairs={{0,2},{1,3},{2,0},{3,1},{4,6},{5,7},{6,4},{7,5},{8,10},{9,11},{10,... | collective-permute-start | bytes 294920 | tf_op jit(solution)/shard_map/ppermute | solution.py:616
  80.0 11.5 %collective-permute-start.21 = (f32[1,144,256]{2,1,0:T(8,128)S(1)}, f32[1,144,256]{2,1,0:T(8,128)S(1)}, u32[]{:S(2)}, u32[]{:S(2)}) collective-permute-start(f32[1,144,256]{2,1,0:T(8,128)S(1)} %get-tuple-element.98), channel_id=1, source_target_pairs={{0,8},{1,9},{2,10},{3,11},{4,12},{5,13},{6,14},{7,15},{8,0},{9,1},... | collective-permute-start | bytes 442376 | tf_op jit(solution)/shard_map/ppermute | solution.py:616
  83.1 9.1 %collective-permute-start.20 = (f32[64,256]{1,0:T(8,128)S(1)}, f32[64,256]{1,0:T(8,128)S(1)}, u32[]{:S(2)}, u32[]{:S(2)}) collective-permute-start(f32[64,256]{1,0:T(8,128)S(1)} %pad_maximum_fusion.2), channel_id=1, source_target_pairs={{0,8},{1,9},{2,10},{3,11},{4,12},{5,13},{6,14},{7,15},{8,0},{9,1},... | collective-permute-start | bytes 196616 | tf_op jit(solution)/shard_map/ppermute | solution.py:616

commit v5 on v4

--- a/solution.py
+++ b/solution.py
@@ -11,7 +11,7 @@
 F32 = jnp.float32
 BF16 = jnp.bfloat16
 EPS = 1e-05
-GROUP_BITS = 2
+GROUP_BITS = (0, 2)
 GELU_A = math.sqrt(2.0 / math.pi)
 GELU_B = 0.044715
 
@@ -30,6 +30,13 @@
     out = 0
     for k in range(bits):
         out = (out << 1) | ((value >> k) & 1)
+    return out
+
+
+def group_of(me):
+    out = 0
+    for k, bit in enumerate(GROUP_BITS):
+        out |= ((me >> bit) & 1) << k
     return out
 
 
@@ -201,7 +208,7 @@
             numerators(h - 1)
     numerators(heads - 1)
 
-    place_groups(lambda g: total[g], keep, send, me & (groups - 1))
+    place_groups(lambda g: total[g], keep, send, group_of(me))
 
 
 tie = lax.optimization_barrier
@@ -319,7 +326,7 @@
     heads = low.shape[0] // slices
     width = model // heads
     per = heads // groups
-    mine = me & (groups - 1)
+    mine = group_of(me)
     for r, piece in zip(rel, pieces):
         canon[mine ^ r] = piece[...]
     for h in range(heads):
@@ -419,7 +426,7 @@
     width, slices = w_slice.shape
     heads = model // width
     per = heads // groups
-    mine = me & (groups - 1)
+    mine = group_of(me)
     base = 2 * per * width
     for r, piece, mix_piece in zip(rel, pieces, mixed):
         canon[mine ^ r] = piece[...]
@@ -520,34 +527,28 @@
         grad_mix[i] = wide[:, i * width : (i + 1) * width]
 
 
-def finish_kernel(keep, got, slice_sum, feat, mid, slice_out):
-    step = feat.shape[0]
-    feat[...] = keep[:step, :] + got[:step, :]
-    mid[...] = keep[step:, :] + got[step : 2 * step, :]
-    slice_out[...] = slice_sum[...] + got[2 * step :, :]
-
-
-def fold_kernel(value, got, keep, send):
-    count = keep.shape[0]
-    keep[...] = value[:count] + got[:count]
-    send[...] = value[count:] + got[count:]
-
-
-def outer_finish_kernel(keep, got, out, up, down):
+def add_kernel(left, right, out):
+    out[...] = left[...] + right[...]
+
+
+def finish_kernel(main_keep, main_got, slice_sum, value, feat, mid, slice_out, out, up, down):
     step, model = out.shape
+    feat[...] = main_keep[:step, :] + main_got[:step, :]
+    mid[...] = main_keep[step:, :] + main_got[step : 2 * step, :]
+    slice_out[...] = slice_sum[...] + main_got[2 * step :, :]
     wide = up.shape[1] // model
-    out[...] = keep[0, :step, :] + got[0, :step, :]
+    out[...] = value[0, :step, :]
     for w in range(wide):
         at = slice(step * (1 + w), step * (2 + w))
-        up[:, w * model : (w + 1) * model] = keep[0, at, :] + got[0, at, :]
-    down[...] = keep[0, step * (1 + wide) :, :] + got[0, step * (1 + wide) :, :]
+        up[:, w * model : (w + 1) * model] = value[0, at, :]
+    down[...] = value[0, step * (1 + wide) :, :]
 
 
 VMEM = pl.BlockSpec(memory_space=pltpu.VMEM)
 SMEM = pl.BlockSpec(memory_space=pltpu.SMEM)
 HBM = pl.BlockSpec(memory_space=pltpu.HBM)
 MIB = 1024 * 1024
-COSTS = {"point_back": 0.001, "mix_back": 0.001, "fold": 8.0}
+COSTS = {"point_back": 0.001, "mix_back": 0.001, "add": 12.0}
 
 
 def shape(dims, dtype=F32):
@@ -603,7 +604,8 @@
     heads = sharpness.shape[0]
     hidden_width = w_up.shape[1]
     all_bits = parts.bit_length() - 1
-    bits = min(GROUP_BITS, all_bits)
+    bits = len(GROUP_BITS)
+    rest_bits = [bit for bit in range(all_bits) if bit not in GROUP_BITS]
     groups = 1 << bits
     per = heads // groups
     token_height = 2 * per * width + pad_to(2 * per, 8)
@@ -619,17 +621,17 @@
         count = keep.shape[0] // 2
         return keep[:count] + got[:count], keep[count:] + got[count:]
 
-    def add_all(value, first, last):
-        for bit in range(first, last):
+    def add_all(value, over):
+        for bit in over:
             value = value + exchange(value, bit)
         return value
 
-    def collect(pieces, first, count):
-        for bit in reversed(range(first, first + count)):
+    def collect(pieces):
+        for bit in reversed(GROUP_BITS):
             pieces = pieces + [exchange(piece, bit) for piece in pieces]
         return pieces
 
-    main_order = outer_order = (0, 2, 1) + tuple(range(3, all_bits))
+    main_order = outer_order = tuple(range(all_bits))
     rel = [0]
     for bit in reversed(range(bits)):
         rel = rel + [r ^ (1 << bit) for r in rel]
@@ -672,11 +674,11 @@
         w_mid,
         w_slice,
     )
-    got = exchange(send, 0)
-    for bit in range(1, bits):
+    got = exchange(send, GROUP_BITS[0])
+    for bit in GROUP_BITS[1:]:
         keep, send = fold(keep, got)
         got = exchange(send, bit)
-    tokens = add_all((keep + got)[0], bits, all_bits)
+    tokens = add_all((keep + got)[0], rest_bits)
     mixed, attention, kept = run(
         mix_kernel,
         "mix_tokens",
@@ -693,7 +695,7 @@
         w_key,
         w_value,
     )
-    mixed_pieces = collect([mixed], 0, bits)
+    mixed_pieces = collect([mixed])
     (
         layer_out,
         grad_att,
@@ -730,7 +732,7 @@
         w_up,
         w_down,
     )
-    got = exchange(send, 0)
+    got = exchange(send, GROUP_BITS[0])
     attended, second, hidden, grad_upper, grad_resid, got = tie(
         (attended, second, hidden, grad_upper, grad_resid, got)
     )
@@ -752,14 +754,15 @@
         grad_resid,
         cotangent,
     )
-    for bit in range(1, bits):
+    for bit in GROUP_BITS[1:]:
         keep, send = fold(keep, got)
         got = exchange(send, bit)
-    outer_got = exchange(outer_send, 0)
-    mixed_grad = add_all((keep + got)[0], bits, all_bits)
+    outer_got = exchange(outer_send, outer_order[0])
+    mixed_grad = add_all((keep + got)[0], rest_bits[:1])
     mixed_grad, outer_got = tie((mixed_grad, outer_got))
     outer_keep, outer_send = fold(outer_keep, outer_got)
     outer_got = exchange(outer_send, outer_order[1])
+    mixed_grad = add_all(mixed_grad, rest_bits[1:])
     token_grad = run(
         mix_back_kernel,
         "mix_back",
@@ -775,7 +778,9 @@
         w_key,
         w_value,
     )
-    grad_pieces = collect([token_grad], 0, bits)
+    grad_pieces = collect([token_grad])
+    outer_keep, outer_send = fold(outer_keep, outer_got)
+    outer_got = exchange(outer_send, outer_order[2])
     keep, send, grad_mix = run(
         functools.partial(back_kernel, tuple(rel), main_order),
         "point_back",
@@ -816,22 +821,15 @@
         if turn == 0:
             send, outer_got = tie((send, outer_got))
             outer_keep, outer_send = fold(outer_keep, outer_got)
-            outer_got = exchange(outer_send, outer_order[2])
-            send, outer_keep = tie((send, outer_keep))
-        if turn == 2:
-            count = outer_keep.shape[0] // 2
-            outer_keep, outer_send = run(
-                fold_kernel,
-                "fold",
-                4,
-                VMEM,
-                (shape((count,) + outer_keep.shape[1:]),) * 2,
-                [],
-                outer_keep,
-                outer_got,
+            outer_got = exchange(outer_send, outer_order[3])
+        if turn == all_bits - 1:
+            for late in outer_order[4:]:
+                outer_keep, outer_send = fold(outer_keep, outer_got)
+                outer_got = exchange(outer_send, late)
+            outer = run(
+                add_kernel, "add", 4, VMEM, shape(outer_keep.shape), [], outer_keep, outer_got
             )
-            send, outer_keep = tie((send, outer_keep))
-            outer_got = exchange(outer_send, outer_order[3])
+            send, outer = tie((send, outer))
         got = exchange(send, bit)
         if turn == all_bits - 1:
             break
@@ -839,29 +837,24 @@
         count = keep.shape[0] // 2
         send = jnp.concatenate([keep[count:] + got[count : 2 * count], slice_sum], axis=0)
         keep = keep[:count] + got[:count]
-    grad_feat, grad_mid, grad_slice = run(
+    grad_feat, grad_mid, grad_slice, grad_out, grad_up, grad_down = run(
         finish_kernel,
         "finish",
         4,
         VMEM,
-        (shape((step, model)), shape((step, model)), shape((width, slices))),
+        (
+            shape((step, model)),
+            shape((step, model)),
+            shape((width, slices)),
+            shape((step, model)),
+            shape((step, hidden_width)),
+            shape((step * wide, model)),
+        ),
         [],
         keep,
         got,
         slice_sum,
-    )
-    for bit in outer_order[4:]:
-        outer_keep, outer_send = fold(outer_keep, outer_got)
-        outer_got = exchange(outer_send, bit)
-    grad_out, grad_up, grad_down = run(
-        outer_finish_kernel,
-        "outer_finish",
-        4,
-        VMEM,
-        (shape((step, model)), shape((step, hidden_width)), shape((step * wide, model))),
-        [],
-        outer_keep,
-        outer_got,
+        outer,
     )
     return (layer_out, grad_feat, grad_mid, grad_out, grad_up, grad_down, grad_slice, grad_mix)
 

time: 93 us -> 92.1 us (level)
  starting transfers between devices: 25.4 us -> 21.8 us
  waiting for transfers between devices: 47.9 us -> 51.1 us
    ppermute x22, starting transfers between devices: 25.4 us -> 21.8 us  [exchange(): return lax.ppermute(value, 'pts', [(i, i ^ 1 << bit) for i in range(parts)])]
    ppermute x22, waiting for transfers between devices: 47.9 us -> 51.1 us  [exchange(): return lax.ppermute(value, 'pts', [(i, i ^ 1 << bit) for i in range(parts)])]
    pallas_call x9 -> x8, Pallas kernels: 17.4 us -> 16.9 us  [run(): pl.pallas_call(body, out_shape=out_shape, in_specs=[first] + [rest] * (le...]
  transfers between devices with their start and end apart: 22 -> 22, of which waited for: 15 -> 18; matrix products, arithmetic and copies ran while one was open for 0% -> 0% of each run, Pallas kernels for 8% -> 7%
where the time goes in v5:
time: 92.1 us; the launch traced here: 92 us
  waiting for transfers between devices  51.1 us (55%)
  starting transfers between devices  21.8 us (24%)
  Pallas kernels  16.9 us (18%)
  between operations  1.55 us (2%)
    ppermute x22, waiting for transfers between devices, exchange(): return lax.ppermute(value, 'pts', [(i, i ^ 1 << bit) for i in range(parts)])  51.1 us
    ppermute x22, starting transfers between devices, exchange(): return lax.ppermute(value, 'pts', [(i, i ^ 1 << bit) for i in range(parts)])  21.8 us
    pallas_call x8, Pallas kernels, run(): pl.pallas_call(body, out_shape=out_shape, in_specs=[first] + [rest] * (le...  16.9 us
  transfers between devices with their start and end apart: 22, of which 18 were waited for; matrix products, arithmetic and copies ran while one was open for 0% of the time, Pallas kernels for 7%

profile of v5, /device:TPU:0, one launch (start us, length us, event | category | flops | bytes accessed | tf_op | source)
XLA Modules:
  0.0 92.0 jit_solution(15421066903795850908)
XLA Ops:
  1.3 0.0 copy-start.5
  1.3 0.0 copy-start.6
  1.3 0.0 copy-start.7
  1.3 0.0 copy-start
  1.3 0.0 copy-start.1
  1.3 0.0 copy-start.2
  1.3 0.0 copy-start.3
  1.4 0.0 copy-start.4
  1.4 0.0 copy-start.10
  1.4 4.8 %slice_sums.1 = (f32[2,136,256]{2,1,0:T(8,128)S(1)}, f32[2,136,256]{2,1,0:T(8,128)S(1)}, bf16[256,768]{1,0:T(8,128)(2,1)S(1)}, bf16[256,768]{1,0:T(8,128)(2,1)S(...) custom-call(s32[1]{0:T(128)S(6)} %copy.24.counts_hbm, ...), custom_call_target="tpu_custom_call" | custom-call | tf_op jit(solution)/shard_map/slice_sums/pallas_call | solution.py:569
  6.2 0.5 collective-permute-start
  6.7 1.2 %collective-permute-done = f32[2,136,256]{2,1,0:T(8,128)S(1)} collective-permute-done((f32[2,136,256]{2,1,0:T(8,128)S(1)}, f32[2,136,256]{2,1,0:T(8,128)S(1)}, u32[]{:S(2)}, u32[]{:S(2)}) %collective-permute-start) | collective-permute-done | bytes 278560 | tf_op jit(solution)/shard_map/ppermute | solution.py:618
  7.9 3.0 %collective-permute-start.1 = (f32[1,136,256]{2,1,0:T(8,128)S(1)}, f32[1,136,256]{2,1,0:T(8,128)S(1)}, u32[]{:S(2)}, u32[]{:S(2)}) collective-permute-start(f32[1,136,256]{2,1,0:T(8,128)S(1)} %slice_add_fusion.6), channel_id=1, source_target_pairs={{0,4},{1,5},{2,6},{3,7},{4,0},{5,1},{6,2},{7,3},{8,12},{9,13},{10,... | collective-permute-start | bytes 417800 | tf_op jit(solution)/shard_map/ppermute | solution.py:618
  10.9 4.0 %collective-permute-done.1 = f32[1,136,256]{2,1,0:T(8,128)S(1)} collective-permute-done((f32[1,136,256]{2,1,0:T(8,128)S(1)}, f32[1,136,256]{2,1,0:T(8,128)S(1)}, u32[]{:S(2)}, u32[]{:S(2)}) %collective-permute-start.1) | collective-permute-done | bytes 139296 | tf_op jit(solution)/shard_map/ppermute | solution.py:618
  14.9 1.7 %collective-permute-start.2 = (f32[136,256]{1,0:T(8,128)S(1)}, f32[136,256]{1,0:T(8,128)S(1)}, u32[]{:S(2)}, u32[]{:S(2)}) collective-permute-start(f32[136,256]{1,0:T(8,128)S(1)} %fusion.1), channel_id=1, source_target_pairs={{0,2},{1,3},{2,0},{3,1},{4,6},{5,7},{6,4},{7,5},{8,10},{9,11},{10,... | collective-permute-start | bytes 417800 | tf_op jit(solution)/shard_map/ppermute | solution.py:618
  16.7 3.5 %collective-permute-done.2 = f32[136,256]{1,0:T(8,128)S(1)} collective-permute-done((f32[136,256]{1,0:T(8,128)S(1)}, f32[136,256]{1,0:T(8,128)S(1)}, u32[]{:S(2)}, u32[]{:S(2)}) %collective-permute-start.2) | collective-permute-done | bytes 139296 | tf_op jit(solution)/shard_map/ppermute | solution.py:618
  20.2 2.7 %collective-permute-start.3 = (f32[136,256]{1,0:T(8,128)S(1)}, f32[136,256]{1,0:T(8,128)S(1)}, u32[]{:S(2)}, u32[]{:S(2)}) collective-permute-start(f32[136,256]{1,0:T(8,128)S(1)} %add.79), channel_id=1, source_target_pairs={{0,8},{1,9},{2,10},{3,11},{4,12},{5,13},{6,14},{7,15},{8,0},{9,1},... | collective-permute-start | bytes 417800 | tf_op jit(solution)/shard_map/ppermute | solution.py:618
  22.9 5.6 %collective-permute-done.3 = f32[136,256]{1,0:T(8,128)S(1)} collective-permute-done((f32[136,256]{1,0:T(8,128)S(1)}, f32[136,256]{1,0:T(8,128)S(1)}, u32[]{:S(2)}, u32[]{:S(2)}) %collective-permute-start.3) | collective-permute-done | bytes 139296 | tf_op jit(solution)/shard_map/ppermute | solution.py:618
  28.5 1.1 %mix_tokens.1 = (f32[64,256]{1,0:T(8,128)S(1)}, f32[2,512,256]{2,1,0:T(8,128)S(1)}, f32[2,96,512]{2,1,0:T(8,128)S(1)}) custom-call(f32[136,256]{1,0:T(8,128)S(1)} %add.80.tokens, f32[32,32]{1,0:T(8,128)S(1)} %copy-done.5, f32[32,32]{1,0:T(8,128)S(1)} %copy-done.6, f32[32,32]{1,0:T(8,128)S(1)} %copy-done.7), custom_call_target="tpu_custom_call" | custom-call | tf_op jit(solution)/shard_map/mix_tokens/pallas_call | solution.py:569
  29.7 0.1 collective-permute-start.4
  29.8 0.0 collective-permute-start.5
  29.8 4.1 %collective-permute-done.4.refs_1_.refs_5_ = f32[64,256]{1,0:T(8,128)S(1)} collective-permute-done((f32[64,256]{1,0:T(8,128)S(1)}, f32[64,256]{1,0:T(8,128)S(1)}, u32[]{:S(2)}, u32[]{:S(2)}) %collective-permute-start.4) | collective-permute-done | bytes 65568 | tf_op jit(solution)/shard_map/ppermute | solution.py:618
  34.0 0.0 collective-permute-start.6
  34.0 0.0 collective-permute-done.5.refs_2_.refs_6_
  34.0 1.2 %collective-permute-done.6.refs_3_.refs_7_ = f32[64,256]{1,0:T(8,128)S(1)} collective-permute-done((f32[64,256]{1,0:T(8,128)S(1)}, f32[64,256]{1,0:T(8,128)S(1)}, u32[]{:S(2)}, u32[]{:S(2)}) %collective-permute-start.6) | collective-permute-done | bytes 65568 | tf_op jit(solution)/shard_map/ppermute | solution.py:618
  35.2 0.0 copy-done.3
  35.3 2.9 %mlp.1 = (bf16[256,256]{1,0:T(8,128)(2,1)}, bf16[256,256]{1,0:T(8,128)(2,1)S(1)}, f32[2,64,256]{2,1,0:T(8,128)S(1)}, f32[2,64,256]{2,1,0:T(8,128)S(1)}, bf16[256...) custom-call(f32[64,256]{1,0:T(8,128)S(1)} %get-tuple-element.54.refs, ...), custom_call_target="tpu_custom_call" | custom-call | tf_op jit(solution)/shard_map/mlp/pallas_call | solution.py:569
  38.2 0.2 collective-permute-start.7
  38.4 1.2 %collective-permute-done.7 = f32[2,64,256]{2,1,0:T(8,128)S(1)} collective-permute-done((f32[2,64,256]{2,1,0:T(8,128)S(1)}, f32[2,64,256]{2,1,0:T(8,128)S(1)}, u32[]{:S(2)}, u32[]{:S(2)}) %collective-permute-start.7) | collective-permute-done | bytes 131104 | tf_op jit(solution)/shard_map/ppermute | solution.py:618
  39.5 0.6 weight_grads.1
  40.1 0.2 collective-permute-start.10
  40.4 0.2 collective-permute-start.8
  40.5 4.2 %collective-permute-done.8 = f32[1,64,256]{2,1,0:T(8,128)S(1)} collective-permute-done((f32[1,64,256]{2,1,0:T(8,128)S(1)}, f32[1,64,256]{2,1,0:T(8,128)S(1)}, u32[]{:S(2)}, u32[]{:S(2)}) %collective-permute-start.8) | collective-permute-done | bytes 65568 | tf_op jit(solution)/shard_map/ppermute | solution.py:618
  44.8 1.0 %collective-permute-start.9 = (f32[64,256]{1,0:T(8,128)S(1)}, f32[64,256]{1,0:T(8,128)S(1)}, u32[]{:S(2)}, u32[]{:S(2)}) collective-permute-start(f32[64,256]{1,0:T(8,128)S(1)} %add_bitcast_fusion), channel_id=1, source_target_pairs={{0,2},{1,3},{2,0},{3,1},{4,6},{5,7},{6,4},{7,5},{8,10},{9,11},{10,... | collective-permute-start | bytes 196616 | tf_op jit(solution)/shard_map/ppermute | solution.py:618
  45.8 3.3 %collective-permute-done.9 = f32[64,256]{1,0:T(8,128)S(1)} collective-permute-done((f32[64,256]{1,0:T(8,128)S(1)}, f32[64,256]{1,0:T(8,128)S(1)}, u32[]{:S(2)}, u32[]{:S(2)}) %collective-permute-start.9) | collective-permute-done | bytes 65568 | tf_op jit(solution)/shard_map/ppermute | solution.py:618
  49.1 0.0 collective-permute-done.10
  49.1 0.2 slice_add_fusion.1
  49.3 1.0 %collective-permute-start.15 = (f32[4,144,256]{2,1,0:T(8,128)S(1)}, f32[4,144,256]{2,1,0:T(8,128)S(1)}, u32[]{:S(2)}, u32[]{:S(2)}) collective-permute-start(f32[4,144,256]{2,1,0:T(8,128)S(1)} %get-tuple-element.97), channel_id=1, source_target_pairs={{0,2},{1,3},{2,0},{3,1},{4,6},{5,7},{6,4},{7,5},{8,10},{9,11},{10,... | collective-permute-start | bytes 1769480 | tf_op jit(solution)/shard_map/ppermute | solution.py:618
  50.3 2.3 %collective-permute-start.11 = (f32[64,256]{1,0:T(8,128)S(1)}, f32[64,256]{1,0:T(8,128)S(1)}, u32[]{:S(2)}, u32[]{:S(2)}) collective-permute-start(f32[64,256]{1,0:T(8,128)S(1)} %add.84), channel_id=1, source_target_pairs={{0,8},{1,9},{2,10},{3,11},{4,12},{5,13},{6,14},{7,15},{8,0},{9,1},... | collective-permute-start | bytes 196616 | tf_op jit(solution)/shard_map/ppermute | solution.py:618
  52.7 3.6 %collective-permute-done.11 = f32[64,256]{1,0:T(8,128)S(1)} collective-permute-done((f32[64,256]{1,0:T(8,128)S(1)}, f32[64,256]{1,0:T(8,128)S(1)}, u32[]{:S(2)}, u32[]{:S(2)}) %collective-permute-start.11) | collective-permute-done | bytes 65568 | tf_op jit(solution)/shard_map/ppermute | solution.py:618
  56.2 1.5 %mix_back.1.refs_0_ = f32[152,256]{1,0:T(8,128)S(1)} custom-call(f32[136,256]{1,0:T(8,128)S(1)} %add.80.tokens, f32[2,512,256]{2,1,0:T(8,128)S(1)} %get-tuple-element.57.attention_in, f32[2,96,512]{2,1,0:T(8,128)S(1)} %get-tuple-element.58.kept, f32[64,256]{1,0:T(8,128)S(1)} %add.85.grad, f32[32,32]{1,0:T(8,128)S(1)} %copy-done.5, f32[32,32]{1,0:T(8,128)S(1)} %copy-done.6, ...), custom_call_target="tpu_custom_call" | custom-call | flops 1000000 | tf_op jit(solution)/shard_map/mix_back/pallas_call | solution.py:569
  57.8 0.0 copy-start.9
  57.8 0.6 collective-permute-start.12
  58.4 4.6 %collective-permute-done.15 = f32[4,144,256]{2,1,0:T(8,128)S(1)} collective-permute-done((f32[4,144,256]{2,1,0:T(8,128)S(1)}, f32[4,144,256]{2,1,0:T(8,128)S(1)}, u32[]{:S(2)}, u32[]{:S(2)}) %collective-permute-start.15) | collective-permute-done | bytes 589856 | tf_op jit(solution)/shard_map/ppermute | solution.py:618
  63.0 0.1 slice_add_fusion.2
  63.1 0.5 collective-permute-start.16
  63.6 0.0 collective-permute-start.13
  63.6 0.0 collective-permute-done.12.refs_1_
  63.7 0.5 collective-permute-start.14
  64.2 0.9 collective-permute-done.13.refs_2_
  65.0 0.2 collective-permute-done.14.refs_3_
  65.3 5.2 %point_back.1 = (f32[16,16,256]{2,1,0:T(8,128)S(1)}, f32[288,256]{1,0:T(8,128)S(1)}, f32[3,32,32]{2,1,0:T(8,128)}) custom-call(f32[8]{0:T(128)S(1)} %copy-done.9, f32[152,256]{1,0:T(8,128)S(1)} %mix_back.1.refs_0_, f32[152,256]{1,0:T(8,128)S(1)} %collective-permute-done.12.refs_1_, f32[152,256]{1,0:T(8,128)S(1)} %collective-permute-done.13.refs_2_, ...), custom_call_target="tpu_custom_call" | custom-call | flops 1000000 | tf_op jit(solution)/shard_map/point_back/pallas_call | solution.py:569
  70.5 0.0 collective-permute-done.16
  70.5 0.3 collective-permute-start.17
  70.8 1.3 %collective-permute-done.17 = f32[288,256]{1,0:T(8,128)S(1)} collective-permute-done((f32[288,256]{1,0:T(8,128)S(1)}, f32[288,256]{1,0:T(8,128)S(1)}, u32[]{:S(2)}, u32[]{:S(2)}) %collective-permute-start.17) | collective-permute-done | bytes 294944 | tf_op jit(solution)/shard_map/ppermute | solution.py:618
  72.1 1.2 %collective-permute-start.18 = (f32[160,256]{1,0:T(8,128)S(1)}, f32[160,256]{1,0:T(8,128)S(1)}, u32[]{:S(2)}, u32[]{:S(2)}) collective-permute-start(f32[160,256]{1,0:T(8,128)S(1)} %pad_maximum_fusion), channel_id=1, source_target_pairs={{0,2},{1,3},{2,0},{3,1},{4,6},{5,7},{6,4},{7,5},{8,10},{9,11},{10,... | collective-permute-start | bytes 491528 | tf_op jit(solution)/shard_map/ppermute | solution.py:618
  73.4 3.4 %collective-permute-start.20 = (f32[1,144,256]{2,1,0:T(8,128)S(1)}, f32[1,144,256]{2,1,0:T(8,128)S(1)}, u32[]{:S(2)}, u32[]{:S(2)}) collective-permute-start(f32[1,144,256]{2,1,0:T(8,128)S(1)} %get-tuple-element.100), channel_id=1, source_target_pairs={{0,8},{1,9},{2,10},{3,11},{4,12},{5,13},{6,14},{7,15},{8,0},{9,1},... | collective-permute-start | bytes 442376 | tf_op jit(solution)/shard_map/ppermute | solution.py:618
  76.8 1.7 %collective-permute-done.18 = f32[160,256]{1,0:T(8,128)S(1)} collective-permute-done((f32[160,256]{1,0:T(8,128)S(1)}, f32[160,256]{1,0:T(8,128)S(1)}, u32[]{:S(2)}, u32[]{:S(2)}) %collective-permute-start.18) | collective-permute-done | bytes 163872 | tf_op jit(solution)/shard_map/ppermute | solution.py:618
  78.6 1.6 %collective-permute-start.19 = (f32[96,256]{1,0:T(8,128)S(1)}, f32[96,256]{1,0:T(8,128)S(1)}, u32[]{:S(2)}, u32[]{:S(2)}) collective-permute-start(f32[96,256]{1,0:T(8,128)S(1)} %pad_maximum_fusion.1), channel_id=1, source_target_pairs={{0,4},{1,5},{2,6},{3,7},{4,0},{5,1},{6,2},{7,3},{8,12},{9,13},{10,... | collective-permute-start | bytes 294920 | tf_op jit(solution)/shard_map/ppermute | solution.py:618
  80.2 3.9 %collective-permute-done.20.right = f32[1,144,256]{2,1,0:T(8,128)S(1)} collective-permute-done((f32[1,144,256]{2,1,0:T(8,128)S(1)}, f32[1,144,256]{2,1,0:T(8,128)S(1)}, u32[]{:S(2)}, u32[]{:S(2)}) %collective-permute-start.20) | collective-permute-done | bytes 147488 | tf_op jit(solution)/shard_map/ppermute | solution.py:618
  84.2 1.7 %collective-permute-done.19 = f32[96,256]{1,0:T(8,128)S(1)} collective-permute-done((f32[96,256]{1,0:T(8,128)S(1)}, f32[96,256]{1,0:T(8,128)S(1)}, u32[]{:S(2)}, u32[]{:S(2)}) %collective-permute-start.19) | collective-permute-done | bytes 98336 | tf_op jit(solution)/shard_map/ppermute | solution.py:618
  85.9 0.5 collective-permute-start.21
  86.5 4.8 %collective-permute-done.21.main_got = f32[64,256]{1,0:T(8,128)S(1)} collective-permute-done((f32[64,256]{1,0:T(8,128)S(1)}, f32[64,256]{1,0:T(8,128)S(1)}, u32[]{:S(2)}, u32[]{:S(2)}) %collective-permute-start.21) | collective-permute-done | bytes 65568 | tf_op jit(solution)/shard_map/ppermute | solution.py:618
  91.3 0.7 finish.1
  (30 shorter events, 0.3 us)
Async XLA Ops:
  1.3 27.2 %copy-start.5 = (f32[32,32]{1,0:T(8,128)S(1)}, f32[32,32]{1,0:T(8,128)}, u32[]{:S(2)}) copy-start(f32[32,32]{1,0:T(8,128)} %w_query.3) | copy-start | bytes 12292
  1.3 27.2 %copy-start.6 = (f32[32,32]{1,0:T(8,128)S(1)}, f32[32,32]{1,0:T(8,128)}, u32[]{:S(2)}) copy-start(f32[32,32]{1,0:T(8,128)} %w_key.3) | copy-start | bytes 12292
  1.3 27.2 %copy-start.7 = (f32[32,32]{1,0:T(8,128)S(1)}, f32[32,32]{1,0:T(8,128)}, u32[]{:S(2)}) copy-start(f32[32,32]{1,0:T(8,128)} %w_value.3) | copy-start | bytes 12292
  1.3 33.9 %copy-start = (bf16[256,1024]{1,0:T(8,128)(2,1)S(1)}, bf16[256,1024]{1,0:T(8,128)(2,1)}, u32[]{:S(2)}) copy-start(bf16[256,1024]{1,0:T(8,128)(2,1)} %refs_9_.1) | copy-start | bytes 1572868
  1.3 33.9 %copy-start.1 = (bf16[1024,256]{1,0:T(8,128)(2,1)S(1)}, bf16[1024,256]{1,0:T(8,128)(2,1)}, u32[]{:S(2)}) copy-start(bf16[1024,256]{1,0:T(8,128)(2,1)} %refs_10_.1) | copy-start | bytes 1572868
  1.3 33.9 %copy-start.2 = (bf16[256,256]{1,0:T(8,128)(2,1)S(1)}, bf16[256,256]{1,0:T(8,128)(2,1)}, u32[]{:S(2)}) copy-start(bf16[256,256]{1,0:T(8,128)(2,1)} %cotangent.1) | copy-start | bytes 393220
  1.3 33.9 %copy-start.3 = (bf16[256,256]{1,0:T(8,128)(2,1)S(1)}, bf16[256,256]{1,0:T(8,128)(2,1)}, u32[]{:S(2)}) copy-start(bf16[256,256]{1,0:T(8,128)(2,1)} %refs_5_.1) | copy-start | bytes 393220
  1.4 33.9 %copy-start.4 = (bf16[256,256]{1,0:T(8,128)(2,1)S(1)}, bf16[256,256]{1,0:T(8,128)(2,1)}, u32[]{:S(2)}) copy-start(bf16[256,256]{1,0:T(8,128)(2,1)} %refs_7_.1) | copy-start | bytes 393220
  1.4 33.9 %copy-start.10 = (f32[256]{0:T(256)S(1)}, f32[256]{0:T(256)}, u32[]{:S(2)}) copy-start(f32[256]{0:T(256)} %refs_8_.1) | copy-start | bytes 3076
  6.2 1.7 %collective-permute-start = (f32[2,136,256]{2,1,0:T(8,128)S(1)}, f32[2,136,256]{2,1,0:T(8,128)S(1)}, u32[]{:S(2)}, u32[]{:S(2)}) collective-permute-start(f32[2,136,256]{2,1,0:T(8,128)S(1)} %get-tuple-element.53), channel_id=1, source_target_pairs={{0,1},{1,0},{2,3},{3,2},{4,5},{5,4},{6,7},{7,6},{8,9},{9,8},{10,11... | collective-permute-start | bytes 835592 | tf_op jit(solution)/shard_map/ppermute | solution.py:618
  7.9 7.0 %collective-permute-start.1 = (f32[1,136,256]{2,1,0:T(8,128)S(1)}, f32[1,136,256]{2,1,0:T(8,128)S(1)}, u32[]{:S(2)}, u32[]{:S(2)}) collective-permute-start(f32[1,136,256]{2,1,0:T(8,128)S(1)} %slice_add_fusion.6), channel_id=1, source_target_pairs={{0,4},{1,5},{2,6},{3,7},{4,0},{5,1},{6,2},{7,3},{8,12},{9,13},{10,... | collective-permute-start | bytes 417800 | tf_op jit(solution)/shard_map/ppermute | solution.py:618
  14.9 5.3 %collective-permute-start.2 = (f32[136,256]{1,0:T(8,128)S(1)}, f32[136,256]{1,0:T(8,128)S(1)}, u32[]{:S(2)}, u32[]{:S(2)}) collective-permute-start(f32[136,256]{1,0:T(8,128)S(1)} %fusion.1), channel_id=1, source_target_pairs={{0,2},{1,3},{2,0},{3,1},{4,6},{5,7},{6,4},{7,5},{8,10},{9,11},{10,... | collective-permute-start | bytes 417800 | tf_op jit(solution)/shard_map/ppermute | solution.py:618
  20.2 8.3 %collective-permute-start.3 = (f32[136,256]{1,0:T(8,128)S(1)}, f32[136,256]{1,0:T(8,128)S(1)}, u32[]{:S(2)}, u32[]{:S(2)}) collective-permute-start(f32[136,256]{1,0:T(8,128)S(1)} %add.79), channel_id=1, source_target_pairs={{0,8},{1,9},{2,10},{3,11},{4,12},{5,13},{6,14},{7,15},{8,0},{9,1},... | collective-permute-start | bytes 417800 | tf_op jit(solution)/shard_map/ppermute | solution.py:618
  29.7 4.3 %collective-permute-start.4 = (f32[64,256]{1,0:T(8,128)S(1)}, f32[64,256]{1,0:T(8,128)S(1)}, u32[]{:S(2)}, u32[]{:S(2)}) collective-permute-start(f32[64,256]{1,0:T(8,128)S(1)} %get-tuple-element.54.refs_0_.refs_4_), channel_id=1, source_target_pairs={{0,4},{1,5},{2,6},{3,7},{4,0},{5,1},{6,2},{7,3},{8,12},{9,13},{10,... | collective-permute-start | bytes 196616 | tf_op jit(solution)/shard_map/ppermute | solution.py:618
  29.8 4.1 %collective-permute-start.5 = (f32[64,256]{1,0:T(8,128)S(1)}, f32[64,256]{1,0:T(8,128)S(1)}, u32[]{:S(2)}, u32[]{:S(2)}) collective-permute-start(f32[64,256]{1,0:T(8,128)S(1)} %get-tuple-element.54.refs_0_.refs_4_), channel_id=1, source_target_pairs={{0,1},{1,0},{2,3},{3,2},{4,5},{5,4},{6,7},{7,6},{8,9},{9,8},{10,11... | collective-permute-start | bytes 196616 | tf_op jit(solution)/shard_map/ppermute | solution.py:618
  34.0 1.3 %collective-permute-start.6 = (f32[64,256]{1,0:T(8,128)S(1)}, f32[64,256]{1,0:T(8,128)S(1)}, u32[]{:S(2)}, u32[]{:S(2)}) collective-permute-start(f32[64,256]{1,0:T(8,128)S(1)} %collective-permute-done.4.refs_1_.refs_5_), channel_id=1, source_target_pairs={{0,1},{1,0},{2,3},{3,2},{4,5},{5,4},{6,7},{7,6},{8,9},{9,8},{10,11... | collective-permute-start | bytes 196616 | tf_op jit(solution)/shard_map/ppermute | solution.py:618
  38.2 1.3 %collective-permute-start.7 = (f32[2,64,256]{2,1,0:T(8,128)S(1)}, f32[2,64,256]{2,1,0:T(8,128)S(1)}, u32[]{:S(2)}, u32[]{:S(2)}) collective-permute-start(f32[2,64,256]{2,1,0:T(8,128)S(1)} %get-tuple-element.65), channel_id=1, source_target_pairs={{0,1},{1,0},{2,3},{3,2},{4,5},{5,4},{6,7},{7,6},{8,9},{9,8},{10,11... | collective-permute-start | bytes 393224 | tf_op jit(solution)/shard_map/ppermute | solution.py:618
  40.1 9.0 %collective-permute-start.10 = (f32[8,144,256]{2,1,0:T(8,128)S(1)}, f32[8,144,256]{2,1,0:T(8,128)S(1)}, u32[]{:S(2)}, u32[]{:S(2)}) collective-permute-start(f32[8,144,256]{2,1,0:T(8,128)S(1)} %get-tuple-element.72), channel_id=1, source_target_pairs={{0,1},{1,0},{2,3},{3,2},{4,5},{5,4},{6,7},{7,6},{8,9},{9,8},{10,11... | collective-permute-start | bytes 3538952 | tf_op jit(solution)/shard_map/ppermute | solution.py:618
  40.4 4.4 %collective-permute-start.8 = (f32[1,64,256]{2,1,0:T(8,128)S(1)}, f32[1,64,256]{2,1,0:T(8,128)S(1)}, u32[]{:S(2)}, u32[]{:S(2)}) collective-permute-start(f32[1,64,256]{2,1,0:T(8,128)S(1)} %slice_add_fusion.12), channel_id=1, source_target_pairs={{0,4},{1,5},{2,6},{3,7},{4,0},{5,1},{6,2},{7,3},{8,12},{9,13},{10,... | collective-permute-start | bytes 196616 | tf_op jit(solution)/shard_map/ppermute | solution.py:618
  44.8 4.3 %collective-permute-start.9 = (f32[64,256]{1,0:T(8,128)S(1)}, f32[64,256]{1,0:T(8,128)S(1)}, u32[]{:S(2)}, u32[]{:S(2)}) collective-permute-start(f32[64,256]{1,0:T(8,128)S(1)} %add_bitcast_fusion), channel_id=1, source_target_pairs={{0,2},{1,3},{2,0},{3,1},{4,6},{5,7},{6,4},{7,5},{8,10},{9,11},{10,... | collective-permute-start | bytes 196616 | tf_op jit(solution)/shard_map/ppermute | solution.py:618
  49.3 13.7 %collective-permute-start.15 = (f32[4,144,256]{2,1,0:T(8,128)S(1)}, f32[4,144,256]{2,1,0:T(8,128)S(1)}, u32[]{:S(2)}, u32[]{:S(2)}) collective-permute-start(f32[4,144,256]{2,1,0:T(8,128)S(1)} %get-tuple-element.97), channel_id=1, source_target_pairs={{0,2},{1,3},{2,0},{3,1},{4,6},{5,7},{6,4},{7,5},{8,10},{9,11},{10,... | collective-permute-start | bytes 1769480 | tf_op jit(solution)/shard_map/ppermute | solution.py:618
  50.3 5.9 %collective-permute-start.11 = (f32[64,256]{1,0:T(8,128)S(1)}, f32[64,256]{1,0:T(8,128)S(1)}, u32[]{:S(2)}, u32[]{:S(2)}) collective-permute-start(f32[64,256]{1,0:T(8,128)S(1)} %add.84), channel_id=1, source_target_pairs={{0,8},{1,9},{2,10},{3,11},{4,12},{5,13},{6,14},{7,15},{8,0},{9,1},... | collective-permute-start | bytes 196616 | tf_op jit(solution)/shard_map/ppermute | solution.py:618
  57.8 7.5 %copy-start.8 = (bf16[32,256]{1,0:T(8,128)(2,1)S(1)}, bf16[32,256]{1,0:T(8,128)(2,1)}, u32[]{:S(2)}) copy-start(bf16[32,256]{1,0:T(8,128)(2,1)} %refs_16_.1) | copy-start | bytes 49156
  57.8 7.5 %copy-start.9 = (f32[8]{0:T(128)S(1)}, f32[8]{0:T(128)}, u32[]{:S(2)}) copy-start(f32[8]{0:T(128)} %sharpness.1) | copy-start | bytes 100
  57.8 5.9 %collective-permute-start.12 = (f32[152,256]{1,0:T(8,128)S(1)}, f32[152,256]{1,0:T(8,128)S(1)}, u32[]{:S(2)}, u32[]{:S(2)}) collective-permute-start(f32[152,256]{1,0:T(8,128)S(1)} %mix_back.1.refs_0_), channel_id=1, source_target_pairs={{0,4},{1,5},{2,6},{3,7},{4,0},{5,1},{6,2},{7,3},{8,12},{9,13},{10,... | collective-permute-start | bytes 466952 | tf_op jit(solution)/shard_map/ppermute | solution.py:618
  63.1 7.4 %collective-permute-start.16 = (f32[2,144,256]{2,1,0:T(8,128)S(1)}, f32[2,144,256]{2,1,0:T(8,128)S(1)}, u32[]{:S(2)}, u32[]{:S(2)}) collective-permute-start(f32[2,144,256]{2,1,0:T(8,128)S(1)} %get-tuple-element.99), channel_id=1, source_target_pairs={{0,4},{1,5},{2,6},{3,7},{4,0},{5,1},{6,2},{7,3},{8,12},{9,13},{10,... | collective-permute-start | bytes 884744 | tf_op jit(solution)/shard_map/ppermute | solution.py:618
  63.6 1.4 %collective-permute-start.13 = (f32[152,256]{1,0:T(8,128)S(1)}, f32[152,256]{1,0:T(8,128)S(1)}, u32[]{:S(2)}, u32[]{:S(2)}) collective-permute-start(f32[152,256]{1,0:T(8,128)S(1)} %mix_back.1.refs_0_), channel_id=1, source_target_pairs={{0,1},{1,0},{2,3},{3,2},{4,5},{5,4},{6,7},{7,6},{8,9},{9,8},{10,11... | collective-permute-start | bytes 466952 | tf_op jit(solution)/shard_map/ppermute | solution.py:618
  63.7 1.6 %collective-permute-start.14 = (f32[152,256]{1,0:T(8,128)S(1)}, f32[152,256]{1,0:T(8,128)S(1)}, u32[]{:S(2)}, u32[]{:S(2)}) collective-permute-start(f32[152,256]{1,0:T(8,128)S(1)} %collective-permute-done.12.refs_1_), channel_id=1, source_target_pairs={{0,1},{1,0},{2,3},{3,2},{4,5},{5,4},{6,7},{7,6},{8,9},{9,8},{10,11... | collective-permute-start | bytes 466952 | tf_op jit(solution)/shard_map/ppermute | solution.py:618
  70.5 1.6 %collective-permute-start.17 = (f32[288,256]{1,0:T(8,128)S(1)}, f32[288,256]{1,0:T(8,128)S(1)}, u32[]{:S(2)}, u32[]{:S(2)}) collective-permute-start(f32[288,256]{1,0:T(8,128)S(1)} %get-tuple-element.85), channel_id=1, source_target_pairs={{0,1},{1,0},{2,3},{3,2},{4,5},{5,4},{6,7},{7,6},{8,9},{9,8},{10,11... | collective-permute-start | bytes 884744 | tf_op jit(solution)/shard_map/ppermute | solution.py:618
  72.1 6.5 %collective-permute-start.18 = (f32[160,256]{1,0:T(8,128)S(1)}, f32[160,256]{1,0:T(8,128)S(1)}, u32[]{:S(2)}, u32[]{:S(2)}) collective-permute-start(f32[160,256]{1,0:T(8,128)S(1)} %pad_maximum_fusion), channel_id=1, source_target_pairs={{0,2},{1,3},{2,0},{3,1},{4,6},{5,7},{6,4},{7,5},{8,10},{9,11},{10,... | collective-permute-start | bytes 491528 | tf_op jit(solution)/shard_map/ppermute | solution.py:618
  73.4 10.7 %collective-permute-start.20 = (f32[1,144,256]{2,1,0:T(8,128)S(1)}, f32[1,144,256]{2,1,0:T(8,128)S(1)}, u32[]{:S(2)}, u32[]{:S(2)}) collective-permute-start(f32[1,144,256]{2,1,0:T(8,128)S(1)} %get-tuple-element.100), channel_id=1, source_target_pairs={{0,8},{1,9},{2,10},{3,11},{4,12},{5,13},{6,14},{7,15},{8,0},{9,1},... | collective-permute-start | bytes 442376 | tf_op jit(solution)/shard_map/ppermute | solution.py:618
  78.6 7.3 %collective-permute-start.19 = (f32[96,256]{1,0:T(8,128)S(1)}, f32[96,256]{1,0:T(8,128)S(1)}, u32[]{:S(2)}, u32[]{:S(2)}) collective-permute-start(f32[96,256]{1,0:T(8,128)S(1)} %pad_maximum_fusion.1), channel_id=1, source_target_pairs={{0,4},{1,5},{2,6},{3,7},{4,0},{5,1},{6,2},{7,3},{8,12},{9,13},{10,... | collective-permute-start | bytes 294920 | tf_op jit(solution)/shard_map/ppermute | solution.py:618
  85.9 5.4 %collective-permute-start.21 = (f32[64,256]{1,0:T(8,128)S(1)}, f32[64,256]{1,0:T(8,128)S(1)}, u32[]{:S(2)}, u32[]{:S(2)}) collective-permute-start(f32[64,256]{1,0:T(8,128)S(1)} %pad_maximum_fusion.2), channel_id=1, source_target_pairs={{0,8},{1,9},{2,10},{3,11},{4,12},{5,13},{6,14},{7,15},{8,0},{9,1},... | collective-permute-start | bytes 196616 | tf_op jit(solution)/shard_map/ppermute | solution.py:618

commit v6 on v5

--- a/solution.py
+++ b/solution.py
@@ -531,16 +531,19 @@
     out[...] = left[...] + right[...]
 
 
-def finish_kernel(main_keep, main_got, slice_sum, value, feat, mid, slice_out, out, up, down):
+def finish_kernel(keep, got, slice_sum, feat, mid, slice_out):
+    step = feat.shape[0]
+    feat[...] = keep[:step, :] + got[:step, :]
+    mid[...] = keep[step:, :] + got[step : 2 * step, :]
+    slice_out[...] = slice_sum[...] + got[2 * step :, :]
+
+
+def place_kernel(value, out, up, down):
     step, model = out.shape
-    feat[...] = main_keep[:step, :] + main_got[:step, :]
-    mid[...] = main_keep[step:, :] + main_got[step : 2 * step, :]
-    slice_out[...] = slice_sum[...] + main_got[2 * step :, :]
     wide = up.shape[1] // model
     out[...] = value[0, :step, :]
     for w in range(wide):
-        at = slice(step * (1 + w), step * (2 + w))
-        up[:, w * model : (w + 1) * model] = value[0, at, :]
+        up[:, w * model : (w + 1) * model] = value[0, step * (1 + w) : step * (2 + w), :]
     down[...] = value[0, step * (1 + wide) :, :]
 
 
@@ -548,7 +551,7 @@
 SMEM = pl.BlockSpec(memory_space=pltpu.SMEM)
 HBM = pl.BlockSpec(memory_space=pltpu.HBM)
 MIB = 1024 * 1024
-COSTS = {"point_back": 0.001, "mix_back": 0.001, "add": 12.0}
+COSTS = {"point_back": 0.5, "mix_back": 0.001, "add": 12.0}
 
 
 def shape(dims, dtype=F32):
@@ -837,24 +840,25 @@
         count = keep.shape[0] // 2
         send = jnp.concatenate([keep[count:] + got[count : 2 * count], slice_sum], axis=0)
         keep = keep[:count] + got[:count]
-    grad_feat, grad_mid, grad_slice, grad_out, grad_up, grad_down = run(
+    grad_out, grad_up, grad_down = run(
+        place_kernel,
+        "place",
+        4,
+        VMEM,
+        (shape((step, model)), shape((step, hidden_width)), shape((step * wide, model))),
+        [],
+        outer,
+    )
+    grad_feat, grad_mid, grad_slice = run(
         finish_kernel,
         "finish",
         4,
         VMEM,
-        (
-            shape((step, model)),
-            shape((step, model)),
-            shape((width, slices)),
-            shape((step, model)),
-            shape((step, hidden_width)),
-            shape((step * wide, model)),
-        ),
+        (shape((step, model)), shape((step, model)), shape((width, slices))),
         [],
         keep,
         got,
         slice_sum,
-        outer,
     )
     return (layer_out, grad_feat, grad_mid, grad_out, grad_up, grad_down, grad_slice, grad_mix)
 

time: 92.1 us -> 92.1 us (level)
    pallas_call x8 -> x9, Pallas kernels: 16.9 us -> 17.5 us  [run(): pl.pallas_call(body, out_shape=out_shape, in_specs=[first] + [rest] * (le...]
  transfers between devices with their start and end apart: 22 -> 22, of which waited for: 18 -> 18; matrix products, arithmetic and copies ran while one was open for 0% -> 0% of each run, Pallas kernels for 7% -> 8%
where the time goes in v6:
time: 92.1 us; the launch traced here: 91.9 us
  waiting for transfers between devices  50.4 us (55%)
  starting transfers between devices  21.8 us (24%)
  Pallas kernels  17.5 us (19%)
  between operations  1.55 us (2%)
    ppermute x22, waiting for transfers between devices, exchange(): return lax.ppermute(value, 'pts', [(i, i ^ 1 << bit) for i in range(parts)])  50.4 us
    ppermute x22, starting transfers between devices, exchange(): return lax.ppermute(value, 'pts', [(i, i ^ 1 << bit) for i in range(parts)])  21.8 us
    pallas_call x9, Pallas kernels, run(): pl.pallas_call(body, out_shape=out_shape, in_specs=[first] + [rest] * (le...  17.5 us
  transfers between devices with their start and end apart: 22, of which 18 were waited for; matrix products, arithmetic and copies ran while one was open for 0% of the time, Pallas kernels for 8%

profile of v6, /device:TPU:0, one launch (start us, length us, event | category | flops | bytes accessed | tf_op | source)
XLA Modules:
  0.0 91.9 jit_solution(14272681673995189605)
XLA Ops:
  1.3 0.0 copy-start.5
  1.3 0.0 copy-start.6
  1.3 0.0 copy-start.7
  1.3 0.0 copy-start
  1.3 0.0 copy-start.1
  1.3 0.0 copy-start.2
  1.4 4.8 %slice_sums.1 = (f32[2,136,256]{2,1,0:T(8,128)S(1)}, f32[2,136,256]{2,1,0:T(8,128)S(1)}, bf16[256,768]{1,0:T(8,128)(2,1)S(1)}, bf16[256,768]{1,0:T(8,128)(2,1)S(...) custom-call(s32[1]{0:T(128)S(6)} %copy.24.counts_hbm, ...), custom_call_target="tpu_custom_call" | custom-call | tf_op jit(solution)/shard_map/slice_sums/pallas_call | solution.py:572
  6.2 0.5 collective-permute-start
  6.7 1.2 %collective-permute-done = f32[2,136,256]{2,1,0:T(8,128)S(1)} collective-permute-done((f32[2,136,256]{2,1,0:T(8,128)S(1)}, f32[2,136,256]{2,1,0:T(8,128)S(1)}, u32[]{:S(2)}, u32[]{:S(2)}) %collective-permute-start) | collective-permute-done | bytes 278560 | tf_op jit(solution)/shard_map/ppermute | solution.py:621
  7.9 3.0 %collective-permute-start.1 = (f32[1,136,256]{2,1,0:T(8,128)S(1)}, f32[1,136,256]{2,1,0:T(8,128)S(1)}, u32[]{:S(2)}, u32[]{:S(2)}) collective-permute-start(f32[1,136,256]{2,1,0:T(8,128)S(1)} %slice_add_fusion.6), channel_id=1, source_target_pairs={{0,4},{1,5},{2,6},{3,7},{4,0},{5,1},{6,2},{7,3},{8,12},{9,13},{10,... | collective-permute-start | bytes 417800 | tf_op jit(solution)/shard_map/ppermute | solution.py:621
  10.9 4.0 %collective-permute-done.1 = f32[1,136,256]{2,1,0:T(8,128)S(1)} collective-permute-done((f32[1,136,256]{2,1,0:T(8,128)S(1)}, f32[1,136,256]{2,1,0:T(8,128)S(1)}, u32[]{:S(2)}, u32[]{:S(2)}) %collective-permute-start.1) | collective-permute-done | bytes 139296 | tf_op jit(solution)/shard_map/ppermute | solution.py:621
  14.9 1.7 %collective-permute-start.2 = (f32[136,256]{1,0:T(8,128)S(1)}, f32[136,256]{1,0:T(8,128)S(1)}, u32[]{:S(2)}, u32[]{:S(2)}) collective-permute-start(f32[136,256]{1,0:T(8,128)S(1)} %fusion.1), channel_id=1, source_target_pairs={{0,2},{1,3},{2,0},{3,1},{4,6},{5,7},{6,4},{7,5},{8,10},{9,11},{10,... | collective-permute-start | bytes 417800 | tf_op jit(solution)/shard_map/ppermute | solution.py:621
  16.7 3.5 %collective-permute-done.2 = f32[136,256]{1,0:T(8,128)S(1)} collective-permute-done((f32[136,256]{1,0:T(8,128)S(1)}, f32[136,256]{1,0:T(8,128)S(1)}, u32[]{:S(2)}, u32[]{:S(2)}) %collective-permute-start.2) | collective-permute-done | bytes 139296 | tf_op jit(solution)/shard_map/ppermute | solution.py:621
  20.2 2.7 %collective-permute-start.3 = (f32[136,256]{1,0:T(8,128)S(1)}, f32[136,256]{1,0:T(8,128)S(1)}, u32[]{:S(2)}, u32[]{:S(2)}) collective-permute-start(f32[136,256]{1,0:T(8,128)S(1)} %add.79), channel_id=1, source_target_pairs={{0,8},{1,9},{2,10},{3,11},{4,12},{5,13},{6,14},{7,15},{8,0},{9,1},... | collective-permute-start | bytes 417800 | tf_op jit(solution)/shard_map/ppermute | solution.py:621
  22.9 5.6 %collective-permute-done.3 = f32[136,256]{1,0:T(8,128)S(1)} collective-permute-done((f32[136,256]{1,0:T(8,128)S(1)}, f32[136,256]{1,0:T(8,128)S(1)}, u32[]{:S(2)}, u32[]{:S(2)}) %collective-permute-start.3) | collective-permute-done | bytes 139296 | tf_op jit(solution)/shard_map/ppermute | solution.py:621
  28.5 1.1 %mix_tokens.1 = (f32[64,256]{1,0:T(8,128)S(1)}, f32[2,512,256]{2,1,0:T(8,128)S(1)}, f32[2,96,512]{2,1,0:T(8,128)S(1)}) custom-call(f32[136,256]{1,0:T(8,128)S(1)} %add.80.tokens, f32[32,32]{1,0:T(8,128)S(1)} %copy-done.5, f32[32,32]{1,0:T(8,128)S(1)} %copy-done.6, f32[32,32]{1,0:T(8,128)S(1)} %copy-done.7), custom_call_target="tpu_custom_call" | custom-call | tf_op jit(solution)/shard_map/mix_tokens/pallas_call | solution.py:572
  29.7 0.1 collective-permute-start.4
  29.8 0.0 collective-permute-start.5
  29.8 4.1 %collective-permute-done.4.refs_1_.refs_5_ = f32[64,256]{1,0:T(8,128)S(1)} collective-permute-done((f32[64,256]{1,0:T(8,128)S(1)}, f32[64,256]{1,0:T(8,128)S(1)}, u32[]{:S(2)}, u32[]{:S(2)}) %collective-permute-start.4) | collective-permute-done | bytes 65568 | tf_op jit(solution)/shard_map/ppermute | solution.py:621
  34.0 0.0 collective-permute-start.6
  34.0 0.0 collective-permute-done.5.refs_2_.refs_6_
  34.0 1.2 %collective-permute-done.6.refs_3_.refs_7_ = f32[64,256]{1,0:T(8,128)S(1)} collective-permute-done((f32[64,256]{1,0:T(8,128)S(1)}, f32[64,256]{1,0:T(8,128)S(1)}, u32[]{:S(2)}, u32[]{:S(2)}) %collective-permute-start.6) | collective-permute-done | bytes 65568 | tf_op jit(solution)/shard_map/ppermute | solution.py:621
  35.2 0.0 copy-done.3
  35.2 0.0 copy-done.4
  35.2 0.0 copy-done.10
  35.3 2.9 %mlp.1 = (bf16[256,256]{1,0:T(8,128)(2,1)}, bf16[256,256]{1,0:T(8,128)(2,1)S(1)}, f32[2,64,256]{2,1,0:T(8,128)S(1)}, f32[2,64,256]{2,1,0:T(8,128)S(1)}, bf16[256...) custom-call(f32[64,256]{1,0:T(8,128)S(1)} %get-tuple-element.54.refs, ...), custom_call_target="tpu_custom_call" | custom-call | tf_op jit(solution)/shard_map/mlp/pallas_call | solution.py:572
  38.2 0.2 collective-permute-start.7
  38.4 1.2 %collective-permute-done.7 = f32[2,64,256]{2,1,0:T(8,128)S(1)} collective-permute-done((f32[2,64,256]{2,1,0:T(8,128)S(1)}, f32[2,64,256]{2,1,0:T(8,128)S(1)}, u32[]{:S(2)}, u32[]{:S(2)}) %collective-permute-start.7) | collective-permute-done | bytes 131104 | tf_op jit(solution)/shard_map/ppermute | solution.py:621
  39.5 0.6 weight_grads.1
  40.1 0.2 collective-permute-start.10
  40.4 0.2 collective-permute-start.8
  40.5 4.2 %collective-permute-done.8 = f32[1,64,256]{2,1,0:T(8,128)S(1)} collective-permute-done((f32[1,64,256]{2,1,0:T(8,128)S(1)}, f32[1,64,256]{2,1,0:T(8,128)S(1)}, u32[]{:S(2)}, u32[]{:S(2)}) %collective-permute-start.8) | collective-permute-done | bytes 65568 | tf_op jit(solution)/shard_map/ppermute | solution.py:621
  44.8 1.0 %collective-permute-start.9 = (f32[64,256]{1,0:T(8,128)S(1)}, f32[64,256]{1,0:T(8,128)S(1)}, u32[]{:S(2)}, u32[]{:S(2)}) collective-permute-start(f32[64,256]{1,0:T(8,128)S(1)} %add_bitcast_fusion), channel_id=1, source_target_pairs={{0,2},{1,3},{2,0},{3,1},{4,6},{5,7},{6,4},{7,5},{8,10},{9,11},{10,... | collective-permute-start | bytes 196616 | tf_op jit(solution)/shard_map/ppermute | solution.py:621
  45.8 3.3 %collective-permute-done.9 = f32[64,256]{1,0:T(8,128)S(1)} collective-permute-done((f32[64,256]{1,0:T(8,128)S(1)}, f32[64,256]{1,0:T(8,128)S(1)}, u32[]{:S(2)}, u32[]{:S(2)}) %collective-permute-start.9) | collective-permute-done | bytes 65568 | tf_op jit(solution)/shard_map/ppermute | solution.py:621
  49.1 0.0 collective-permute-done.10
  49.1 0.2 slice_add_fusion.1
  49.3 1.0 %collective-permute-start.15 = (f32[4,144,256]{2,1,0:T(8,128)S(1)}, f32[4,144,256]{2,1,0:T(8,128)S(1)}, u32[]{:S(2)}, u32[]{:S(2)}) collective-permute-start(f32[4,144,256]{2,1,0:T(8,128)S(1)} %get-tuple-element.97), channel_id=1, source_target_pairs={{0,2},{1,3},{2,0},{3,1},{4,6},{5,7},{6,4},{7,5},{8,10},{9,11},{10,... | collective-permute-start | bytes 1769480 | tf_op jit(solution)/shard_map/ppermute | solution.py:621
  50.3 2.3 %collective-permute-start.11 = (f32[64,256]{1,0:T(8,128)S(1)}, f32[64,256]{1,0:T(8,128)S(1)}, u32[]{:S(2)}, u32[]{:S(2)}) collective-permute-start(f32[64,256]{1,0:T(8,128)S(1)} %add.84), channel_id=1, source_target_pairs={{0,8},{1,9},{2,10},{3,11},{4,12},{5,13},{6,14},{7,15},{8,0},{9,1},... | collective-permute-start | bytes 196616 | tf_op jit(solution)/shard_map/ppermute | solution.py:621
  52.7 3.6 %collective-permute-done.11 = f32[64,256]{1,0:T(8,128)S(1)} collective-permute-done((f32[64,256]{1,0:T(8,128)S(1)}, f32[64,256]{1,0:T(8,128)S(1)}, u32[]{:S(2)}, u32[]{:S(2)}) %collective-permute-start.11) | collective-permute-done | bytes 65568 | tf_op jit(solution)/shard_map/ppermute | solution.py:621
  56.2 1.5 %mix_back.1.refs_0_ = f32[152,256]{1,0:T(8,128)S(1)} custom-call(f32[136,256]{1,0:T(8,128)S(1)} %add.80.tokens, f32[2,512,256]{2,1,0:T(8,128)S(1)} %get-tuple-element.57.attention_in, f32[2,96,512]{2,1,0:T(8,128)S(1)} %get-tuple-element.58.kept, f32[64,256]{1,0:T(8,128)S(1)} %add.85.grad, f32[32,32]{1,0:T(8,128)S(1)} %copy-done.5, f32[32,32]{1,0:T(8,128)S(1)} %copy-done.6, ...), custom_call_target="tpu_custom_call" | custom-call | flops 1000000 | tf_op jit(solution)/shard_map/mix_back/pallas_call | solution.py:572
  57.8 0.0 copy-start.9
  57.8 0.6 collective-permute-start.12
  58.4 4.6 %collective-permute-done.15 = f32[4,144,256]{2,1,0:T(8,128)S(1)} collective-permute-done((f32[4,144,256]{2,1,0:T(8,128)S(1)}, f32[4,144,256]{2,1,0:T(8,128)S(1)}, u32[]{:S(2)}, u32[]{:S(2)}) %collective-permute-start.15) | collective-permute-done | bytes 589856 | tf_op jit(solution)/shard_map/ppermute | solution.py:621
  63.0 0.1 slice_add_fusion.2
  63.1 0.5 collective-permute-start.16
  63.6 0.0 collective-permute-start.13
  63.6 0.0 collective-permute-done.12.refs_1_
  63.7 0.5 collective-permute-start.14
  64.2 0.9 collective-permute-done.13.refs_2_
  65.0 0.2 collective-permute-done.14.refs_3_
  65.3 5.2 %point_back.1 = (f32[16,16,256]{2,1,0:T(8,128)S(1)}, f32[288,256]{1,0:T(8,128)S(1)}, f32[3,32,32]{2,1,0:T(8,128)}) custom-call(f32[8]{0:T(128)S(1)} %copy-done.9, f32[152,256]{1,0:T(8,128)S(1)} %mix_back.1.refs_0_, f32[152,256]{1,0:T(8,128)S(1)} %collective-permute-done.12.refs_1_, f32[152,256]{1,0:T(8,128)S(1)} %collective-permute-done.13.refs_2_, ...), custom_call_target="tpu_custom_call" | custom-call | flops 500000000 | tf_op jit(solution)/shard_map/point_back/pallas_call | solution.py:572
  70.5 0.0 collective-permute-done.16
  70.5 0.3 collective-permute-start.17
  70.8 1.3 %collective-permute-done.17 = f32[288,256]{1,0:T(8,128)S(1)} collective-permute-done((f32[288,256]{1,0:T(8,128)S(1)}, f32[288,256]{1,0:T(8,128)S(1)}, u32[]{:S(2)}, u32[]{:S(2)}) %collective-permute-start.17) | collective-permute-done | bytes 294944 | tf_op jit(solution)/shard_map/ppermute | solution.py:621
  72.1 1.2 %collective-permute-start.18 = (f32[160,256]{1,0:T(8,128)S(1)}, f32[160,256]{1,0:T(8,128)S(1)}, u32[]{:S(2)}, u32[]{:S(2)}) collective-permute-start(f32[160,256]{1,0:T(8,128)S(1)} %pad_maximum_fusion), channel_id=1, source_target_pairs={{0,2},{1,3},{2,0},{3,1},{4,6},{5,7},{6,4},{7,5},{8,10},{9,11},{10,... | collective-permute-start | bytes 491528 | tf_op jit(solution)/shard_map/ppermute | solution.py:621
  73.4 3.4 %collective-permute-start.20 = (f32[1,144,256]{2,1,0:T(8,128)S(1)}, f32[1,144,256]{2,1,0:T(8,128)S(1)}, u32[]{:S(2)}, u32[]{:S(2)}) collective-permute-start(f32[1,144,256]{2,1,0:T(8,128)S(1)} %get-tuple-element.100), channel_id=1, source_target_pairs={{0,8},{1,9},{2,10},{3,11},{4,12},{5,13},{6,14},{7,15},{8,0},{9,1},... | collective-permute-start | bytes 442376 | tf_op jit(solution)/shard_map/ppermute | solution.py:621
  76.8 1.7 %collective-permute-done.18 = f32[160,256]{1,0:T(8,128)S(1)} collective-permute-done((f32[160,256]{1,0:T(8,128)S(1)}, f32[160,256]{1,0:T(8,128)S(1)}, u32[]{:S(2)}, u32[]{:S(2)}) %collective-permute-start.18) | collective-permute-done | bytes 163872 | tf_op jit(solution)/shard_map/ppermute | solution.py:621
  78.6 1.6 %collective-permute-start.19 = (f32[96,256]{1,0:T(8,128)S(1)}, f32[96,256]{1,0:T(8,128)S(1)}, u32[]{:S(2)}, u32[]{:S(2)}) collective-permute-start(f32[96,256]{1,0:T(8,128)S(1)} %pad_maximum_fusion.1), channel_id=1, source_target_pairs={{0,4},{1,5},{2,6},{3,7},{4,0},{5,1},{6,2},{7,3},{8,12},{9,13},{10,... | collective-permute-start | bytes 294920 | tf_op jit(solution)/shard_map/ppermute | solution.py:621
  80.2 3.9 %collective-permute-done.20.right = f32[1,144,256]{2,1,0:T(8,128)S(1)} collective-permute-done((f32[1,144,256]{2,1,0:T(8,128)S(1)}, f32[1,144,256]{2,1,0:T(8,128)S(1)}, u32[]{:S(2)}, u32[]{:S(2)}) %collective-permute-start.20) | collective-permute-done | bytes 147488 | tf_op jit(solution)/shard_map/ppermute | solution.py:621
  84.2 1.7 %collective-permute-done.19 = f32[96,256]{1,0:T(8,128)S(1)} collective-permute-done((f32[96,256]{1,0:T(8,128)S(1)}, f32[96,256]{1,0:T(8,128)S(1)}, u32[]{:S(2)}, u32[]{:S(2)}) %collective-permute-start.19) | collective-permute-done | bytes 98336 | tf_op jit(solution)/shard_map/ppermute | solution.py:621
  85.9 0.5 collective-permute-start.21
  86.5 0.7 place.1
  87.1 4.2 %collective-permute-done.21.got = f32[64,256]{1,0:T(8,128)S(1)} collective-permute-done((f32[64,256]{1,0:T(8,128)S(1)}, f32[64,256]{1,0:T(8,128)S(1)}, u32[]{:S(2)}, u32[]{:S(2)}) %collective-permute-start.21) | collective-permute-done | bytes 65568 | tf_op jit(solution)/shard_map/ppermute | solution.py:621
  91.3 0.6 finish.1
  (31 shorter events, 0.3 us)
Async XLA Ops:
  1.3 27.2 %copy-start.5 = (f32[32,32]{1,0:T(8,128)S(1)}, f32[32,32]{1,0:T(8,128)}, u32[]{:S(2)}) copy-start(f32[32,32]{1,0:T(8,128)} %w_query.3) | copy-start | bytes 12292
  1.3 27.2 %copy-start.6 = (f32[32,32]{1,0:T(8,128)S(1)}, f32[32,32]{1,0:T(8,128)}, u32[]{:S(2)}) copy-start(f32[32,32]{1,0:T(8,128)} %w_key.3) | copy-start | bytes 12292
  1.3 27.2 %copy-start.7 = (f32[32,32]{1,0:T(8,128)S(1)}, f32[32,32]{1,0:T(8,128)}, u32[]{:S(2)}) copy-start(f32[32,32]{1,0:T(8,128)} %w_value.3) | copy-start | bytes 12292
  1.3 33.9 %copy-start = (bf16[256,1024]{1,0:T(8,128)(2,1)S(1)}, bf16[256,1024]{1,0:T(8,128)(2,1)}, u32[]{:S(2)}) copy-start(bf16[256,1024]{1,0:T(8,128)(2,1)} %refs_9_.1) | copy-start | bytes 1572868
  1.3 33.9 %copy-start.1 = (bf16[1024,256]{1,0:T(8,128)(2,1)S(1)}, bf16[1024,256]{1,0:T(8,128)(2,1)}, u32[]{:S(2)}) copy-start(bf16[1024,256]{1,0:T(8,128)(2,1)} %refs_10_.1) | copy-start | bytes 1572868
  1.3 33.9 %copy-start.2 = (bf16[256,256]{1,0:T(8,128)(2,1)S(1)}, bf16[256,256]{1,0:T(8,128)(2,1)}, u32[]{:S(2)}) copy-start(bf16[256,256]{1,0:T(8,128)(2,1)} %cotangent.1) | copy-start | bytes 393220
  1.3 33.9 %copy-start.3 = (bf16[256,256]{1,0:T(8,128)(2,1)S(1)}, bf16[256,256]{1,0:T(8,128)(2,1)}, u32[]{:S(2)}) copy-start(bf16[256,256]{1,0:T(8,128)(2,1)} %refs_5_.1) | copy-start | bytes 393220
  1.4 33.9 %copy-start.4 = (bf16[256,256]{1,0:T(8,128)(2,1)S(1)}, bf16[256,256]{1,0:T(8,128)(2,1)}, u32[]{:S(2)}) copy-start(bf16[256,256]{1,0:T(8,128)(2,1)} %refs_7_.1) | copy-start | bytes 393220
  1.4 33.9 %copy-start.10 = (f32[256]{0:T(256)S(1)}, f32[256]{0:T(256)}, u32[]{:S(2)}) copy-start(f32[256]{0:T(256)} %refs_8_.1) | copy-start | bytes 3076
  6.2 1.7 %collective-permute-start = (f32[2,136,256]{2,1,0:T(8,128)S(1)}, f32[2,136,256]{2,1,0:T(8,128)S(1)}, u32[]{:S(2)}, u32[]{:S(2)}) collective-permute-start(f32[2,136,256]{2,1,0:T(8,128)S(1)} %get-tuple-element.53), channel_id=1, source_target_pairs={{0,1},{1,0},{2,3},{3,2},{4,5},{5,4},{6,7},{7,6},{8,9},{9,8},{10,11... | collective-permute-start | bytes 835592 | tf_op jit(solution)/shard_map/ppermute | solution.py:621
  7.9 7.0 %collective-permute-start.1 = (f32[1,136,256]{2,1,0:T(8,128)S(1)}, f32[1,136,256]{2,1,0:T(8,128)S(1)}, u32[]{:S(2)}, u32[]{:S(2)}) collective-permute-start(f32[1,136,256]{2,1,0:T(8,128)S(1)} %slice_add_fusion.6), channel_id=1, source_target_pairs={{0,4},{1,5},{2,6},{3,7},{4,0},{5,1},{6,2},{7,3},{8,12},{9,13},{10,... | collective-permute-start | bytes 417800 | tf_op jit(solution)/shard_map/ppermute | solution.py:621
  14.9 5.3 %collective-permute-start.2 = (f32[136,256]{1,0:T(8,128)S(1)}, f32[136,256]{1,0:T(8,128)S(1)}, u32[]{:S(2)}, u32[]{:S(2)}) collective-permute-start(f32[136,256]{1,0:T(8,128)S(1)} %fusion.1), channel_id=1, source_target_pairs={{0,2},{1,3},{2,0},{3,1},{4,6},{5,7},{6,4},{7,5},{8,10},{9,11},{10,... | collective-permute-start | bytes 417800 | tf_op jit(solution)/shard_map/ppermute | solution.py:621
  20.2 8.3 %collective-permute-start.3 = (f32[136,256]{1,0:T(8,128)S(1)}, f32[136,256]{1,0:T(8,128)S(1)}, u32[]{:S(2)}, u32[]{:S(2)}) collective-permute-start(f32[136,256]{1,0:T(8,128)S(1)} %add.79), channel_id=1, source_target_pairs={{0,8},{1,9},{2,10},{3,11},{4,12},{5,13},{6,14},{7,15},{8,0},{9,1},... | collective-permute-start | bytes 417800 | tf_op jit(solution)/shard_map/ppermute | solution.py:621
  29.7 4.3 %collective-permute-start.4 = (f32[64,256]{1,0:T(8,128)S(1)}, f32[64,256]{1,0:T(8,128)S(1)}, u32[]{:S(2)}, u32[]{:S(2)}) collective-permute-start(f32[64,256]{1,0:T(8,128)S(1)} %get-tuple-element.54.refs_0_.refs_4_), channel_id=1, source_target_pairs={{0,4},{1,5},{2,6},{3,7},{4,0},{5,1},{6,2},{7,3},{8,12},{9,13},{10,... | collective-permute-start | bytes 196616 | tf_op jit(solution)/shard_map/ppermute | solution.py:621
  29.8 4.1 %collective-permute-start.5 = (f32[64,256]{1,0:T(8,128)S(1)}, f32[64,256]{1,0:T(8,128)S(1)}, u32[]{:S(2)}, u32[]{:S(2)}) collective-permute-start(f32[64,256]{1,0:T(8,128)S(1)} %get-tuple-element.54.refs_0_.refs_4_), channel_id=1, source_target_pairs={{0,1},{1,0},{2,3},{3,2},{4,5},{5,4},{6,7},{7,6},{8,9},{9,8},{10,11... | collective-permute-start | bytes 196616 | tf_op jit(solution)/shard_map/ppermute | solution.py:621
  34.0 1.3 %collective-permute-start.6 = (f32[64,256]{1,0:T(8,128)S(1)}, f32[64,256]{1,0:T(8,128)S(1)}, u32[]{:S(2)}, u32[]{:S(2)}) collective-permute-start(f32[64,256]{1,0:T(8,128)S(1)} %collective-permute-done.4.refs_1_.refs_5_), channel_id=1, source_target_pairs={{0,1},{1,0},{2,3},{3,2},{4,5},{5,4},{6,7},{7,6},{8,9},{9,8},{10,11... | collective-permute-start | bytes 196616 | tf_op jit(solution)/shard_map/ppermute | solution.py:621
  38.2 1.3 %collective-permute-start.7 = (f32[2,64,256]{2,1,0:T(8,128)S(1)}, f32[2,64,256]{2,1,0:T(8,128)S(1)}, u32[]{:S(2)}, u32[]{:S(2)}) collective-permute-start(f32[2,64,256]{2,1,0:T(8,128)S(1)} %get-tuple-element.65), channel_id=1, source_target_pairs={{0,1},{1,0},{2,3},{3,2},{4,5},{5,4},{6,7},{7,6},{8,9},{9,8},{10,11... | collective-permute-start | bytes 393224 | tf_op jit(solution)/shard_map/ppermute | solution.py:621
  40.1 9.0 %collective-permute-start.10 = (f32[8,144,256]{2,1,0:T(8,128)S(1)}, f32[8,144,256]{2,1,0:T(8,128)S(1)}, u32[]{:S(2)}, u32[]{:S(2)}) collective-permute-start(f32[8,144,256]{2,1,0:T(8,128)S(1)} %get-tuple-element.72), channel_id=1, source_target_pairs={{0,1},{1,0},{2,3},{3,2},{4,5},{5,4},{6,7},{7,6},{8,9},{9,8},{10,11... | collective-permute-start | bytes 3538952 | tf_op jit(solution)/shard_map/ppermute | solution.py:621
  40.4 4.4 %collective-permute-start.8 = (f32[1,64,256]{2,1,0:T(8,128)S(1)}, f32[1,64,256]{2,1,0:T(8,128)S(1)}, u32[]{:S(2)}, u32[]{:S(2)}) collective-permute-start(f32[1,64,256]{2,1,0:T(8,128)S(1)} %slice_add_fusion.12), channel_id=1, source_target_pairs={{0,4},{1,5},{2,6},{3,7},{4,0},{5,1},{6,2},{7,3},{8,12},{9,13},{10,... | collective-permute-start | bytes 196616 | tf_op jit(solution)/shard_map/ppermute | solution.py:621
  44.8 4.3 %collective-permute-start.9 = (f32[64,256]{1,0:T(8,128)S(1)}, f32[64,256]{1,0:T(8,128)S(1)}, u32[]{:S(2)}, u32[]{:S(2)}) collective-permute-start(f32[64,256]{1,0:T(8,128)S(1)} %add_bitcast_fusion), channel_id=1, source_target_pairs={{0,2},{1,3},{2,0},{3,1},{4,6},{5,7},{6,4},{7,5},{8,10},{9,11},{10,... | collective-permute-start | bytes 196616 | tf_op jit(solution)/shard_map/ppermute | solution.py:621
  49.3 13.7 %collective-permute-start.15 = (f32[4,144,256]{2,1,0:T(8,128)S(1)}, f32[4,144,256]{2,1,0:T(8,128)S(1)}, u32[]{:S(2)}, u32[]{:S(2)}) collective-permute-start(f32[4,144,256]{2,1,0:T(8,128)S(1)} %get-tuple-element.97), channel_id=1, source_target_pairs={{0,2},{1,3},{2,0},{3,1},{4,6},{5,7},{6,4},{7,5},{8,10},{9,11},{10,... | collective-permute-start | bytes 1769480 | tf_op jit(solution)/shard_map/ppermute | solution.py:621
  50.3 5.9 %collective-permute-start.11 = (f32[64,256]{1,0:T(8,128)S(1)}, f32[64,256]{1,0:T(8,128)S(1)}, u32[]{:S(2)}, u32[]{:S(2)}) collective-permute-start(f32[64,256]{1,0:T(8,128)S(1)} %add.84), channel_id=1, source_target_pairs={{0,8},{1,9},{2,10},{3,11},{4,12},{5,13},{6,14},{7,15},{8,0},{9,1},... | collective-permute-start | bytes 196616 | tf_op jit(solution)/shard_map/ppermute | solution.py:621
  57.8 7.5 %copy-start.8 = (bf16[32,256]{1,0:T(8,128)(2,1)S(1)}, bf16[32,256]{1,0:T(8,128)(2,1)}, u32[]{:S(2)}) copy-start(bf16[32,256]{1,0:T(8,128)(2,1)} %refs_16_.1) | copy-start | bytes 49156
  57.8 7.5 %copy-start.9 = (f32[8]{0:T(128)S(1)}, f32[8]{0:T(128)}, u32[]{:S(2)}) copy-start(f32[8]{0:T(128)} %sharpness.1) | copy-start | bytes 100
  57.8 5.9 %collective-permute-start.12 = (f32[152,256]{1,0:T(8,128)S(1)}, f32[152,256]{1,0:T(8,128)S(1)}, u32[]{:S(2)}, u32[]{:S(2)}) collective-permute-start(f32[152,256]{1,0:T(8,128)S(1)} %mix_back.1.refs_0_), channel_id=1, source_target_pairs={{0,4},{1,5},{2,6},{3,7},{4,0},{5,1},{6,2},{7,3},{8,12},{9,13},{10,... | collective-permute-start | bytes 466952 | tf_op jit(solution)/shard_map/ppermute | solution.py:621
  63.1 7.4 %collective-permute-start.16 = (f32[2,144,256]{2,1,0:T(8,128)S(1)}, f32[2,144,256]{2,1,0:T(8,128)S(1)}, u32[]{:S(2)}, u32[]{:S(2)}) collective-permute-start(f32[2,144,256]{2,1,0:T(8,128)S(1)} %get-tuple-element.99), channel_id=1, source_target_pairs={{0,4},{1,5},{2,6},{3,7},{4,0},{5,1},{6,2},{7,3},{8,12},{9,13},{10,... | collective-permute-start | bytes 884744 | tf_op jit(solution)/shard_map/ppermute | solution.py:621
  63.6 1.4 %collective-permute-start.13 = (f32[152,256]{1,0:T(8,128)S(1)}, f32[152,256]{1,0:T(8,128)S(1)}, u32[]{:S(2)}, u32[]{:S(2)}) collective-permute-start(f32[152,256]{1,0:T(8,128)S(1)} %mix_back.1.refs_0_), channel_id=1, source_target_pairs={{0,1},{1,0},{2,3},{3,2},{4,5},{5,4},{6,7},{7,6},{8,9},{9,8},{10,11... | collective-permute-start | bytes 466952 | tf_op jit(solution)/shard_map/ppermute | solution.py:621
  63.7 1.6 %collective-permute-start.14 = (f32[152,256]{1,0:T(8,128)S(1)}, f32[152,256]{1,0:T(8,128)S(1)}, u32[]{:S(2)}, u32[]{:S(2)}) collective-permute-start(f32[152,256]{1,0:T(8,128)S(1)} %collective-permute-done.12.refs_1_), channel_id=1, source_target_pairs={{0,1},{1,0},{2,3},{3,2},{4,5},{5,4},{6,7},{7,6},{8,9},{9,8},{10,11... | collective-permute-start | bytes 466952 | tf_op jit(solution)/shard_map/ppermute | solution.py:621
  70.5 1.6 %collective-permute-start.17 = (f32[288,256]{1,0:T(8,128)S(1)}, f32[288,256]{1,0:T(8,128)S(1)}, u32[]{:S(2)}, u32[]{:S(2)}) collective-permute-start(f32[288,256]{1,0:T(8,128)S(1)} %get-tuple-element.85), channel_id=1, source_target_pairs={{0,1},{1,0},{2,3},{3,2},{4,5},{5,4},{6,7},{7,6},{8,9},{9,8},{10,11... | collective-permute-start | bytes 884744 | tf_op jit(solution)/shard_map/ppermute | solution.py:621
  72.1 6.5 %collective-permute-start.18 = (f32[160,256]{1,0:T(8,128)S(1)}, f32[160,256]{1,0:T(8,128)S(1)}, u32[]{:S(2)}, u32[]{:S(2)}) collective-permute-start(f32[160,256]{1,0:T(8,128)S(1)} %pad_maximum_fusion), channel_id=1, source_target_pairs={{0,2},{1,3},{2,0},{3,1},{4,6},{5,7},{6,4},{7,5},{8,10},{9,11},{10,... | collective-permute-start | bytes 491528 | tf_op jit(solution)/shard_map/ppermute | solution.py:621
  73.4 10.7 %collective-permute-start.20 = (f32[1,144,256]{2,1,0:T(8,128)S(1)}, f32[1,144,256]{2,1,0:T(8,128)S(1)}, u32[]{:S(2)}, u32[]{:S(2)}) collective-permute-start(f32[1,144,256]{2,1,0:T(8,128)S(1)} %get-tuple-element.100), channel_id=1, source_target_pairs={{0,8},{1,9},{2,10},{3,11},{4,12},{5,13},{6,14},{7,15},{8,0},{9,1},... | collective-permute-start | bytes 442376 | tf_op jit(solution)/shard_map/ppermute | solution.py:621
  78.6 7.3 %collective-permute-start.19 = (f32[96,256]{1,0:T(8,128)S(1)}, f32[96,256]{1,0:T(8,128)S(1)}, u32[]{:S(2)}, u32[]{:S(2)}) collective-permute-start(f32[96,256]{1,0:T(8,128)S(1)} %pad_maximum_fusion.1), channel_id=1, source_target_pairs={{0,4},{1,5},{2,6},{3,7},{4,0},{5,1},{6,2},{7,3},{8,12},{9,13},{10,... | collective-permute-start | bytes 294920 | tf_op jit(solution)/shard_map/ppermute | solution.py:621
  85.9 5.4 %collective-permute-start.21 = (f32[64,256]{1,0:T(8,128)S(1)}, f32[64,256]{1,0:T(8,128)S(1)}, u32[]{:S(2)}, u32[]{:S(2)}) collective-permute-start(f32[64,256]{1,0:T(8,128)S(1)} %pad_maximum_fusion.2), channel_id=1, source_target_pairs={{0,8},{1,9},{2,10},{3,11},{4,12},{5,13},{6,14},{7,15},{8,0},{9,1},... | collective-permute-start | bytes 196616 | tf_op jit(solution)/shard_map/ppermute | solution.py:621
